TPU v7x, 32 devices: a whole 2x2x4 slice. The times are simulated.
32 devices in a mesh: groups: 2 (over x), seq: 16 (over z, y, core).
Axes of the slice: x: 2, y: 2, z: 4, core: 2. Of those that a mesh axis runs over, the one named last changes fastest.
Arguments:
- queries: bfloat16 [8192, 2048], P(('groups', 'seq')), parts along dimension 0, may hold values from -14 to 14
- ctx_keys: bfloat16 [8192, 512], P(('groups', 'seq')), parts along dimension 0, may hold values from -11.5 to 11.5
- ctx_values: bfloat16 [8192, 512], P(('groups', 'seq')), parts along dimension 0, may hold values from -5 to 5
- store_keys: bfloat16 [512, 128, 512], P(('groups', 'seq')), parts along dimension 0, may hold values from -11.5 to 11.5
- store_values: bfloat16 [512, 128, 512], P(('groups', 'seq')), parts along dimension 0, may hold values from -5 to 5
- block_ids: int32 [32, 32], P(('groups', 'seq')), parts along dimension 0, may hold values from 0 to 255, as said below
- block_slot: int32 [512], P('groups'), parts along dimension 0, may hold values from 0 to 255, as said below
- gate_logit: float32 [16], replicated, may hold values from -2 to 2
Outputs:
- mixed: bfloat16 [8192, 2048], P(('groups', 'seq')), parts along dimension 0
There are 2 independent parts, one for each index of `groups`. A program takes and returns all parts, laid end to end along the dimension named above; an argument that names none is the same for every part. Nothing has to cross between parts.
Inputs may be any that keep to these rules, and one draw needn't show every extreme that they name: block_slot is a permutation of 0 to 255; memory block b lies on seq index block_slot[b] // 16 at local position block_slot[b] % 16. `block_ids`: the 32 ids of one row are distinct; at most 2 of them lie on any one seq index, and in every draw some seq index holds exactly 2 blocks of every row.
All inputs are finite; a program needn't handle non-finite values.
Results may differ from a plain program's by a relative error of at most 0.0052.
Values may be sent and summed in bfloat16 or wider, within the bound.
No kernel may reach another device: no remote copies, remote signals or barrier semaphores. Data moves between devices by JAX's collectives and lax.ppermute only.
A program may use at most 192 MiB of HBM per device.

v0:
```python
import math

import jax
import jax.numpy as jnp
from jax import lax
from jax.sharding import PartitionSpec as P

H = 16
KVH = 4
HD = 128
QBLK = 256
MROWS = 128
TOPM = 32
CAP = 2


masked_score = -1e30
key_block = 1024


def fresh_state(row_count, kv_heads):
    group = H // KVH
    return (
        jnp.full((kv_heads, group, row_count), masked_score, jnp.float32),
        jnp.zeros((kv_heads, group, row_count), jnp.float32),
        jnp.zeros((kv_heads, group, row_count, HD), jnp.float32),
    )


def split_heads(query_part):
    group = H // KVH
    kv_heads = query_part.shape[1] // (group * HD)
    return query_part.reshape(query_part.shape[0], kv_heads, group, HD)


def block_update(state, query_heads, key_rows, value_rows, allowed):
    row_max, row_sum, weighted = state
    kv_heads = query_heads.shape[1]
    scores = jnp.einsum(
        "rhgd,khd->hgrk",
        query_heads,
        key_rows.reshape(-1, kv_heads, HD),
        preferred_element_type=jnp.float32,
    ) * HD ** (-0.5)
    if allowed is not None:
        scores = jnp.where(allowed, scores, masked_score)
    new_max = jnp.maximum(row_max, jnp.max(scores, axis=-1))
    decay = jnp.exp(row_max - new_max)
    probs = jnp.exp(scores - new_max[..., None])
    row_sum = row_sum * decay + jnp.sum(probs, axis=-1)
    update = jnp.einsum(
        "hgrk,khd->hgrd",
        probs.astype(jnp.bfloat16),
        value_rows.reshape(-1, kv_heads, HD),
        preferred_element_type=jnp.float32,
    )
    weighted = weighted * decay[..., None] + update
    return (new_max, row_sum, weighted)


def finish_state(state):
    row_max, row_sum, weighted = state
    result = weighted / row_sum[..., None]
    row_count = result.shape[2]
    return jnp.transpose(result, (2, 0, 1, 3)).reshape(row_count, -1).astype(jnp.bfloat16)


def causal_step(state, query_heads, positions, key_rows, value_rows, key_positions):

    def run_block(current):
        allowed = key_positions[None, :] <= positions[:, None]
        return block_update(current, query_heads, key_rows, value_rows, allowed)

    def keep_block(current):
        return current

    return lax.cond(key_positions[0] <= positions[-1], run_block, keep_block, state)


def memory_attend(query_part, key_rows, value_rows):
    count = key_rows.shape[0]
    width = math.gcd(count, key_block)
    query_heads = split_heads(query_part)

    def memory_inner(step_no, state):
        key_part = lax.dynamic_slice_in_dim(key_rows, step_no * width, width, 0)
        value_part = lax.dynamic_slice_in_dim(value_rows, step_no * width, width, 0)
        return block_update(state, query_heads, key_part, value_part, None)

    start_state = fresh_state(query_part.shape[0], query_heads.shape[1])
    return finish_state(lax.fori_loop(0, count // width, memory_inner, start_state))


def list_memory(query_cols, got_keys, got_values, pick):
    width = got_keys.shape[-1]
    slot_total = got_keys.shape[0] * got_keys.shape[1]
    mine_keys = got_keys.reshape(slot_total, MROWS, width)[pick]
    mine_values = got_values.reshape(slot_total, MROWS, width)[pick]
    list_keys = mine_keys.reshape(TOPM * MROWS, width)
    list_values = mine_values.reshape(TOPM * MROWS, width)
    memory_parts = memory_attend(query_cols, list_keys, list_values)
    return memory_parts


def request_table(slots, owners_count, capacity, local_count):
    entries = slots.shape[0]
    owner = slots // local_count
    local = slots % local_count
    order = jnp.arange(entries, dtype=jnp.int32)
    earlier = (owner[:, None] == owner[None, :]) & (order[None, :] < order[:, None])
    rank = jnp.sum(earlier.astype(jnp.int32), axis=1)
    chosen = (owner[:, None, None] == jnp.arange(owners_count, dtype=jnp.int32)[None, :, None]) & (
        rank[:, None, None] == jnp.arange(capacity, dtype=jnp.int32)[None, None, :]
    )
    table = jnp.sum(jnp.where(chosen, local[:, None, None] + 1, 0), axis=0) - 1
    return (table, owner, rank)


def lookup_slots(wanted_ids, block_slot):
    hits = wanted_ids[..., None] == jnp.arange(block_slot.shape[0], dtype=jnp.int32)
    return jnp.sum(jnp.where(hits, block_slot, 0), axis=-1)


def on_device(
    queries, ctx_keys, ctx_values, store_keys, store_values, block_ids, block_slot, gate_logit
):
    shard_rows = queries.shape[0]
    half = shard_rows // 2
    devices = lax.axis_size("seq")
    my_index = lax.axis_index("seq")
    lists = shard_rows // QBLK
    capacity = lists * CAP
    local_count = store_keys.shape[0]
    my_slots = lookup_slots(block_ids.reshape(-1), block_slot)
    my_table, my_owner, my_rank = request_table(my_slots, devices, capacity, local_count)
    wanted = lax.all_to_all(my_table, "seq", split_axis=0, concat_axis=0, tiled=True)
    rows_wanted = jnp.maximum(wanted, 0)
    pick = my_owner * capacity + my_rank
    got_keys, got_values = (
        lax.all_to_all(store_keys[rows_wanted], "seq", split_axis=0, concat_axis=0, tiled=True),
        lax.all_to_all(store_values[rows_wanted], "seq", split_axis=0, concat_axis=0, tiled=True),
    )
    memory = list_memory(queries, got_keys, got_values, pick)
    base = my_index * shard_rows
    first_pos = base + jnp.arange(half, dtype=jnp.int32)
    first_heads = split_heads(queries[:half])
    moved = queries[half:]
    second_pos = my_index * shard_rows + half + jnp.arange(half, dtype=jnp.int32)
    second_heads = split_heads(moved)
    start_states = (fresh_state(half, KVH), fresh_state(half, KVH))
    key_piece = lax.all_gather(ctx_keys, "seq", axis=0, tiled=True)
    value_piece = lax.all_gather(ctx_values, "seq", axis=0, tiled=True)
    count = key_piece.shape[0]
    width = math.gcd(count, key_block)

    def take_inner(step_no, current):
        offset = step_no * width
        key_part = lax.dynamic_slice_in_dim(key_piece, offset, width, 0)
        value_part = lax.dynamic_slice_in_dim(value_piece, offset, width, 0)
        key_positions = offset + jnp.arange(width, dtype=jnp.int32)
        return (
            causal_step(current[0], first_heads, first_pos, key_part, value_part, key_positions),
            causal_step(current[1], second_heads, second_pos, key_part, value_part, key_positions),
        )

    states = lax.fori_loop(0, count // width, take_inner, start_states)
    first_context = finish_state(states[0])
    second_context = finish_state(states[1])
    context = jnp.concatenate([first_context, second_context], axis=0)
    gate = jnp.repeat(jax.nn.sigmoid(gate_logit), HD)
    memory_wide = lax.optimization_barrier(memory).astype(jnp.float32)
    context_wide = lax.optimization_barrier(context).astype(jnp.float32)
    return (gate * memory_wide + (1.0 - gate) * context_wide).astype(jnp.bfloat16)


def solution(mesh):
    placed = (
        P(("groups", "seq"), None),
        P(("groups", "seq"), None),
        P(("groups", "seq"), None),
        P(("groups", "seq"), None, None),
        P(("groups", "seq"), None, None),
        P(("groups", "seq"), None),
        P("groups"),
        P(),
    )
    return jax.shard_map(
        on_device, mesh=mesh, in_specs=placed, out_specs=P(("groups", "seq"), None), check_vma=False
    )
```

profile of v0, /device:TPU:25, one launch (start us, length us, event | category | flops | bytes accessed | tf_op | source)
XLA Modules:
  0.0 462.9 jit_solution(4397273095732336967)
XLA Ops:
  8.6 9.1 %all_to_all.16 = s32[16,1,2]{2,1,0:T(1,128)S(1)} all-to-all(s32[16,1,2]{2,1,0:T(1,128)S(1)} %copy.90), channel_id=1, replica_groups=mesh['groups'=2,'seq'=16] {'seq'}, dimensions={0} | all-to-all | bytes 256 | tf_op jit(solution)/shard_map/all_to_all | solution.py:136
  32.2 108.6 %all-to-all-done.1 = bf16[16,2,128,512]{3,2,1,0:T(8,128)(2,1)} async-done(((bf16[16,2,128,512]{3,2,1,0:T(8,128)(2,1)}), bf16[16,2,128,512]{3,2,1,0:T(8,128)(2,1)}, u32[]{:S(2)}, u32[]{:S(2)}) %all-to-all-start.1) | async-done | bytes 4194336 | tf_op jit(solution)/shard_map/all_to_all | solution.py:140
  140.8 21.5 %all-to-all-start.2 = ((bf16[16,2,128,512]{3,2,1,0:T(8,128)(2,1)}), bf16[16,2,128,512]{3,2,1,0:T(8,128)(2,1)}, u32[]{:S(2)}, u32[]{:S(2)}) async-start(bf16[16,2,128,512]{3,2,1,0:T(8,128)(2,1)} %bitcast.132), calls=%async_computation.2 | async-start | bytes 8388608 | tf_op jit(solution)/shard_map/all_to_all | solution.py:141
  169.9 142.3 %while.41 = (s32[]{:T(128)}, f32[4,4,128]{2,1,0:T(4,128)S(1)}, f32[4,4,128]{2,1,0:T(4,128)S(1)}, f32[4,4,128,128]{3,2,1,0:T(8,128)}, f32[4,4,128]{2,1,0:T(4,128)...) while((s32[]{:T(128)}, f32[4,4,128]{2,1,0:T(4,128)S(1)}, ...), condition=%wide.region_16.17_spmd, body=%wide.region_7.16_spmd.sunk | while | flops 2194940928 | bytes 149173872 | solution.py:166
  174.2 15.3 %conditional.5 = ((f32[4,4,128]{2,1,0:T(4,128)S(1)}, f32[4,4,128]{2,1,0:T(4,128)S(1)}, f32[4,4,128,128]{3,2,1,0:T(8,128)})) conditional(s32[]{:T(128)} %bitcast.115, (f32[4,4,128]{2,1,0:T(4,128)S(1)}, f32[4,4,128]{2,1,0:T(4,128)S(1)}, f32[4,4,128,128]{3,2,1,0:T(8,128)}) %tuple.100, (s32[1024]{0:T(1024)S(1)}, s32[128]{0:T(128)S(1)}, ...), branch_computations={%region_12.12_spmd, %region_13.15_spmd} | conditional | flops 1097469952 | bytes 68293184 | solution.py:77
  191.4 14.2 %conditional.4 = ((f32[4,4,128]{2,1,0:T(4,128)S(1)}, f32[4,4,128]{2,1,0:T(4,128)S(1)}, f32[4,4,128,128]{3,2,1,0:T(8,128)})) conditional(s32[]{:T(128)} %bitcast.114, (f32[4,4,128]{2,1,0:T(4,128)S(1)}, f32[4,4,128]{2,1,0:T(4,128)S(1)}, f32[4,4,128,128]{3,2,1,0:T(8,128)}) %tuple.98, (s32[1024]{0:T(1024)S(1)}, s32[128]{0:T(128)S(1)}, ...), branch_computations={%region_8.8_spmd, %region_9.11_spmd} | conditional | flops 1097469952 | bytes 76681848 | solution.py:77
  209.7 15.4 %conditional.5 = ((f32[4,4,128]{2,1,0:T(4,128)S(1)}, f32[4,4,128]{2,1,0:T(4,128)S(1)}, f32[4,4,128,128]{3,2,1,0:T(8,128)})) conditional(s32[]{:T(128)} %bitcast.115, (f32[4,4,128]{2,1,0:T(4,128)S(1)}, f32[4,4,128]{2,1,0:T(4,128)S(1)}, f32[4,4,128,128]{3,2,1,0:T(8,128)}) %tuple.100, (s32[1024]{0:T(1024)S(1)}, s32[128]{0:T(128)S(1)}, ...), branch_computations={%region_12.12_spmd, %region_13.15_spmd} | conditional | flops 1097469952 | bytes 68293184 | solution.py:77
  227.0 14.2 %conditional.4 = ((f32[4,4,128]{2,1,0:T(4,128)S(1)}, f32[4,4,128]{2,1,0:T(4,128)S(1)}, f32[4,4,128,128]{3,2,1,0:T(8,128)})) conditional(s32[]{:T(128)} %bitcast.114, (f32[4,4,128]{2,1,0:T(4,128)S(1)}, f32[4,4,128]{2,1,0:T(4,128)S(1)}, f32[4,4,128,128]{3,2,1,0:T(8,128)}) %tuple.98, (s32[1024]{0:T(1024)S(1)}, s32[128]{0:T(128)S(1)}, ...), branch_computations={%region_8.8_spmd, %region_9.11_spmd} | conditional | flops 1097469952 | bytes 76681848 | solution.py:77
  245.3 15.4 %conditional.5 = ((f32[4,4,128]{2,1,0:T(4,128)S(1)}, f32[4,4,128]{2,1,0:T(4,128)S(1)}, f32[4,4,128,128]{3,2,1,0:T(8,128)})) conditional(s32[]{:T(128)} %bitcast.115, (f32[4,4,128]{2,1,0:T(4,128)S(1)}, f32[4,4,128]{2,1,0:T(4,128)S(1)}, f32[4,4,128,128]{3,2,1,0:T(8,128)}) %tuple.100, (s32[1024]{0:T(1024)S(1)}, s32[128]{0:T(128)S(1)}, ...), branch_computations={%region_12.12_spmd, %region_13.15_spmd} | conditional | flops 1097469952 | bytes 68293184 | solution.py:77
  262.5 14.2 %conditional.4 = ((f32[4,4,128]{2,1,0:T(4,128)S(1)}, f32[4,4,128]{2,1,0:T(4,128)S(1)}, f32[4,4,128,128]{3,2,1,0:T(8,128)})) conditional(s32[]{:T(128)} %bitcast.114, (f32[4,4,128]{2,1,0:T(4,128)S(1)}, f32[4,4,128]{2,1,0:T(4,128)S(1)}, f32[4,4,128,128]{3,2,1,0:T(8,128)}) %tuple.98, (s32[1024]{0:T(1024)S(1)}, s32[128]{0:T(128)S(1)}, ...), branch_computations={%region_8.8_spmd, %region_9.11_spmd} | conditional | flops 1097469952 | bytes 76681848 | solution.py:77
  280.8 15.4 %conditional.5 = ((f32[4,4,128]{2,1,0:T(4,128)S(1)}, f32[4,4,128]{2,1,0:T(4,128)S(1)}, f32[4,4,128,128]{3,2,1,0:T(8,128)})) conditional(s32[]{:T(128)} %bitcast.115, (f32[4,4,128]{2,1,0:T(4,128)S(1)}, f32[4,4,128]{2,1,0:T(4,128)S(1)}, f32[4,4,128,128]{3,2,1,0:T(8,128)}) %tuple.100, (s32[1024]{0:T(1024)S(1)}, s32[128]{0:T(128)S(1)}, ...), branch_computations={%region_12.12_spmd, %region_13.15_spmd} | conditional | flops 1097469952 | bytes 68293184 | solution.py:77
  298.0 14.2 %conditional.4 = ((f32[4,4,128]{2,1,0:T(4,128)S(1)}, f32[4,4,128]{2,1,0:T(4,128)S(1)}, f32[4,4,128,128]{3,2,1,0:T(8,128)})) conditional(s32[]{:T(128)} %bitcast.114, (f32[4,4,128]{2,1,0:T(4,128)S(1)}, f32[4,4,128]{2,1,0:T(4,128)S(1)}, f32[4,4,128,128]{3,2,1,0:T(8,128)}) %tuple.98, (s32[1024]{0:T(1024)S(1)}, s32[128]{0:T(128)S(1)}, ...), branch_computations={%region_8.8_spmd, %region_9.11_spmd} | conditional | flops 1097469952 | bytes 76681848 | solution.py:77
  328.0 119.7 %while.42 = (s32[]{:T(128)}, f32[4,4,256]{2,1,0:T(4,128)S(1)}, f32[4,4,256]{2,1,0:T(4,128)S(1)}, f32[4,4,256,128]{3,2,1,0:T(8,128)}, bf16[4096,512]{1,0:T(8,128)...) while((s32[]{:T(128)}, f32[4,4,256]{2,1,0:T(4,128)S(1)}, ...), condition=%wide.region_6.7_spmd.clone, body=%wide.region_3.6_spmd.clone.sunk | while | flops 2182631424 | bytes 66322600 | solution.py:91
  330.2 9.4 %bitcast_reduce_fusion.2 = (f32[4,4,256]{2,1,0:T(4,128)S(1)}, f32[4,1024,256,4]{2,1,3,0:T(8,128)}) fusion(bf16[1024,4,128,1]{0,2,3,1:T(8,128)(2,1)S(1)} %bitcast.127, bf16[256,4,4,128]{3,0,2,1:T(8,128)(2,1)} %get-tuple-element.841), kind=kOutput, calls=%fused_computation.40.clone.1 | convolution fusion | flops 1082126336 | bytes 18890752 | tf_op jit(solution)/shard_map/while/body/eval_jaxpr/rhgd,khd->hgrk/dot_general | solution.py:39
  339.6 8.5 %fusion.63 = f32[4,4,256]{2,1,0:T(4,128)S(1)} fusion(f32[4,1024,256,4]{2,1,3,0:T(8,128)} %get-tuple-element.747, f32[4,4,256]{2,1,0:T(4,128)S(1)} %select_maximum_fusion.2), kind=kLoop, calls=%fused_computation.43.clone.1 | loop fusion | flops 12578816 | bytes 16809984 | tf_op jit(solution)/shard_map/while/body/eval_jaxpr/reduce_sum | solution.py:50
  348.7 8.8 %fusion.65 = f32[4,4,256,128]{3,2,1,0:T(8,128)} fusion(f32[4,4,256,128]{3,2,1,0:T(8,128)} %get-tuple-element.828, bf16[1024,4,128,1]{0,2,3,1:T(8,128)(2,1)S(1)} %bitcast.124, f32[4,1024,256,4]{2,1,3,0:T(8,128)} %get-tuple-element.747, f32[4,4,256]{2,1,0:T(4,128)S(1)} %select_maximum_fusion.2, f32[4,4,256]{2,1,0:T(4,128)S(1)} %get-tuple-element.750, ...), kind=kOutput, calls=%fused_computation.48.clone.1 | convolution fusion | flops 1087897600 | bytes 22052864 | tf_op jit(solution)/shard_map/while/body/eval_jaxpr/hgrk,khd->hgrd/dot_general | solution.py:51
  359.8 9.4 %bitcast_reduce_fusion.2 = (f32[4,4,256]{2,1,0:T(4,128)S(1)}, f32[4,1024,256,4]{2,1,3,0:T(8,128)}) fusion(bf16[1024,4,128,1]{0,2,3,1:T(8,128)(2,1)S(1)} %bitcast.127, bf16[256,4,4,128]{3,0,2,1:T(8,128)(2,1)} %get-tuple-element.841), kind=kOutput, calls=%fused_computation.40.clone.1 | convolution fusion | flops 1082126336 | bytes 18890752 | tf_op jit(solution)/shard_map/while/body/eval_jaxpr/rhgd,khd->hgrk/dot_general | solution.py:39
  369.1 8.5 %fusion.63 = f32[4,4,256]{2,1,0:T(4,128)S(1)} fusion(f32[4,1024,256,4]{2,1,3,0:T(8,128)} %get-tuple-element.747, f32[4,4,256]{2,1,0:T(4,128)S(1)} %select_maximum_fusion.2), kind=kLoop, calls=%fused_computation.43.clone.1 | loop fusion | flops 12578816 | bytes 16809984 | tf_op jit(solution)/shard_map/while/body/eval_jaxpr/reduce_sum | solution.py:50
  378.2 9.3 %fusion.65 = f32[4,4,256,128]{3,2,1,0:T(8,128)} fusion(f32[4,4,256,128]{3,2,1,0:T(8,128)} %get-tuple-element.828, bf16[1024,4,128,1]{0,2,3,1:T(8,128)(2,1)S(1)} %bitcast.124, f32[4,1024,256,4]{2,1,3,0:T(8,128)} %get-tuple-element.747, f32[4,4,256]{2,1,0:T(4,128)S(1)} %select_maximum_fusion.2, f32[4,4,256]{2,1,0:T(4,128)S(1)} %get-tuple-element.750, ...), kind=kOutput, calls=%fused_computation.48.clone.1 | convolution fusion | flops 1087897600 | bytes 22052864 | tf_op jit(solution)/shard_map/while/body/eval_jaxpr/hgrk,khd->hgrd/dot_general | solution.py:51
  389.8 9.4 %bitcast_reduce_fusion.2 = (f32[4,4,256]{2,1,0:T(4,128)S(1)}, f32[4,1024,256,4]{2,1,3,0:T(8,128)}) fusion(bf16[1024,4,128,1]{0,2,3,1:T(8,128)(2,1)S(1)} %bitcast.127, bf16[256,4,4,128]{3,0,2,1:T(8,128)(2,1)} %get-tuple-element.841), kind=kOutput, calls=%fused_computation.40.clone.1 | convolution fusion | flops 1082126336 | bytes 18890752 | tf_op jit(solution)/shard_map/while/body/eval_jaxpr/rhgd,khd->hgrk/dot_general | solution.py:39
  399.2 8.5 %fusion.63 = f32[4,4,256]{2,1,0:T(4,128)S(1)} fusion(f32[4,1024,256,4]{2,1,3,0:T(8,128)} %get-tuple-element.747, f32[4,4,256]{2,1,0:T(4,128)S(1)} %select_maximum_fusion.2), kind=kLoop, calls=%fused_computation.43.clone.1 | loop fusion | flops 12578816 | bytes 16809984 | tf_op jit(solution)/shard_map/while/body/eval_jaxpr/reduce_sum | solution.py:50
  408.3 9.3 %fusion.65 = f32[4,4,256,128]{3,2,1,0:T(8,128)} fusion(f32[4,4,256,128]{3,2,1,0:T(8,128)} %get-tuple-element.828, bf16[1024,4,128,1]{0,2,3,1:T(8,128)(2,1)S(1)} %bitcast.124, f32[4,1024,256,4]{2,1,3,0:T(8,128)} %get-tuple-element.747, f32[4,4,256]{2,1,0:T(4,128)S(1)} %select_maximum_fusion.2, f32[4,4,256]{2,1,0:T(4,128)S(1)} %get-tuple-element.750, ...), kind=kOutput, calls=%fused_computation.48.clone.1 | convolution fusion | flops 1087897600 | bytes 22052864 | tf_op jit(solution)/shard_map/while/body/eval_jaxpr/hgrk,khd->hgrd/dot_general | solution.py:51
  419.8 9.4 %bitcast_reduce_fusion.2 = (f32[4,4,256]{2,1,0:T(4,128)S(1)}, f32[4,1024,256,4]{2,1,3,0:T(8,128)}) fusion(bf16[1024,4,128,1]{0,2,3,1:T(8,128)(2,1)S(1)} %bitcast.127, bf16[256,4,4,128]{3,0,2,1:T(8,128)(2,1)} %get-tuple-element.841), kind=kOutput, calls=%fused_computation.40.clone.1 | convolution fusion | flops 1082126336 | bytes 18890752 | tf_op jit(solution)/shard_map/while/body/eval_jaxpr/rhgd,khd->hgrk/dot_general | solution.py:39
  438.3 9.3 %fusion.65 = f32[4,4,256,128]{3,2,1,0:T(8,128)} fusion(f32[4,4,256,128]{3,2,1,0:T(8,128)} %get-tuple-element.828, bf16[1024,4,128,1]{0,2,3,1:T(8,128)(2,1)S(1)} %bitcast.124, f32[4,1024,256,4]{2,1,3,0:T(8,128)} %get-tuple-element.747, f32[4,4,256]{2,1,0:T(4,128)S(1)} %select_maximum_fusion.2, f32[4,4,256]{2,1,0:T(4,128)S(1)} %get-tuple-element.750, ...), kind=kOutput, calls=%fused_computation.48.clone.1 | convolution fusion | flops 1087897600 | bytes 22052864 | tf_op jit(solution)/shard_map/while/body/eval_jaxpr/hgrk,khd->hgrd/dot_general | solution.py:51
  (217 shorter events, 199.0 us)
Async XLA Ops:
  6.5 11.3 %copy-start = (bf16[16,128,512]{2,1,0:T(8,128)(2,1)S(1)}, bf16[16,128,512]{2,1,0:T(8,128)(2,1)}, u32[]{:S(2)}) copy-start(bf16[16,128,512]{2,1,0:T(8,128)(2,1)} %param.19) | copy-start | bytes 6291460
  6.5 161.2 %all-gather.3.cloned.1.call-start = ((), (), s32[]{:S(2)}) async-start(), calls=%async_computation.3 | async-start | bytes 4456448 | tf_op jit(solution)/shard_map/all_gather | solution.py:151
  20.5 8.9 %copy-start.4 = (bf16[16,128,512]{2,1,0:T(8,128)(2,1)S(1)}, bf16[16,128,512]{2,1,0:T(8,128)(2,1)}, u32[]{:S(2)}) copy-start(bf16[16,128,512]{2,1,0:T(8,128)(2,1)} %param.20) | copy-start | bytes 6291460
  20.5 120.2 %all-to-all-start.1 = ((bf16[16,2,128,512]{3,2,1,0:T(8,128)(2,1)}), bf16[16,2,128,512]{3,2,1,0:T(8,128)(2,1)}, u32[]{:S(2)}, u32[]{:S(2)}) async-start(bf16[16,2,128,512]{3,2,1,0:T(8,128)(2,1)} %bitcast.133), calls=%async_computation.1 | async-start | bytes 8388608 | tf_op jit(solution)/shard_map/all_to_all | solution.py:140
  28.6 139.0 %all-gather.5.cloned.1.call-start = ((), (), s32[]{:S(2)}) async-start(), calls=%async_computation.4 | async-start | bytes 4456448 | tf_op jit(solution)/shard_map/all_gather | solution.py:152
  29.4 132.9 %copy-start.7 = (bf16[256,2048]{1,0:T(8,128)(2,1)S(1)}, bf16[256,2048]{1,0:T(8,128)(2,1)}, u32[]{:S(2)}) copy-start(bf16[256,2048]{1,0:T(8,128)(2,1)} %param.16) | copy-start | bytes 3145732
  140.8 25.5 %copy-start.10 = (f32[16]{0:T(128)S(1)}, f32[16]{0:T(128)}, u32[]{:S(2)}) copy-start(f32[16]{0:T(128)} %param.23) | copy-start | bytes 196
  140.8 182.2 %all-to-all-start.2 = ((bf16[16,2,128,512]{3,2,1,0:T(8,128)(2,1)}), bf16[16,2,128,512]{3,2,1,0:T(8,128)(2,1)}, u32[]{:S(2)}, u32[]{:S(2)}) async-start(bf16[16,2,128,512]{3,2,1,0:T(8,128)(2,1)} %bitcast.132), calls=%async_computation.2 | async-start | bytes 8388608 | tf_op jit(solution)/shard_map/all_to_all | solution.py:141
  177.2 3.2 copy-start.2
  194.4 3.2 copy-start.3
  194.4 5.3 %copy-start.5 = (f32[4,4,128,128]{3,2,1,0:T(8,128)S(1)}, f32[4,4,128,128]{3,2,1,0:T(8,128)}, u32[]{:S(2)}) copy-start(f32[4,4,128,128]{3,2,1,0:T(8,128)} %get-tuple-element.389) | copy-start | bytes 3145732 | tf_op jit(solution)/shard_map/while/body/eval_jaxpr/cond
  204.6 1.0 copy-start.6
  212.7 3.2 copy-start.2
  229.9 3.2 copy-start.3
  229.9 5.3 %copy-start.5 = (f32[4,4,128,128]{3,2,1,0:T(8,128)S(1)}, f32[4,4,128,128]{3,2,1,0:T(8,128)}, u32[]{:S(2)}) copy-start(f32[4,4,128,128]{3,2,1,0:T(8,128)} %get-tuple-element.389) | copy-start | bytes 3145732 | tf_op jit(solution)/shard_map/while/body/eval_jaxpr/cond
  248.2 3.2 copy-start.2
  265.5 3.2 copy-start.3
  265.5 5.3 %copy-start.5 = (f32[4,4,128,128]{3,2,1,0:T(8,128)S(1)}, f32[4,4,128,128]{3,2,1,0:T(8,128)}, u32[]{:S(2)}) copy-start(f32[4,4,128,128]{3,2,1,0:T(8,128)} %get-tuple-element.389) | copy-start | bytes 3145732 | tf_op jit(solution)/shard_map/while/body/eval_jaxpr/cond
  283.8 3.2 copy-start.2
  301.0 3.2 copy-start.3
  301.0 5.3 %copy-start.5 = (f32[4,4,128,128]{3,2,1,0:T(8,128)S(1)}, f32[4,4,128,128]{3,2,1,0:T(8,128)}, u32[]{:S(2)}) copy-start(f32[4,4,128,128]{3,2,1,0:T(8,128)} %get-tuple-element.389) | copy-start | bytes 3145732 | tf_op jit(solution)/shard_map/while/body/eval_jaxpr/cond
  328.0 125.4 %copy-start.8 = (f32[2048]{0:T(1024)S(1)}, f32[2048]{0:T(1024)}, u32[]{:S(2)}) copy-start(f32[2048]{0:T(1024)} %bitcast_subtract_fusion.1) | copy-start | bytes 24580
  328.0 125.4 %copy-start.9 = (f32[2048]{0:T(1024)S(1)}, f32[2048]{0:T(1024)}, u32[]{:S(2)}) copy-start(f32[2048]{0:T(1024)} %broadcast_bitcast_fusion) | copy-start | bytes 24580
  447.7 8.4 %copy-start.1 = (bf16[16,128,512]{2,1,0:T(8,128)(2,1)S(1)}, bf16[16,128,512]{2,1,0:T(8,128)(2,1)}, u32[]{:S(2)}) copy-start(bf16[16,128,512]{2,1,0:T(8,128)(2,1)} %param.19) | copy-start | bytes 6291460
  (3 other events, 2.9 us)
Sparse Core Ops, SparseCore 0:
  9.5 82.8 all-gather.2
  94.5 72.7 all-gather.4
where the time goes:
time: 464 us; the launch traced here: 463 us
  matrix products  142 us (31%)
  waiting for transfers between devices  110 us (24%)
  local copies, waits for them, and re-layouts  86.5 us (19%)
  other arithmetic  60.8 us (13%)
  starting transfers between devices  29.6 us (6%)
  between operations  13.6 us (3%)
  loops' own time  11.2 us (2%)
  blocking collectives  9.1 us (2%)
    all_to_all x1, waiting for transfers between devices, on_device(): lax.all_to_all(store_keys[rows_wanted], 'seq', split_axis=0, concat_axis=...  109 us
    dot_general x12, matrix products, block_update(): jnp.einsum('hgrk,khd->hgrd', probs.astype(jnp.bfloat16), value_rows.resha...  85 us
    dot_general x12, matrix products, block_update(): jnp.einsum('rhgd,khd->hgrk', query_heads, key_rows.reshape(-1, kv_heads,...  57 us
    reduce_sum x12, other arithmetic, block_update(): row_sum = row_sum * decay + jnp.sum(probs, axis=-1)  48 us
    cond x40, local copies, waits for them, and re-layouts  29.4 us
    all_to_all x1, starting transfers between devices, on_device(): lax.all_to_all(store_values[rows_wanted], 'seq', split_axis=0, concat_axi...  21.5 us
    another operation x1, loops' own time, on_device(): states = lax.fori_loop(0, count // width, take_inner, start_states)  10.4 us
  transfers between devices with their start and end apart: 4, of which 1 were waited for; matrix products, arithmetic and copies ran while one was open for 27% of the time, Pallas kernels for 0%

commit v1 on v0

v1 whole, which is shorter than its diff:
```python
import functools

import jax
import jax.numpy as jnp
from jax import lax
from jax.experimental import pallas as pl
from jax.experimental.pallas import tpu as pltpu
from jax.sharding import PartitionSpec as P

H = 16
KVH = 4
HD = 128
QBLK = 256
MROWS = 128
TOPM = 32
CAP = 2
G = H // KVH
WITHIN = 4
LOG2E = 1.4426950408889634
SCALE = HD**-0.5 * LOG2E
MASKED = -1e30
QW = G * HD
STAGES = ((0, 1), (1, 1), (2, 1), (3, 1))


def request_table(slots, owners_count, local_count):
    entries = slots.shape[0]
    owner = slots // local_count
    local = slots % local_count
    order = jnp.arange(entries, dtype=jnp.int32)
    earlier = (owner[:, None] == owner[None, :]) & (order[None, :] < order[:, None])
    rank = jnp.sum(earlier.astype(jnp.int32), axis=1)
    chosen = (owner[:, None, None] == jnp.arange(owners_count, dtype=jnp.int32)[None, :, None]) & (
        rank[:, None, None] == jnp.arange(CAP, dtype=jnp.int32)[None, None, :]
    )
    return jnp.sum(jnp.where(chosen, local[:, None, None] + 1, 0), axis=0) - 1


def lookup_slots(wanted_ids, block_slot):
    hits = wanted_ids[..., None] == jnp.arange(block_slot.shape[0], dtype=jnp.int32)
    return jnp.sum(jnp.where(hits, block_slot, 0), axis=-1)


def attend_heads(q, k, v, allowed, out_ref, lse_rows):
    keys = k.shape[0]
    vx = jnp.concatenate([v, jnp.ones((keys, HD), jnp.bfloat16)], axis=1)
    lane = lax.broadcasted_iota(jnp.int32, (QBLK, HD), 1)
    for g in range(G):
        s = lax.dot_general(
            q[:, g * HD : (g + 1) * HD], k, (((1,), (1,)), ((), ())), preferred_element_type=jnp.float32
        )
        s = s * SCALE
        if allowed is not None:
            s = jnp.where(allowed, s, MASKED)
        m = jnp.max(s, axis=1, keepdims=True)
        p = jnp.exp2(s - m).astype(jnp.bfloat16)
        o = jnp.dot(p, vx, preferred_element_type=jnp.float32)
        total = o[:, HD:]
        out_ref[0, :, g * HD : (g + 1) * HD] = (o[:, :HD] / total).astype(jnp.bfloat16)
        lse_rows = jnp.where(lane == g, m + jnp.log2(total), lse_rows)
    return lse_rows


def ctx_kernel(info, q_ref, k0, k1, k2, k3, v0, v1, v2, v3, out_ref, lse_ref):
    slot = pl.program_id(1)
    plane, within = info[0], info[1]
    target = info[2 + slot]

    def run(allowed):
        k = jnp.concatenate([k0[...], k1[...], k2[...], k3[...]], axis=0)
        v = jnp.concatenate([v0[...], v1[...], v2[...], v3[...]], axis=0)
        rows = attend_heads(q_ref[0], k, v, allowed, out_ref, jnp.zeros((QBLK, HD), jnp.float32))
        lse_ref[0, 0] = rows.T[:8]

    @pl.when(target > plane)
    def _():
        run(None)

    @pl.when(target == plane)
    def _():
        keys = WITHIN * QBLK
        col = lax.broadcasted_iota(jnp.int32, (QBLK, keys), 1)
        row = lax.broadcasted_iota(jnp.int32, (QBLK, keys), 0)
        key_pos = jnp.bitwise_xor(col // QBLK, within) * QBLK + col % QBLK
        run(key_pos <= within * QBLK + row)

    @pl.when(target < plane)
    def _():
        out_ref[...] = jnp.zeros_like(out_ref)
        lse_ref[...] = jnp.full_like(lse_ref, MASKED)


def mem_kernel(masked, info, q_ref, k0, k1, k2, k3, v0, v1, v2, v3, ctx_lse_ref, out_ref, lse_ref, kbuf, vbuf):
    slot = pl.program_id(1)
    allowed = None
    keys = WITHIN * CAP * MROWS
    if masked:
        col = lax.broadcasted_iota(jnp.int32, (QBLK, keys), 1) // MROWS
        allowed = jnp.zeros((QBLK, keys), jnp.bool_)
    for s, (kr, vr) in enumerate(((k0, v0), (k1, v1), (k2, v2), (k3, v3))):
        for r in range(CAP):
            n = s * CAP + r
            entry = info[slot, n]
            start = pl.multiple_of(jnp.maximum(entry, 0) * MROWS, MROWS)
            kbuf[n * MROWS : (n + 1) * MROWS, :] = kr[pl.ds(start, MROWS), :]
            vbuf[n * MROWS : (n + 1) * MROWS, :] = vr[pl.ds(start, MROWS), :]
            if masked:
                allowed = allowed | ((col == n) & (entry >= 0))
    rows = attend_heads(q_ref[0], kbuf[...], vbuf[...], allowed, out_ref, jnp.zeros((QBLK, HD), jnp.float32))
    lse_ref[0, 0, :G] = rows.T[:G]
    lse_ref[0, 0, G:] = ctx_lse_ref[0, 0, :G]


def scale_kernel(planes, info, um_ref, uc_ref, gate_ref, *rest):
    lse_refs, out_ref = rest[:-1], rest[-1]
    slot = pl.program_id(1)
    own = info[planes, slot]
    parts = [lse_refs[k][info[k, slot], 0] for k in range(planes)]
    top = functools.reduce(jnp.maximum, parts)
    total = functools.reduce(jnp.add, [jnp.exp2(p - top) for p in parts])
    mine = lse_refs[0][own, 0] if planes == WITHIN else parts[0]
    if planes != WITHIN:
        for k in range(1, planes):
            mine = jnp.where(info[planes + 1, 0] == k, parts[k], mine)
    weight = jnp.exp2(mine - top) / total * gate_ref[0]
    wt = jnp.concatenate([weight, jnp.zeros((HD - 8, QBLK), jnp.float32)], axis=0).T
    for g in range(G):
        cols = slice(g * HD, (g + 1) * HD)
        mixed = wt[:, g : g + 1] * um_ref[0, :, cols].astype(jnp.float32)
        mixed += wt[:, G + g : G + g + 1] * uc_ref[0, :, cols].astype(jnp.float32)
        out_ref[0, :, cols] = mixed.astype(jnp.bfloat16)


def cost(tiles, rows_bytes):
    return pl.CostEstimate(
        flops=tiles * 2 * 1024 * 1024 * 128 * 2, bytes_accessed=rows_bytes, transcendentals=tiles * 1024 * 1024
    )


PARAMS = pltpu.CompilerParams(vmem_limit_bytes=48 * 1024 * 1024)


def ctx_call(info, q, sources, first, count):
    planes = q.shape[0]
    kspec = pl.BlockSpec((QBLK, HD), lambda h, j, info: (0, first + h))
    vspec = pl.BlockSpec((QBLK, HD), lambda h, j, info: (0, KVH + first + h))
    block = pl.BlockSpec((1, QBLK, QW), lambda h, j, info: (j, 0, h))
    return pl.pallas_call(
        ctx_kernel,
        grid_spec=pltpu.PrefetchScalarGridSpec(
            num_scalar_prefetch=1,
            grid=(count, planes),
            in_specs=[block] + [kspec] * WITHIN + [vspec] * WITHIN,
            out_specs=[block, pl.BlockSpec((1, 1, 8, QBLK), lambda h, j, info: (j, h, 0, 0))],
        ),
        out_shape=[
            jax.ShapeDtypeStruct(q.shape, jnp.bfloat16),
            jax.ShapeDtypeStruct((planes, count, 8, QBLK), jnp.float32),
        ],
        compiler_params=PARAMS,
        cost_estimate=cost(count * planes, 4 * 1024 * 1024),
        name="ctx_attend",
    )(info, q, *sources, *sources)


def mem_call(info, q, wide, narrow, ctx_lse, first, count, masked):
    planes = q.shape[0]
    rows = wide[0].shape[0]
    wspec = pl.BlockSpec((rows, HD), lambda h, j, info: (0, first + h))
    kspec = pl.BlockSpec((rows, HD), lambda h, j, info: (0, h))
    vspec = pl.BlockSpec((rows, HD), lambda h, j, info: (0, count + h))
    block = pl.BlockSpec((1, QBLK, QW), lambda h, j, info: (j, 0, h))
    lse = pl.BlockSpec((1, 1, 8, QBLK), lambda h, j, info: (j, h, 0, 0))
    own_k, own_v, near_k, near_v = wide
    far, diag = narrow
    keys = WITHIN * CAP * MROWS
    return pl.pallas_call(
        functools.partial(mem_kernel, masked),
        grid_spec=pltpu.PrefetchScalarGridSpec(
            num_scalar_prefetch=1,
            grid=(count, planes),
            in_specs=[block, wspec, wspec, kspec, kspec, wspec, wspec, vspec, vspec, lse],
            out_specs=[block, lse],
            scratch_shapes=[pltpu.VMEM((keys, HD), jnp.bfloat16), pltpu.VMEM((keys, HD), jnp.bfloat16)],
        ),
        out_shape=[
            jax.ShapeDtypeStruct(q.shape, jnp.bfloat16),
            jax.ShapeDtypeStruct((planes, count, 8, QBLK), jnp.float32),
        ],
        compiler_params=PARAMS,
        cost_estimate=cost(count * planes, 4 * 1024 * 1024),
        name="mem_attend",
    )(info, q, own_k, near_k, far, diag, own_v, near_v, far, diag, ctx_lse)


def scale_call(info, um, uc, gate_rows, lses):
    planes, _, width = um.shape
    count = width // QW
    block = pl.BlockSpec((1, QBLK, QW), lambda h, j, info: (j, 0, h))
    lse = pl.BlockSpec((planes, 1, 8, QBLK), lambda h, j, info: (0, h, 0, 0))
    return pl.pallas_call(
        functools.partial(scale_kernel, planes),
        grid_spec=pltpu.PrefetchScalarGridSpec(
            num_scalar_prefetch=1,
            grid=(count, planes),
            in_specs=[block, block, pl.BlockSpec((1, 8, 1), lambda h, j, info: (h, 0, 0))] + [lse] * planes,
            out_specs=block,
        ),
        out_shape=jax.ShapeDtypeStruct(um.shape, jnp.bfloat16),
        compiler_params=PARAMS,
        cost_estimate=pl.CostEstimate(flops=8 * um.size, bytes_accessed=6 * um.size, transcendentals=0),
        name="scale_mix",
    )(info, um, uc, gate_rows, *lses)


def on_device(
    queries, ctx_keys, ctx_values, store_keys, store_values, block_ids, block_slot, gate_logit
):
    devices = lax.axis_size("seq")
    planes = devices // WITHIN
    chain = planes == WITHIN
    me = lax.axis_index("seq")
    plane, within = me // WITHIN, me % WITHIN
    local_count = store_keys.shape[0]
    masked = devices * CAP != TOPM

    def move(x, pairs):
        return lax.ppermute(x, "seq", pairs)

    def xor(x, bits):
        return move(x, [(i, i ^ bits) for i in range(devices)])

    def between(x, plane_pairs):
        return move(x, [(a * WITHIN + w, b * WITHIN + w) for a, b in plane_pairs for w in range(WITHIN)])

    columns = [[p * WITHIN + w for p in range(planes)] for w in range(WITHIN)]

    def gather_planes(x):
        return lax.all_gather(x, "seq", axis=0, axis_index_groups=columns)

    keys = store_keys.reshape(local_count * MROWS, KVH * HD)
    values = store_values.reshape(local_count * MROWS, KVH * HD)

    def store_part(first, count):
        cols = slice(first * HD, (first + count) * HD)
        return jnp.concatenate([keys[:, cols], values[:, cols]], axis=1)

    ctx_own = jnp.concatenate([ctx_keys, ctx_values], axis=1)

    table = request_table(lookup_slots(block_ids.reshape(-1), block_slot), devices, local_count)

    if chain:
        inner = (plane == 1) | (plane == 2)
        low = jnp.where(inner, 3, 2)

        def place(p, target):
            x = p ^ target
            p_inner = (p == 1) | (p == 2)
            return jnp.where(p_inner & (x >= 2), 5 - x, x)

        slot_plane = jnp.stack([plane, plane ^ 1, plane ^ low, plane ^ (5 - low)])
        tables = [table, xor(table, 4), xor(table, 8), xor(table, 12)]
        far_a = jnp.where(inner, tables[3], tables[2])
        far_b = jnp.where(inner, tables[2], tables[3])
        tables = jnp.stack([tables[0], tables[1], far_a, far_b])
        lse_index = jnp.stack([place(plane ^ k, slot_plane) for k in range(planes)] + [jnp.arange(planes)])
    else:
        slot_plane = jnp.arange(planes, dtype=jnp.int32)
        tables = gather_planes(table)
        steps = jnp.arange(planes, dtype=jnp.int32)
        lse_index = jnp.concatenate(
            [jnp.broadcast_to(steps, (planes + 1, planes)), jnp.broadcast_to(plane, (1, planes))]
        )
    lse_index = lse_index.astype(jnp.int32)
    wanted = lax.dynamic_slice_in_dim(tables, plane * WITHIN, WITHIN, 1)
    wanted = jnp.stack([jnp.take(wanted, within ^ s, axis=1) for s in range(WITHIN)], axis=1)
    wanted = wanted.reshape(planes, WITHIN * CAP).astype(jnp.int32)
    ctx_info = jnp.concatenate([jnp.stack([plane, within]), slot_plane]).astype(jnp.int32)

    gate = 1.0 / (1.0 + jnp.exp(-gate_logit))
    gate_rows = jnp.concatenate([gate.reshape(KVH, G), 1.0 - gate.reshape(KVH, G)], axis=1)[:, :, None]

    def spread_queries(part):
        if not chain:
            return gather_planes(part)
        near = xor(part, 4)
        pair = jnp.stack([part, near])
        crossed = between(pair, [(1, 2), (2, 1)])
        handed = between(crossed, [(1, 0), (2, 3)])
        far = jnp.where(inner, crossed, handed)
        return jnp.concatenate([pair, far], axis=0)

    def collect(parts):
        if not chain:
            return lax.psum_scatter(parts, "seq", scatter_dimension=0, axis_index_groups=columns)
        handed = between(parts[2:], [(0, 1), (3, 2)])
        crossed = between(
            (parts[2:].astype(jnp.float32) + handed.astype(jnp.float32)).astype(jnp.bfloat16), [(1, 2), (2, 1)]
        )
        pair = parts[:2].astype(jnp.float32) + crossed.astype(jnp.float32)
        near = xor(pair[1].astype(jnp.bfloat16), 4)
        return (pair[0] + near.astype(jnp.float32)).astype(jnp.bfloat16)

    far_stores = [xor(store_part(first, count), 2) for first, count in STAGES[:1]]
    ctx_far = xor(ctx_own, 2)
    far_stores += [xor(store_part(first, count), 2) for first, count in STAGES[1:]]
    near_keys, near_values = xor(keys, 1), xor(values, 1)
    ctx_near = xor(ctx_own, 1)
    ctx_diag = xor(ctx_far, 1)
    wide = (keys, values, near_keys, near_values)

    results = []
    for (first, count), far in zip(STAGES, far_stores, strict=True):
        q = spread_queries(queries[:, first * QW : (first + count) * QW])
        uc, ctx_lse = ctx_call(ctx_info, q, (ctx_own, ctx_near, ctx_far, ctx_diag), first, count)
        um, lse = mem_call(wanted, q, wide, (far, xor(far, 1)), ctx_lse, first, count, masked)
        if chain:
            lses = [lse, xor(lse, 4), xor(lse, 8), xor(lse, 12)]
        else:
            every = gather_planes(lse)
            lses = [every[k] for k in range(planes)]
        parts = scale_call(lse_index, um, uc, gate_rows[first : first + count], lses)
        results.append(collect(parts))
    return jnp.concatenate(results, axis=1)


def solution(mesh):
    placed = (
        P(("groups", "seq"), None),
        P(("groups", "seq"), None),
        P(("groups", "seq"), None),
        P(("groups", "seq"), None, None),
        P(("groups", "seq"), None, None),
        P(("groups", "seq"), None),
        P("groups"),
        P(),
    )
    return jax.shard_map(
        on_device, mesh=mesh, in_specs=placed, out_specs=P(("groups", "seq"), None), check_vma=False
    )
```

time: 464 us -> 285 us (0.61)
  the two profiles are of different devices: /device:TPU:25 before, /device:TPU:0 now
where the time goes in v1:
time: 285 us; the launch traced here: 284 us
  Pallas kernels  85.8 us (30%)
  starting transfers between devices  85.7 us (30%)
  waiting for transfers between devices  76.5 us (27%)
  other arithmetic  20.5 us (7%)
  local copies, waits for them, and re-layouts  14.5 us (5%)
    ppermute x52, starting transfers between devices, move(): return lax.ppermute(x, 'seq', pairs)  85.7 us
    ppermute x52, waiting for transfers between devices, move(): return lax.ppermute(x, 'seq', pairs)  76.5 us
    pallas_call x4, Pallas kernels, mem_call(): pl.pallas_call(functools.partial(mem_kernel, masked), grid_spec=pltpu.Pre...  38.9 us
    pallas_call x4, Pallas kernels, ctx_call(): pl.pallas_call(ctx_kernel, grid_spec=pltpu.PrefetchScalarGridSpec(num_sca...  36.2 us
    pallas_call x4, Pallas kernels, scale_call(): pl.pallas_call(functools.partial(scale_kernel, planes), grid_spec=pltpu.P...  10.8 us
    unnamed x89, local copies, waits for them, and re-layouts  6.87 us
  transfers between devices with their start and end apart: 52, of which 9 were waited for; matrix products, arithmetic and copies ran while one was open for 9% of the time, Pallas kernels for 30%

profile of v1, /device:TPU:0, one launch (start us, length us, event | category | flops | bytes accessed | tf_op | source)
XLA Modules:
  0.0 283.9 jit_solution(10853040119909212052)
XLA Ops:
  1.4 5.1 %collective-permute-start.1 = (s32[16,2]{0,1:T(2,128)S(1)}, s32[16,2]{0,1:T(2,128)S(1)}, u32[]{:S(2)}, u32[]{:S(2)}) collective-permute-start(s32[16,2]{0,1:T(2,128)S(1)} %get-tuple-element.78), channel_id=1, source_target_pairs={{0,12},{1,13},{2,14},{3,15},{4,8},{5,9},{6,10},{7,11},{8,4},{9,5},... | collective-permute-start | bytes 392 | tf_op jit(solution)/shard_map/ppermute | solution.py:228
  26.9 4.5 %collective-permute-done.30 = bf16[256,512]{1,0:T(8,128)(2,1)S(1)} collective-permute-done((bf16[256,512]{1,0:T(8,128)(2,1)S(1)}, bf16[256,512]{1,0:T(8,128)(2,1)S(1)}, u32[]{:S(2)}, u32[]{:S(2)}) %collective-permute-start.30) | collective-permute-done | bytes 262176 | tf_op jit(solution)/shard_map/ppermute | solution.py:228
  46.8 16.0 %collective-permute-done.7.k2.v2 = bf16[2048,256]{1,0:T(8,128)(2,1)S(1)} collective-permute-done((bf16[2048,256]{1,0:T(8,128)(2,1)}, bf16[2048,256]{1,0:T(8,128)(2,1)S(1)}, u32[]{:S(2)}, u32[]{:S(2)}) %collective-permute-start.7) | collective-permute-done | bytes 1048608 | tf_op jit(solution)/shard_map/ppermute | solution.py:228
  62.8 3.6 %collective-permute-done.5 = bf16[2,256,512]{2,1,0:T(8,128)(2,1)} collective-permute-done((bf16[2,256,512]{2,1,0:T(8,128)(2,1)}, bf16[2,256,512]{2,1,0:T(8,128)(2,1)}, u32[]{:S(2)}, u32[]{:S(2)}) %collective-permute-start.5) | collective-permute-done | bytes 524320 | tf_op jit(solution)/shard_map/ppermute | solution.py:228
  67.7 21.5 %collective-permute-done.21 = bf16[2,256,512]{2,1,0:T(8,128)(2,1)} collective-permute-done((bf16[2,256,512]{2,1,0:T(8,128)(2,1)}, bf16[2,256,512]{2,1,0:T(8,128)(2,1)}, u32[]{:S(2)}, u32[]{:S(2)}) %collective-permute-start.21) | collective-permute-done | bytes 524320 | tf_op jit(solution)/shard_map/ppermute | solution.py:228
  94.4 13.3 %collective-permute-done.33.k2.v2 = bf16[2048,256]{1,0:T(8,128)(2,1)S(1)} collective-permute-done((bf16[2048,256]{1,0:T(8,128)(2,1)}, bf16[2048,256]{1,0:T(8,128)(2,1)S(1)}, u32[]{:S(2)}, u32[]{:S(2)}) %collective-permute-start.33) | collective-permute-done | bytes 1048608 | tf_op jit(solution)/shard_map/ppermute | solution.py:228
  109.5 9.0 %ctx_attend.4 = (bf16[4,256,512]{2,1,0:T(8,128)(2,1)S(1)}, f32[4,1,8,256]{3,2,1,0:T(8,128)S(1)}) custom-call(s32[6]{0:T(128)S(1)} %concatenate.71.info, bf16[4,256,512]{2,1,0:T(8,128)(2,1)S(1)} %pad_maximum_fusion.q_ref, bf16[256,1024]{1,0:T(8,128)(2,1)S(1)} %copy-done.13, bf16[256,1024]{1,0:T(8,128)(2,1)S(1)} %copy-done.17, ...), custom_call_target="tpu_custom_call" | custom-call | flops 2147483648 | bytes 4194304 | tf_op jit(solution)/shard_map/ctx_attend/pallas_call | solution.py:148
  118.5 9.0 %ctx_attend.5 = (bf16[4,256,512]{2,1,0:T(8,128)(2,1)S(1)}, f32[4,1,8,256]{3,2,1,0:T(8,128)S(1)}) custom-call(s32[6]{0:T(128)S(1)} %concatenate.71.info, bf16[4,256,512]{2,1,0:T(8,128)(2,1)S(1)} %pad_maximum_fusion.2.q_ref, bf16[256,1024]{1,0:T(8,128)(2,1)S(1)} %copy-done.13, bf16[256,1024]{1,0:T(8,128)(2,1)S(1)} %copy-done.17, ...), custom_call_target="tpu_custom_call" | custom-call | flops 2147483648 | bytes 4194304 | tf_op jit(solution)/shard_map/ctx_attend/pallas_call | solution.py:148
  131.0 9.0 %ctx_attend.6 = (bf16[4,256,512]{2,1,0:T(8,128)(2,1)S(1)}, f32[4,1,8,256]{3,2,1,0:T(8,128)S(1)}) custom-call(s32[6]{0:T(128)S(1)} %concatenate.71.info, bf16[4,256,512]{2,1,0:T(8,128)(2,1)S(1)} %pad_maximum_fusion.4.q_ref, bf16[256,1024]{1,0:T(8,128)(2,1)S(1)} %copy-done.14, bf16[256,1024]{1,0:T(8,128)(2,1)S(1)} %copy-done.18, ...), custom_call_target="tpu_custom_call" | custom-call | flops 2147483648 | bytes 4194304 | tf_op jit(solution)/shard_map/ctx_attend/pallas_call | solution.py:148
  141.0 9.8 %mem_attend.4 = (bf16[4,256,512]{2,1,0:T(8,128)(2,1)S(1)}, f32[4,1,8,256]{3,2,1,0:T(8,128)S(1)}) custom-call(s32[4,8]{1,0:T(4,128)S(1)} %copy.25.info, bf16[4,256,512]{2,1,0:T(8,128)(2,1)S(1)} %pad_maximum_fusion.q_ref, bf16[2048,512]{1,0:T(8,128)(2,1)} %bitcast.77, bf16[2048,512]{1,0:T(8,128)(2,1)} %collective-permute-done.6.k1, ...), custom_call_target="tpu_custom_call" | custom-call | flops 2147483648 | bytes 4194304 | tf_op jit(solution)/shard_map/mem_attend/pallas_call | solution.py:177
  156.3 9.6 %mem_attend.5 = (bf16[4,256,512]{2,1,0:T(8,128)(2,1)S(1)}, f32[4,1,8,256]{3,2,1,0:T(8,128)S(1)}) custom-call(s32[4,8]{1,0:T(4,128)S(1)} %copy.25.info, bf16[4,256,512]{2,1,0:T(8,128)(2,1)S(1)} %pad_maximum_fusion.2.q_ref, bf16[2048,512]{1,0:T(8,128)(2,1)} %bitcast.78, bf16[2048,512]{1,0:T(8,128)(2,1)} %collective-permute-done.6.k1, ...), custom_call_target="tpu_custom_call" | custom-call | flops 2147483648 | bytes 4194304 | tf_op jit(solution)/shard_map/mem_attend/pallas_call | solution.py:177
  174.1 2.9 %collective-permute-start.16 = (bf16[2,256,512]{2,1,0:T(8,128)(2,1)}, bf16[2,256,512]{2,1,0:T(8,128)(2,1)}, u32[]{:S(2)}, u32[]{:S(2)}) collective-permute-start(bf16[2,256,512]{2,1,0:T(8,128)(2,1)} %slice.164), channel_id=1, source_target_pairs={{0,4},{1,5},{2,6},{3,7},{12,8},{13,9},{14,10},{15,11},{16,20},{17,... | collective-permute-start | bytes 1572872 | tf_op jit(solution)/shard_map/ppermute | solution.py:228
  177.1 9.0 %ctx_attend.7 = (bf16[4,256,512]{2,1,0:T(8,128)(2,1)S(1)}, f32[4,1,8,256]{3,2,1,0:T(8,128)S(1)}) custom-call(s32[6]{0:T(128)S(1)} %concatenate.71.info, bf16[4,256,512]{2,1,0:T(8,128)(2,1)S(1)} %pad_maximum_fusion.6.q_ref, bf16[256,1024]{1,0:T(8,128)(2,1)S(1)} %copy-done.15, bf16[256,1024]{1,0:T(8,128)(2,1)S(1)} %copy-done.19, ...), custom_call_target="tpu_custom_call" | custom-call | flops 2147483648 | bytes 4194304 | tf_op jit(solution)/shard_map/ctx_attend/pallas_call | solution.py:148
  191.8 9.9 %mem_attend.6 = (bf16[4,256,512]{2,1,0:T(8,128)(2,1)S(1)}, f32[4,1,8,256]{3,2,1,0:T(8,128)S(1)}) custom-call(s32[4,8]{1,0:T(4,128)S(1)} %copy.25.info, bf16[4,256,512]{2,1,0:T(8,128)(2,1)S(1)} %pad_maximum_fusion.4.q_ref, bf16[2048,512]{1,0:T(8,128)(2,1)} %bitcast.79, bf16[2048,512]{1,0:T(8,128)(2,1)} %collective-permute-done.6.k1, ...), custom_call_target="tpu_custom_call" | custom-call | flops 2147483648 | bytes 4194304 | tf_op jit(solution)/shard_map/mem_attend/pallas_call | solution.py:177
  202.8 4.4 %collective-permute-start.37 = (f32[4,1,8,256]{3,2,1,0:T(8,128)S(1)}, f32[4,1,8,256]{3,2,1,0:T(8,128)S(1)}, u32[]{:S(2)}, u32[]{:S(2)}) collective-permute-start(f32[4,1,8,256]{3,2,1,0:T(8,128)S(1)} %get-tuple-element.33.rest_0_), channel_id=1, source_target_pairs={{0,12},{1,13},{2,14},{3,15},{4,8},{5,9},{6,10},{7,11},{8,4},{9,5},... | collective-permute-start | bytes 98312 | tf_op jit(solution)/shard_map/ppermute | solution.py:228
  207.2 9.6 %mem_attend.7 = (bf16[4,256,512]{2,1,0:T(8,128)(2,1)S(1)}, f32[4,1,8,256]{3,2,1,0:T(8,128)S(1)}) custom-call(s32[4,8]{1,0:T(4,128)S(1)} %copy.25.info, bf16[4,256,512]{2,1,0:T(8,128)(2,1)S(1)} %pad_maximum_fusion.6.q_ref, bf16[2048,512]{1,0:T(8,128)(2,1)} %bitcast.80, bf16[2048,512]{1,0:T(8,128)(2,1)} %collective-permute-done.6.k1, ...), custom_call_target="tpu_custom_call" | custom-call | flops 2147483648 | bytes 4194304 | tf_op jit(solution)/shard_map/mem_attend/pallas_call | solution.py:177
  218.4 3.8 %collective-permute-start.48 = (f32[4,1,8,256]{3,2,1,0:T(8,128)S(1)}, f32[4,1,8,256]{3,2,1,0:T(8,128)S(1)}, u32[]{:S(2)}, u32[]{:S(2)}) collective-permute-start(f32[4,1,8,256]{3,2,1,0:T(8,128)S(1)} %get-tuple-element.37.rest_0_), channel_id=1, source_target_pairs={{0,12},{1,13},{2,14},{3,15},{4,8},{5,9},{6,10},{7,11},{8,4},{9,5},... | collective-permute-start | bytes 98312 | tf_op jit(solution)/shard_map/ppermute | solution.py:228
  235.5 4.4 %collective-permute-done.38 = bf16[2,256,512]{2,1,0:T(8,128)(2,1)S(1)} collective-permute-done((bf16[2,256,512]{2,1,0:T(8,128)(2,1)S(1)}, bf16[2,256,512]{2,1,0:T(8,128)(2,1)S(1)}, u32[]{:S(2)}, u32[]{:S(2)}) %collective-permute-start.38) | collective-permute-done | bytes 524320 | tf_op jit(solution)/shard_map/ppermute | solution.py:228
  240.8 6.0 %collective-permute-done.49 = bf16[2,256,512]{2,1,0:T(8,128)(2,1)S(1)} collective-permute-done((bf16[2,256,512]{2,1,0:T(8,128)(2,1)S(1)}, bf16[2,256,512]{2,1,0:T(8,128)(2,1)S(1)}, u32[]{:S(2)}, u32[]{:S(2)}) %collective-permute-start.49) | collective-permute-done | bytes 524320 | tf_op jit(solution)/shard_map/ppermute | solution.py:228
  247.9 4.1 %collective-permute-start.18 = (bf16[256,512]{1,0:T(8,128)(2,1)S(1)}, bf16[256,512]{1,0:T(8,128)(2,1)S(1)}, u32[]{:S(2)}, u32[]{:S(2)}) collective-permute-start(bf16[256,512]{1,0:T(8,128)(2,1)S(1)} %fusion.8), channel_id=1, source_target_pairs={{0,4},{1,5},{2,6},{3,7},{4,0},{5,1},{6,2},{7,3},{8,12},{9,13},{10,... | collective-permute-start | bytes 786440 | tf_op jit(solution)/shard_map/ppermute | solution.py:228
  252.2 8.1 %collective-permute-start.29 = (bf16[256,512]{1,0:T(8,128)(2,1)S(1)}, bf16[256,512]{1,0:T(8,128)(2,1)S(1)}, u32[]{:S(2)}, u32[]{:S(2)}) collective-permute-start(bf16[256,512]{1,0:T(8,128)(2,1)S(1)} %fusion.9), channel_id=1, source_target_pairs={{0,4},{1,5},{2,6},{3,7},{4,0},{5,1},{6,2},{7,3},{8,12},{9,13},{10,... | collective-permute-start | bytes 786440 | tf_op jit(solution)/shard_map/ppermute | solution.py:228
  260.5 11.0 %collective-permute-start.40 = (bf16[256,512]{1,0:T(8,128)(2,1)S(1)}, bf16[256,512]{1,0:T(8,128)(2,1)S(1)}, u32[]{:S(2)}, u32[]{:S(2)}) collective-permute-start(bf16[256,512]{1,0:T(8,128)(2,1)S(1)} %fusion.10), channel_id=1, source_target_pairs={{0,4},{1,5},{2,6},{3,7},{4,0},{5,1},{6,2},{7,3},{8,12},{9,13},{10,... | collective-permute-start | bytes 786440 | tf_op jit(solution)/shard_map/ppermute | solution.py:228
  271.8 6.7 %collective-permute-start.51 = (bf16[256,512]{1,0:T(8,128)(2,1)S(1)}, bf16[256,512]{1,0:T(8,128)(2,1)S(1)}, u32[]{:S(2)}, u32[]{:S(2)}) collective-permute-start(bf16[256,512]{1,0:T(8,128)(2,1)S(1)} %fusion.11), channel_id=1, source_target_pairs={{0,4},{1,5},{2,6},{3,7},{4,0},{5,1},{6,2},{7,3},{8,12},{9,13},{10,... | collective-permute-start | bytes 786440 | tf_op jit(solution)/shard_map/ppermute | solution.py:228
  278.7 4.1 %collective-permute-done.51 = bf16[256,512]{1,0:T(8,128)(2,1)S(1)} collective-permute-done((bf16[256,512]{1,0:T(8,128)(2,1)S(1)}, bf16[256,512]{1,0:T(8,128)(2,1)S(1)}, u32[]{:S(2)}, u32[]{:S(2)}) %collective-permute-start.51) | collective-permute-done | bytes 262176 | tf_op jit(solution)/shard_map/ppermute | solution.py:228
  (252 shorter events, 88.3 us)
Async XLA Ops:
  1.4 19.1 %collective-permute-start.1 = (s32[16,2]{0,1:T(2,128)S(1)}, s32[16,2]{0,1:T(2,128)S(1)}, u32[]{:S(2)}, u32[]{:S(2)}) collective-permute-start(s32[16,2]{0,1:T(2,128)S(1)} %get-tuple-element.78), channel_id=1, source_target_pairs={{0,12},{1,13},{2,14},{3,15},{4,8},{5,9},{6,10},{7,11},{8,4},{9,5},... | collective-permute-start | bytes 392 | tf_op jit(solution)/shard_map/ppermute | solution.py:228
  36.5 26.3 %collective-permute-start.7 = (bf16[2048,256]{1,0:T(8,128)(2,1)}, bf16[2048,256]{1,0:T(8,128)(2,1)S(1)}, u32[]{:S(2)}, u32[]{:S(2)}) collective-permute-start(bf16[2048,256]{1,0:T(8,128)(2,1)} %pad_maximum_fusion.1), channel_id=1, source_target_pairs={{0,2},{1,3},{2,0},{3,1},{4,6},{5,7},{6,4},{7,5},{8,10},{9,11},{10,... | collective-permute-start | bytes 3145736 | tf_op jit(solution)/shard_map/ppermute | solution.py:228
  40.9 25.6 %collective-permute-start.5 = (bf16[2,256,512]{2,1,0:T(8,128)(2,1)}, bf16[2,256,512]{2,1,0:T(8,128)(2,1)}, u32[]{:S(2)}, u32[]{:S(2)}) collective-permute-start(bf16[2,256,512]{2,1,0:T(8,128)(2,1)} %collective-permute-done.4), channel_id=1, source_target_pairs={{4,0},{5,1},{6,2},{7,3},{8,12},{9,13},{10,14},{11,15},{20,16},{21,... | collective-permute-start | bytes 1572872 | tf_op jit(solution)/shard_map/ppermute | solution.py:228
  42.5 50.3 %collective-permute-start.22 = (bf16[2048,256]{1,0:T(8,128)(2,1)}, bf16[2048,256]{1,0:T(8,128)(2,1)S(1)}, u32[]{:S(2)}, u32[]{:S(2)}) collective-permute-start(bf16[2048,256]{1,0:T(8,128)(2,1)} %pad_maximum_fusion.3), channel_id=1, source_target_pairs={{0,2},{1,3},{2,0},{3,1},{4,6},{5,7},{6,4},{7,5},{8,10},{9,11},{10,... | collective-permute-start | bytes 3145736 | tf_op jit(solution)/shard_map/ppermute | solution.py:228
  44.3 63.5 %collective-permute-start.33 = (bf16[2048,256]{1,0:T(8,128)(2,1)}, bf16[2048,256]{1,0:T(8,128)(2,1)S(1)}, u32[]{:S(2)}, u32[]{:S(2)}) collective-permute-start(bf16[2048,256]{1,0:T(8,128)(2,1)} %pad_maximum_fusion.5), channel_id=1, source_target_pairs={{0,2},{1,3},{2,0},{3,1},{4,6},{5,7},{6,4},{7,5},{8,10},{9,11},{10,... | collective-permute-start | bytes 3145736 | tf_op jit(solution)/shard_map/ppermute | solution.py:228
  45.0 44.2 %collective-permute-start.21 = (bf16[2,256,512]{2,1,0:T(8,128)(2,1)}, bf16[2,256,512]{2,1,0:T(8,128)(2,1)}, u32[]{:S(2)}, u32[]{:S(2)}) collective-permute-start(bf16[2,256,512]{2,1,0:T(8,128)(2,1)} %collective-permute-done.20), channel_id=1, source_target_pairs={{4,0},{5,1},{6,2},{7,3},{8,12},{9,13},{10,14},{11,15},{20,16},{21,... | collective-permute-start | bytes 1572872 | tf_op jit(solution)/shard_map/ppermute | solution.py:228
  62.8 78.2 %collective-permute-start.6 = (bf16[2048,512]{1,0:T(8,128)(2,1)}, bf16[2048,512]{1,0:T(8,128)(2,1)}, u32[]{:S(2)}, u32[]{:S(2)}) collective-permute-start(bf16[2048,512]{1,0:T(8,128)(2,1)} %bitcast.76), channel_id=1, source_target_pairs={{0,1},{1,0},{2,3},{3,2},{4,5},{5,4},{6,7},{7,6},{8,9},{9,8},{10,11... | collective-permute-start | bytes 6291464 | tf_op jit(solution)/shard_map/ppermute | solution.py:228
  66.5 74.6 %collective-permute-start.9 = (bf16[2048,512]{1,0:T(8,128)(2,1)}, bf16[2048,512]{1,0:T(8,128)(2,1)}, u32[]{:S(2)}, u32[]{:S(2)}) collective-permute-start(bf16[2048,512]{1,0:T(8,128)(2,1)} %bitcast.82), channel_id=1, source_target_pairs={{0,1},{1,0},{2,3},{3,2},{4,5},{5,4},{6,7},{7,6},{8,9},{9,8},{10,11... | collective-permute-start | bytes 6291464 | tf_op jit(solution)/shard_map/ppermute | solution.py:228
  89.2 20.2 %collective-permute-start.32 = (bf16[2,256,512]{2,1,0:T(8,128)(2,1)}, bf16[2,256,512]{2,1,0:T(8,128)(2,1)S(1)}, u32[]{:S(2)}, u32[]{:S(2)}) collective-permute-start(bf16[2,256,512]{2,1,0:T(8,128)(2,1)} %copy-done.37), channel_id=1, source_target_pairs={{4,0},{5,1},{6,2},{7,3},{8,12},{9,13},{10,14},{11,15},{20,16},{21,... | collective-permute-start | bytes 1572872 | tf_op jit(solution)/shard_map/ppermute | solution.py:228
  92.8 37.4 %collective-permute-start.44 = (bf16[2048,256]{1,0:T(8,128)(2,1)S(1)}, bf16[2048,256]{1,0:T(8,128)(2,1)S(1)}, u32[]{:S(2)}, u32[]{:S(2)}) collective-permute-start(bf16[2048,256]{1,0:T(8,128)(2,1)S(1)} %copy-done.30), channel_id=1, source_target_pairs={{0,2},{1,3},{2,0},{3,1},{4,6},{5,7},{6,4},{7,5},{8,10},{9,11},{10,... | collective-permute-start | bytes 3145736 | tf_op jit(solution)/shard_map/ppermute | solution.py:228
  107.8 19.9 %collective-permute-start.43 = (bf16[2,256,512]{2,1,0:T(8,128)(2,1)}, bf16[2,256,512]{2,1,0:T(8,128)(2,1)}, u32[]{:S(2)}, u32[]{:S(2)}) collective-permute-start(bf16[2,256,512]{2,1,0:T(8,128)(2,1)} %collective-permute-done.42), channel_id=1, source_target_pairs={{4,0},{5,1},{6,2},{7,3},{8,12},{9,13},{10,14},{11,15},{20,16},{21,... | collective-permute-start | bytes 1572872 | tf_op jit(solution)/shard_map/ppermute | solution.py:228
  109.4 21.0 %collective-permute-start.8 = (bf16[2048,256]{1,0:T(8,128)(2,1)S(1)}, bf16[2048,256]{1,0:T(8,128)(2,1)S(1)}, u32[]{:S(2)}, u32[]{:S(2)}) collective-permute-start(bf16[2048,256]{1,0:T(8,128)(2,1)S(1)} %collective-permute-done.7.k2.v2), channel_id=1, source_target_pairs={{0,1},{1,0},{2,3},{3,2},{4,5},{5,4},{6,7},{7,6},{8,9},{9,8},{10,11... | collective-permute-start | bytes 3145736 | tf_op jit(solution)/shard_map/ppermute | solution.py:228
  127.6 26.3 %collective-permute-start.23 = (bf16[2048,256]{1,0:T(8,128)(2,1)S(1)}, bf16[2048,256]{1,0:T(8,128)(2,1)S(1)}, u32[]{:S(2)}, u32[]{:S(2)}) collective-permute-start(bf16[2048,256]{1,0:T(8,128)(2,1)S(1)} %collective-permute-done.22.k2.v2), channel_id=1, source_target_pairs={{0,1},{1,0},{2,3},{3,2},{4,5},{5,4},{6,7},{7,6},{8,9},{9,8},{10,11... | collective-permute-start | bytes 3145736 | tf_op jit(solution)/shard_map/ppermute | solution.py:228
  130.3 61.5 %collective-permute-start.34 = (bf16[2048,256]{1,0:T(8,128)(2,1)S(1)}, bf16[2048,256]{1,0:T(8,128)(2,1)S(1)}, u32[]{:S(2)}, u32[]{:S(2)}) collective-permute-start(bf16[2048,256]{1,0:T(8,128)(2,1)S(1)} %collective-permute-done.33.k2.v2), channel_id=1, source_target_pairs={{0,1},{1,0},{2,3},{3,2},{4,5},{5,4},{6,7},{7,6},{8,9},{9,8},{10,11... | collective-permute-start | bytes 3145736 | tf_op jit(solution)/shard_map/ppermute | solution.py:228
  130.4 72.4 %collective-permute-start.45 = (bf16[2048,256]{1,0:T(8,128)(2,1)S(1)}, bf16[2048,256]{1,0:T(8,128)(2,1)S(1)}, u32[]{:S(2)}, u32[]{:S(2)}) collective-permute-start(bf16[2048,256]{1,0:T(8,128)(2,1)S(1)} %collective-permute-done.44.k2.v2), channel_id=1, source_target_pairs={{0,1},{1,0},{2,3},{3,2},{4,5},{5,4},{6,7},{7,6},{8,9},{9,8},{10,11... | collective-permute-start | bytes 3145736 | tf_op jit(solution)/shard_map/ppermute | solution.py:228
  167.3 18.9 %collective-permute-start.25 = (f32[4,1,8,256]{3,2,1,0:T(8,128)S(1)}, f32[4,1,8,256]{3,2,1,0:T(8,128)S(1)}, u32[]{:S(2)}, u32[]{:S(2)}) collective-permute-start(f32[4,1,8,256]{3,2,1,0:T(8,128)S(1)} %get-tuple-element.29.rest_0_), channel_id=1, source_target_pairs={{0,8},{1,9},{2,10},{3,11},{4,12},{5,13},{6,14},{7,15},{8,0},{9,1},... | collective-permute-start | bytes 98312 | tf_op jit(solution)/shard_map/ppermute | solution.py:228
  168.2 17.9 %collective-permute-start.26 = (f32[4,1,8,256]{3,2,1,0:T(8,128)S(1)}, f32[4,1,8,256]{3,2,1,0:T(8,128)S(1)}, u32[]{:S(2)}, u32[]{:S(2)}) collective-permute-start(f32[4,1,8,256]{3,2,1,0:T(8,128)S(1)} %get-tuple-element.29.rest_0_), channel_id=1, source_target_pairs={{0,12},{1,13},{2,14},{3,15},{4,8},{5,9},{6,10},{7,11},{8,4},{9,5},... | collective-permute-start | bytes 98312 | tf_op jit(solution)/shard_map/ppermute | solution.py:228
  174.1 57.6 %collective-permute-start.16 = (bf16[2,256,512]{2,1,0:T(8,128)(2,1)}, bf16[2,256,512]{2,1,0:T(8,128)(2,1)}, u32[]{:S(2)}, u32[]{:S(2)}) collective-permute-start(bf16[2,256,512]{2,1,0:T(8,128)(2,1)} %slice.164), channel_id=1, source_target_pairs={{0,4},{1,5},{2,6},{3,7},{12,8},{13,9},{14,10},{15,11},{16,20},{17,... | collective-permute-start | bytes 1572872 | tf_op jit(solution)/shard_map/ppermute | solution.py:228
  189.7 43.9 %collective-permute-start.27 = (bf16[2,256,512]{2,1,0:T(8,128)(2,1)}, bf16[2,256,512]{2,1,0:T(8,128)(2,1)}, u32[]{:S(2)}, u32[]{:S(2)}) collective-permute-start(bf16[2,256,512]{2,1,0:T(8,128)(2,1)} %slice.170), channel_id=1, source_target_pairs={{0,4},{1,5},{2,6},{3,7},{12,8},{13,9},{14,10},{15,11},{16,20},{17,... | collective-permute-start | bytes 1572872 | tf_op jit(solution)/shard_map/ppermute | solution.py:228
  240.1 20.2 %collective-permute-start.39 = (bf16[2,256,512]{2,1,0:T(8,128)(2,1)S(1)}, bf16[2,256,512]{2,1,0:T(8,128)(2,1)S(1)}, u32[]{:S(2)}, u32[]{:S(2)}) collective-permute-start(bf16[2,256,512]{2,1,0:T(8,128)(2,1)S(1)} %add_convert_fusion.1), channel_id=1, source_target_pairs={{4,8},{5,9},{6,10},{7,11},{8,4},{9,5},{10,6},{11,7},{20,24},{21,25... | collective-permute-start | bytes 1572872 | tf_op jit(solution)/shard_map/ppermute | solution.py:228
  247.0 24.6 %collective-permute-start.50 = (bf16[2,256,512]{2,1,0:T(8,128)(2,1)S(1)}, bf16[2,256,512]{2,1,0:T(8,128)(2,1)S(1)}, u32[]{:S(2)}, u32[]{:S(2)}) collective-permute-start(bf16[2,256,512]{2,1,0:T(8,128)(2,1)S(1)} %add_convert_fusion), channel_id=1, source_target_pairs={{4,8},{5,9},{6,10},{7,11},{8,4},{9,5},{10,6},{11,7},{20,24},{21,25... | collective-permute-start | bytes 1572872 | tf_op jit(solution)/shard_map/ppermute | solution.py:228
  247.9 30.5 %collective-permute-start.18 = (bf16[256,512]{1,0:T(8,128)(2,1)S(1)}, bf16[256,512]{1,0:T(8,128)(2,1)S(1)}, u32[]{:S(2)}, u32[]{:S(2)}) collective-permute-start(bf16[256,512]{1,0:T(8,128)(2,1)S(1)} %fusion.8), channel_id=1, source_target_pairs={{0,4},{1,5},{2,6},{3,7},{4,0},{5,1},{6,2},{7,3},{8,12},{9,13},{10,... | collective-permute-start | bytes 786440 | tf_op jit(solution)/shard_map/ppermute | solution.py:228
  252.2 26.3 %collective-permute-start.29 = (bf16[256,512]{1,0:T(8,128)(2,1)S(1)}, bf16[256,512]{1,0:T(8,128)(2,1)S(1)}, u32[]{:S(2)}, u32[]{:S(2)}) collective-permute-start(bf16[256,512]{1,0:T(8,128)(2,1)S(1)} %fusion.9), channel_id=1, source_target_pairs={{0,4},{1,5},{2,6},{3,7},{4,0},{5,1},{6,2},{7,3},{8,12},{9,13},{10,... | collective-permute-start | bytes 786440 | tf_op jit(solution)/shard_map/ppermute | solution.py:228
  260.5 18.1 %collective-permute-start.40 = (bf16[256,512]{1,0:T(8,128)(2,1)S(1)}, bf16[256,512]{1,0:T(8,128)(2,1)S(1)}, u32[]{:S(2)}, u32[]{:S(2)}) collective-permute-start(bf16[256,512]{1,0:T(8,128)(2,1)S(1)} %fusion.10), channel_id=1, source_target_pairs={{0,4},{1,5},{2,6},{3,7},{4,0},{5,1},{6,2},{7,3},{8,12},{9,13},{10,... | collective-permute-start | bytes 786440 | tf_op jit(solution)/shard_map/ppermute | solution.py:228
  (72 other events, 737.5 us)

commit v2 on v1

v2 whole, which is shorter than its diff:
```python
import functools

import jax
import jax.numpy as jnp
from jax import lax
from jax.experimental import pallas as pl
from jax.experimental.pallas import tpu as pltpu
from jax.sharding import PartitionSpec as P

H = 16
KVH = 4
HD = 128
QBLK = 256
MROWS = 128
TOPM = 32
CAP = 2
G = H // KVH
WITHIN = 4
LOG2E = 1.4426950408889634
SCALE = HD**-0.5 * LOG2E
MASKED = -1e30
QW = G * HD
QUERY_PLAN = (((0,), "direct"), ((1,), "gather"), ((2, 3), "gather"))
GROUPS = (((0, 1), "scatter"), ((2,), "direct"), ((3,), "direct"))


def wanted_blocks(slots, plane, within, local_count):
    owner = (slots // local_count)[:, None, :]
    holder = plane * WITHIN + (within ^ jnp.arange(WITHIN, dtype=jnp.int32))
    hits = (owner == holder[None, :, None]).astype(jnp.int32)
    rank = jnp.cumsum(hits, axis=2) * hits
    local = (slots % local_count + 1)[:, None, :]
    picked = [jnp.sum(jnp.where(rank == r + 1, local, 0), axis=2) - 1 for r in range(CAP)]
    return jnp.stack(picked, axis=2).reshape(slots.shape[0], WITHIN * CAP)


def lookup_slots(wanted_ids, block_slot):
    hits = wanted_ids[..., None] == jnp.arange(block_slot.shape[0], dtype=jnp.int32)
    return jnp.sum(jnp.where(hits, block_slot, 0), axis=-1)


def scores_of(q, k):
    return lax.dot_general(q, k, (((1,), (1,)), ((), ())), preferred_element_type=jnp.float32)


def attend_heads(q, k, v, allowed, out_ref):
    keys = k.shape[0]
    vx = jnp.concatenate([v, jnp.ones((keys, HD), jnp.bfloat16)], axis=1)
    lane = lax.broadcasted_iota(jnp.int32, (QBLK, HD), 1)
    rows = jnp.zeros((QBLK, HD), jnp.float32)
    ahead = scores_of(q[:, :HD], k)
    for g in range(G):
        s = ahead
        if g + 1 < G:
            ahead = scores_of(q[:, (g + 1) * HD : (g + 2) * HD], k)
        if allowed is not None:
            s = jnp.where(allowed, s, MASKED)
        m = jnp.max(s, axis=1, keepdims=True)
        p = jnp.exp2((s - m) * SCALE).astype(jnp.bfloat16)
        o = jnp.dot(p, vx, preferred_element_type=jnp.float32)
        total = o[:, HD:]
        out_ref[0, :, g * HD : (g + 1) * HD] = (o[:, :HD] / total).astype(jnp.bfloat16)
        rows = jnp.where(lane == g, m * SCALE + jnp.log2(total), rows)
    return rows.T[:8]


def pick_query(slot, q_refs, qbuf):
    if len(q_refs) == 1:
        return q_refs[0][0]
    for i, ref in enumerate(q_refs):

        @pl.when(slot == i)
        def _(ref=ref):
            qbuf[...] = ref[...]

    return qbuf[...]


def ctx_kernel(n_q, info, *refs):
    q_refs = refs[:n_q]
    k0, k1, k2, k3, v0, v1, v2, v3, out_ref, lse_ref, qbuf = refs[n_q:]
    slot = pl.program_id(1)
    plane, within = info[0, 0], info[0, 1]
    target = jnp.bitwise_xor(plane, slot)

    def run(allowed):
        k = jnp.concatenate([k0[...], k1[...], k2[...], k3[...]], axis=0)
        v = jnp.concatenate([v0[...], v1[...], v2[...], v3[...]], axis=0)
        lse_ref[0, 0] = attend_heads(pick_query(slot, q_refs, qbuf), k, v, allowed, out_ref.at[0])

    @pl.when(target > plane)
    def _():
        run(None)

    @pl.when(target == plane)
    def _():
        keys = WITHIN * QBLK
        col = lax.broadcasted_iota(jnp.int32, (QBLK, keys), 1)
        row = lax.broadcasted_iota(jnp.int32, (QBLK, keys), 0)
        key_pos = jnp.bitwise_xor(col // QBLK, within) * QBLK + col % QBLK
        run(key_pos <= within * QBLK + row)

    @pl.when(target < plane)
    def _():
        out_ref[...] = jnp.zeros_like(out_ref)
        lse_ref[...] = jnp.full_like(lse_ref, MASKED)


def mem_kernel(masked, n_q, info, *refs):
    q_refs = refs[:n_q]
    stores = refs[n_q : n_q + WITHIN]
    ctx_lse_ref, out_ref, lse_ref, kbuf, vbuf, qbuf = refs[n_q + WITHIN :]
    slot = pl.program_id(0)
    allowed = None
    keys = WITHIN * CAP * MROWS
    if masked:
        col = lax.broadcasted_iota(jnp.int32, (QBLK, keys), 1) // MROWS
        allowed = jnp.zeros((QBLK, keys), jnp.bool_)
    for n in range(WITHIN * CAP):
        entry = info[1 + slot, n]
        start = pl.multiple_of(jnp.maximum(entry, 0) * MROWS, MROWS)
        rows, to = pl.ds(start, MROWS), slice(n * MROWS, (n + 1) * MROWS)
        kbuf[to, :] = stores[n // CAP][0, rows, :]
        vbuf[to, :] = stores[n // CAP][1, rows, :]
        if masked:
            allowed = allowed | ((col == n) & (entry >= 0))
    query = pick_query(slot, q_refs, qbuf)
    lse_ref[0] = attend_heads(query, kbuf[...], vbuf[...], allowed, out_ref)
    lse_ref[0, G:] = ctx_lse_ref[0, 0, :G]


def scale_kernel(planes, heads, info, *refs):
    um_refs, uc_refs, gate_ref = refs[:heads], refs[heads : 2 * heads], refs[2 * heads]
    lse_refs, out_refs = refs[2 * heads + 1 : 2 * heads + 1 + planes], refs[2 * heads + 1 + planes :]
    slot = pl.program_id(0)
    for h in range(heads):
        parts = [lse_refs[k][h, jnp.bitwise_xor(slot, k)] for k in range(planes)]
        top = functools.reduce(jnp.maximum, parts)
        total = functools.reduce(jnp.add, [jnp.exp2(p - top) for p in parts])
        weight = jnp.exp2(parts[0] - top) / total * gate_ref[h]
        wt = jnp.concatenate([weight, jnp.zeros((HD - 8, QBLK), jnp.float32)], axis=0).T
        for g in range(G):
            cols = slice(g * HD, (g + 1) * HD)
            term = wt[:, g : g + 1] * um_refs[h][0, :, cols].astype(jnp.float32)
            term += wt[:, G + g : G + g + 1] * uc_refs[h][0, 0, :, cols].astype(jnp.float32)
            term = term.astype(jnp.bfloat16)
            if len(out_refs) == 1:
                out_refs[0][0, h, :, cols] = term
                continue
            for i, ref in enumerate(out_refs):

                @pl.when(slot == i)
                def _(ref=ref):
                    ref[h, :, cols] = term


PARAMS = pltpu.CompilerParams(vmem_limit_bytes=20 * 1024 * 1024)
PACK_PARAMS = pltpu.CompilerParams(vmem_limit_bytes=60 * 1024 * 1024)
SMALL = pl.CostEstimate(flops=1000, bytes_accessed=1000, transcendentals=0)


def query_place(head):
    return next((n, heads.index(head)) for n, (heads, _) in enumerate(QUERY_PLAN) if head in heads)


def whole(shape):
    return pl.BlockSpec(shape, lambda *_: (0,) * len(shape))


def query_specs(qs, chosen):
    if len(qs) == 1:
        return [pl.BlockSpec((1, QBLK, QW), lambda *i: (jnp.bitwise_xor(i[-1][0, 0], i[-2]), 0, chosen(*i)))]
    return [pl.BlockSpec((QBLK, QW), lambda *i: (0, chosen(*i)))] * len(qs)


def ctx_call(info, qs, sources, first, count, planes):
    kspec = pl.BlockSpec((QBLK, HD), lambda h, j, info: (0, first + h))
    vspec = pl.BlockSpec((QBLK, HD), lambda h, j, info: (0, KVH + first + h))
    return pl.pallas_call(
        functools.partial(ctx_kernel, len(qs)),
        grid_spec=pltpu.PrefetchScalarGridSpec(
            num_scalar_prefetch=1,
            grid=(count, planes),
            in_specs=query_specs(qs, lambda h, j, info: query_place(first)[1] + h) + [kspec] * WITHIN + [vspec] * WITHIN,
            out_specs=[
                pl.BlockSpec((1, 1, QBLK, QW), lambda h, j, info: (h, j, 0, 0)),
                pl.BlockSpec((1, 1, 8, QBLK), lambda h, j, info: (h, j, 0, 0)),
            ],
            scratch_shapes=[pltpu.VMEM((QBLK, QW), jnp.bfloat16)],
        ),
        out_shape=[
            jax.ShapeDtypeStruct((count, planes, QBLK, QW), jnp.bfloat16),
            jax.ShapeDtypeStruct((count, planes, 8, QBLK), jnp.float32),
        ],
        compiler_params=PARAMS,
        cost_estimate=SMALL,
        name="ctx_attend",
    )(info, *qs, *sources, *sources)


def mem_call(info, qs, stores, ctx_lse, head, nth, planes, masked):
    keys = WITHIN * CAP * MROWS
    return pl.pallas_call(
        functools.partial(mem_kernel, masked, len(qs)),
        grid_spec=pltpu.PrefetchScalarGridSpec(
            num_scalar_prefetch=1,
            grid=(planes,),
            in_specs=query_specs(qs, lambda j, info: query_place(head)[1])
            + [whole(stores[0].shape)] * WITHIN
            + [pl.BlockSpec((1, 1, 8, QBLK), lambda j, info: (nth, j, 0, 0))],
            out_specs=[
                pl.BlockSpec((1, QBLK, QW), lambda j, info: (j, 0, 0)),
                pl.BlockSpec((1, 8, QBLK), lambda j, info: (j, 0, 0)),
            ],
            scratch_shapes=[
                pltpu.VMEM((keys, HD), jnp.bfloat16),
                pltpu.VMEM((keys, HD), jnp.bfloat16),
                pltpu.VMEM((QBLK, QW), jnp.bfloat16),
            ],
        ),
        out_shape=[
            jax.ShapeDtypeStruct((planes, QBLK, QW), jnp.bfloat16),
            jax.ShapeDtypeStruct((planes, 8, QBLK), jnp.float32),
        ],
        compiler_params=PARAMS,
        cost_estimate=SMALL,
        name="mem_attend",
    )(info, *qs, *stores, ctx_lse)


def scale_call(info, ums, ucs, gate_rows, lses, apart):
    heads, planes = len(ums), ums[0].shape[0]
    if apart:
        out_specs = [whole((heads, QBLK, QW))] * planes
        out_shape = [jax.ShapeDtypeStruct((heads, QBLK, QW), jnp.bfloat16)] * planes
    else:
        out_specs = [pl.BlockSpec((1, heads, QBLK, QW), lambda j, info: (jnp.bitwise_xor(info[0, 0], j), 0, 0, 0))]
        out_shape = [jax.ShapeDtypeStruct((planes, heads, QBLK, QW), jnp.bfloat16)]
    return pl.pallas_call(
        functools.partial(scale_kernel, planes, heads),
        grid_spec=pltpu.PrefetchScalarGridSpec(
            num_scalar_prefetch=1,
            grid=(planes,),
            in_specs=[pl.BlockSpec((1, QBLK, QW), lambda j, info: (j, 0, 0))] * heads
            + [pl.BlockSpec((1, 1, QBLK, QW), lambda j, info: (0, j, 0, 0))] * heads
            + [whole((heads, 8, 1))]
            + [whole((heads, planes, 8, QBLK))] * planes,
            out_specs=out_specs,
        ),
        out_shape=out_shape,
        compiler_params=PARAMS,
        cost_estimate=SMALL,
        name="scale_mix",
    )(info, *ums, *ucs, gate_rows, *lses)


def pack_kernel(heads, with_ctx, q, ck, cv, k, v, *outs):
    for n, head in enumerate(heads):
        cols = slice(head * HD, (head + 1) * HD)
        outs[n][0] = k[:, cols]
        outs[n][1] = v[:, cols]
    if with_ctx:
        for n, (chunk, _) in enumerate(QUERY_PLAN):
            outs[len(heads) + n][...] = q[:, chunk[0] * QW : (chunk[-1] + 1) * QW]
        outs[-1][:, : KVH * HD] = ck[...]
        outs[-1][:, KVH * HD :] = cv[...]


def pack_call(heads, with_ctx, q, ck, cv, k, v):
    rows, steps = k.shape[0], 4
    wide = len(heads) > 1
    part, piece = rows // steps, q.shape[0] // steps

    def row_block(r, c):
        return pl.BlockSpec((r, c), lambda i: (i, 0))

    shapes, specs = [], []
    for _ in heads:
        shapes.append(jax.ShapeDtypeStruct((2, rows, HD), jnp.bfloat16))
        specs.append(pl.BlockSpec((2, part, HD), lambda i: (0, i, 0)))
    if with_ctx:
        for chunk, _ in QUERY_PLAN:
            shapes.append(jax.ShapeDtypeStruct((q.shape[0], len(chunk) * QW), jnp.bfloat16))
            specs.append(row_block(piece, len(chunk) * QW))
        shapes.append(jax.ShapeDtypeStruct((ck.shape[0], 2 * KVH * HD), jnp.bfloat16))
        specs.append(row_block(piece, 2 * KVH * HD))
    ctx = row_block(piece, KVH * HD)
    store = row_block(part, (KVH if wide else 1) * HD)
    return pl.pallas_call(
        functools.partial(pack_kernel, heads, with_ctx),
        grid=(steps,),
        in_specs=[row_block(piece, KVH * QW), ctx, ctx, store, store],
        out_specs=specs,
        out_shape=shapes,
        compiler_params=PACK_PARAMS,
        cost_estimate=SMALL,
        name="pack_heads",
    )(q, ck, cv, k, v)


class Order:
    def __init__(self):
        self.last = ()

    def before(self, *arrays):
        if not self.last:
            return arrays
        return lax.optimization_barrier((*arrays, *self.last))[: len(arrays)]

    def done(self, *arrays):
        self.last = arrays


def on_device(
    queries, ctx_keys, ctx_values, store_keys, store_values, block_ids, block_slot, gate_logit
):
    devices = lax.axis_size("seq")
    planes = devices // WITHIN
    me = lax.axis_index("seq")
    plane, within = me // WITHIN, me % WITHIN
    local_count = store_keys.shape[0]
    masked = devices * CAP != TOPM

    def xor(x, bits):
        return lax.ppermute(x, "seq", [(i, i ^ bits) for i in range(devices)])

    def all_planes(x):
        return [x] + [xor(x, k * WITHIN) for k in range(1, planes)]

    columns = [[p * WITHIN + w for p in range(planes)] for w in range(WITHIN)]
    keys = store_keys.reshape(local_count * MROWS, KVH * HD)
    values = store_values.reshape(local_count * MROWS, KVH * HD)
    order = Order()

    ids = all_planes(block_ids.reshape(-1))
    kv, *q_chunks, ctx_own = pack_call((0,), True, queries, ctx_keys, ctx_values, keys, values)
    ctx_far = xor(ctx_own, 2)
    own = [kv]
    far = [xor(kv, 2)]
    order.done(ctx_own, *ids)
    own += pack_call((1, 2, 3), False, *order.before(queries, ctx_keys, ctx_values, keys, values))
    order.done(own[1])
    far += [xor(part, 2) for part in own[1:]]
    ctx_near = xor(ctx_own, 1)
    near = [xor(part, 1) for part in own]
    ctx_diag = xor(ctx_far, 1)

    wanted = wanted_blocks(lookup_slots(jnp.stack(ids), block_slot), plane, within, local_count)
    info = jnp.concatenate([jnp.stack([plane, within] + [plane] * 6)[None], wanted]).astype(jnp.int32)

    gate = 1.0 / (1.0 + jnp.exp(-gate_logit))
    gate_rows = jnp.concatenate([gate.reshape(KVH, G), 1.0 - gate.reshape(KVH, G)], axis=1)[:, :, None]

    def spread_queries(part, how):
        if how == "direct":
            return all_planes(part)
        return [lax.all_gather(part, "seq", axis=0, axis_index_groups=columns)]

    spread = [spread_queries(part, how) for part, (_, how) in zip(q_chunks, QUERY_PLAN, strict=True)]
    sources = (ctx_own, ctx_near, ctx_far, ctx_diag)
    diag = [None] * KVH

    def fetch_step(head):
        (far[head],) = order.before(far[head])
        order.done(far[head])
        diag[head] = xor(far[head], 1)

    def ctx_step(first, count):
        qs = spread[query_place(first)[0]]
        args = order.before(info, *qs, *sources)
        n = len(qs) + 1
        uc, lse = ctx_call(args[0], args[1:n], args[n:], first, count, planes)
        order.done(lse)
        return uc, lse

    def mem_step(head, ctx_lse):
        qs = spread[query_place(head)[0]]
        args = order.before(info, *qs, own[head], near[head], far[head], diag[head], ctx_lse)
        n = len(qs) + 1
        um, lse = mem_call(args[0], args[1:n], args[n : n + WITHIN], args[n + WITHIN], head, 0, planes, masked)
        order.done(lse)
        return um, lse

    def exchange(parts):
        return all_planes(jnp.stack([lse for _, lse in parts]))

    def scale_step(nth, ums, ucs, lses):
        group, how = GROUPS[nth]
        n, m = len(ums), len(ums) + len(ucs)
        args = order.before(*ums, *ucs, *lses)
        gates = gate_rows[group[0] : group[-1] + 1]
        parts = scale_call(info, args[:n], args[n:m], gates, args[m:], how == "direct")
        order.done(*parts[:1])
        if how == "direct":
            return [parts[0]] + [xor(parts[k], k * WITHIN) for k in range(1, planes)]
        return [lax.psum_scatter(parts[0], "seq", scatter_dimension=0, axis_index_groups=columns)]

    def total(parts):
        return sum(part.astype(jnp.float32) for part in parts).astype(jnp.bfloat16)

    fetch_step(0)
    uc0, ctx_lse0 = ctx_step(0, 1)
    mem0 = mem_step(0, ctx_lse0)
    fetch_step(1)
    uc1, ctx_lse1 = ctx_step(1, 1)
    mem1 = mem_step(1, ctx_lse1)
    lses = exchange([mem0, mem1])
    fetch_step(2)
    uc2, ctx_lse2 = ctx_step(2, 1)
    coming = [scale_step(0, [mem0[0], mem1[0]], [uc0, uc1], lses)]
    mem2 = mem_step(2, ctx_lse2)
    lses = exchange([mem2])
    fetch_step(3)
    uc3, ctx_lse3 = ctx_step(3, 1)
    coming.append(scale_step(1, [mem2[0]], [uc2], lses))
    mem3 = mem_step(3, ctx_lse3)
    coming.append(scale_step(2, [mem3[0]], [uc3], exchange([mem3])))
    return jnp.concatenate([part for parts in coming for part in total(parts)], axis=1)


def solution(mesh):
    placed = (
        P(("groups", "seq"), None),
        P(("groups", "seq"), None),
        P(("groups", "seq"), None),
        P(("groups", "seq"), None, None),
        P(("groups", "seq"), None, None),
        P(("groups", "seq"), None),
        P("groups"),
        P(),
    )
    return jax.shard_map(
        on_device, mesh=mesh, in_specs=placed, out_specs=P(("groups", "seq"), None), check_vma=False
    )
```

time: 285 us -> 230 us (0.81)
  starting transfers between devices: 85.7 us -> 47.7 us
  waiting for transfers between devices: 76.5 us -> 59.7 us
  other arithmetic: 20.5 us -> 4.02 us
  between operations: 0.93 us -> 13.5 us
    ppermute x52 -> x36, starting transfers between devices: 85.7 us -> 47.6 us  [xor(): return lax.ppermute(x, 'seq', [(i, i ^ bits) for i in range(devices)])]
    ppermute x52 -> x36, waiting for transfers between devices: 76.5 us -> 59.6 us  [xor(): return lax.ppermute(x, 'seq', [(i, i ^ bits) for i in range(devices)])]
    unnamed x89 -> x66, local copies, waits for them, and re-layouts: 6.87 us -> 14.5 us
    concatenate x9 -> x2, other arithmetic: 8.19 us -> 1.11 us  [the longest x1 1.1 us: on_device(): jnp.concatenate([part for parts in coming for part in total(parts)], axis=1)]
    select_n x8 -> x0, other arithmetic: 4.57 us -> none  [the longest x4 4.36 us: spread_queries(): far = jnp.where(inner, crossed, handed)]
    slice x11 -> x5, local copies, waits for them, and re-layouts: 4.56 us -> 0.26 us  [scale_step(): gates = gate_rows[group[0]:group[-1] + 1]]
    convert_element_type x8 -> x1, other arithmetic: 2.94 us -> 0.07 us  [wanted_blocks(): hits = (owner == holder[None, :, None]).astype(jnp.int32)]
    pallas_call x12 -> x13, Pallas kernels: 85.8 us -> 86.8 us  [the longest x4 35.8 us: mem_call(): pl.pallas_call(functools.partial(mem_kernel, masked, len(qs)), grid_spec=...]
  transfers between devices with their start and end apart: 52 -> 39, of which waited for: 9 -> 13; matrix products, arithmetic and copies ran while one was open for 9% -> 2% of each run, Pallas kernels for 30% -> 35%
where the time goes in v2:
time: 230 us; the launch traced here: 228 us
  Pallas kernels  86.8 us (38%)
  waiting for transfers between devices  59.7 us (26%)
  starting transfers between devices  47.7 us (21%)
  local copies, waits for them, and re-layouts  16.2 us (7%)
  between operations  13.5 us (6%)
  other arithmetic  4.02 us (2%)
    ppermute x36, waiting for transfers between devices, xor(): return lax.ppermute(x, 'seq', [(i, i ^ bits) for i in range(devices)])  59.6 us
    ppermute x36, starting transfers between devices, xor(): return lax.ppermute(x, 'seq', [(i, i ^ bits) for i in range(devices)])  47.6 us
    pallas_call x4, Pallas kernels, mem_call(): pl.pallas_call(functools.partial(mem_kernel, masked, len(qs)), grid_spec=...  35.8 us
    pallas_call x4, Pallas kernels, ctx_call(): pl.pallas_call(functools.partial(ctx_kernel, len(qs)), grid_spec=pltpu.Pr...  29.8 us
    unnamed x66, local copies, waits for them, and re-layouts  14.5 us
    pallas_call x3, Pallas kernels, scale_call(): pl.pallas_call(functools.partial(scale_kernel, planes, heads), grid_spec=...  12.2 us
    pallas_call x2, Pallas kernels, pack_call(): pl.pallas_call(functools.partial(pack_kernel, heads, with_ctx), grid=(ste...  9 us
  transfers between devices with their start and end apart: 39, of which 13 were waited for; matrix products, arithmetic and copies ran while one was open for 2% of the time, Pallas kernels for 35%

profile of v2, /device:TPU:0, one launch (start us, length us, event | category | flops | bytes accessed | tf_op | source)
XLA Modules:
  0.0 227.8 jit_solution(13288799456322459691)
XLA Ops:
  6.5 4.0 %pack_heads.2 = (bf16[2,2048,128]{2,1,0:T(8,128)(2,1)}, bf16[256,512]{1,0:T(8,128)(2,1)}, bf16[256,512]{1,0:T(8,128)(2,1)}, bf16[256,1024]{1,0:T(8,128)(2,1)}, bf16[256,1024]{1,0:T(8,128)(2,1)}) custom-call(bf16[256,2048]{1,0:T(8,128)(2,1)} %q.2, bf16[256,512]{1,0:T(8,128)(2,1)} %ck.2, bf16[256,512]{1,0:T(8,128)(2,1)} %cv.2, bf16[2048,512]{1,0:T(8,128)(2,1)} %bitcast.50, ...), custom_call_target="tpu_custom_call" | custom-call | flops 1000 | bytes 1000 | tf_op jit(solution)/shard_map/pack_heads/pallas_call | solution.py:289
  10.6 3.0 %collective-permute-start.7 = (bf16[2,2048,128]{2,1,0:T(8,128)(2,1)}, bf16[2,2048,128]{2,1,0:T(8,128)(2,1)}, u32[]{:S(2)}, u32[]{:S(2)}) collective-permute-start(bf16[2,2048,128]{2,1,0:T(8,128)(2,1)} %get-tuple-element.149.refs_4_), channel_id=1, source_target_pairs={{0,2},{1,3},{2,0},{3,1},{4,6},{5,7},{6,4},{7,5},{8,10},{9,11},{10,... | collective-permute-start | bytes 3145736 | tf_op jit(solution)/shard_map/ppermute | solution.py:325
  18.8 6.2 %collective-permute-done = s32[32]{0:T(128)S(1)} collective-permute-done((s32[32]{0:T(128)S(1)}, s32[32]{0:T(128)S(1)}, u32[]{:S(2)}, u32[]{:S(2)}) %collective-permute-start) | collective-permute-done | bytes 160 | tf_op jit(solution)/shard_map/ppermute | solution.py:325
  25.0 8.6 %collective-permute-start.2 = (s32[32]{0:T(128)S(1)}, s32[32]{0:T(128)S(1)}, u32[]{:S(2)}, u32[]{:S(2)}) collective-permute-start(s32[32]{0:T(128)S(1)} %bitcast.58), channel_id=1, source_target_pairs={{0,12},{1,13},{2,14},{3,15},{4,8},{5,9},{6,10},{7,11},{8,4},{9,5},... | collective-permute-start | bytes 392 | tf_op jit(solution)/shard_map/ppermute | solution.py:325
  35.1 5.0 %pack_heads.3 = (bf16[2,2048,128]{2,1,0:T(8,128)(2,1)}, bf16[2,2048,128]{2,1,0:T(8,128)(2,1)}, bf16[2,2048,128]{2,1,0:T(8,128)(2,1)}) custom-call(bf16[256,2048]{1,0:T(8,128)(2,1)} %q.2, bf16[256,512]{1,0:T(8,128)(2,1)} %ck.2, bf16[256,512]{1,0:T(8,128)(2,1)} %cv.2, bf16[2048,512]{1,0:T(8,128)(2,1)} %bitcast.51, bf16[2048,512]{1,0:T(8,128)(2,1)} %bitcast.53), custom_call_target="tpu_custom_call" | custom-call | flops 1000 | bytes 1000 | tf_op jit(solution)/shard_map/pack_heads/pallas_call | solution.py:289
  47.2 6.3 %collective-permute-done.5.refs_3_ = bf16[256,512]{1,0:T(8,128)(2,1)S(1)} collective-permute-done((bf16[256,512]{1,0:T(8,128)(2,1)S(1)}, bf16[256,512]{1,0:T(8,128)(2,1)S(1)}, u32[]{:S(2)}, u32[]{:S(2)}) %collective-permute-start.5) | collective-permute-done | bytes 262176 | tf_op jit(solution)/shard_map/ppermute | solution.py:325
  56.1 7.6 %ctx_attend.4 = (bf16[1,4,256,512]{3,2,1,0:T(8,128)(2,1)S(1)}, f32[1,4,8,256]{3,2,1,0:T(8,128)S(1)}) custom-call(s32[5,8]{1,0:T(8,128)S(1)} %pad_add_fusion.1.info, bf16[256,512]{1,0:T(8,128)(2,1)S(1)} %copy-done.10, bf16[256,512]{1,0:T(8,128)(2,1)S(1)} %collective-permute-done.3.refs_1_, bf16[256,512]{1,0:T(8,128)(2,1)S(1)} %collective-permute-done.4.refs_2_, ...), custom_call_target="tpu_custom_call" | custom-call | flops 1000 | bytes 1000 | tf_op jit(solution)/shard_map/ctx_attend/pallas_call | solution.py:179
  64.7 9.1 %mem_attend.4 = (bf16[4,256,512]{2,1,0:T(8,128)(2,1)S(1)}, f32[4,8,256]{2,1,0:T(8,128)S(1)}) custom-call(s32[5,8]{1,0:T(8,128)S(1)} %pad_add_fusion.1.info, bf16[256,512]{1,0:T(8,128)(2,1)S(1)} %copy-done.10, bf16[256,512]{1,0:T(8,128)(2,1)S(1)} %collective-permute-done.3.refs_1_, bf16[256,512]{1,0:T(8,128)(2,1)S(1)} %collective-permute-done.4.refs_2_, ...), custom_call_target="tpu_custom_call" | custom-call | flops 1000 | bytes 1000 | tf_op jit(solution)/shard_map/mem_attend/pallas_call | solution.py:203
  77.4 7.3 %ctx_attend.5 = (bf16[1,4,256,512]{3,2,1,0:T(8,128)(2,1)S(1)}, f32[1,4,8,256]{3,2,1,0:T(8,128)S(1)}) custom-call(s32[5,8]{1,0:T(8,128)S(1)} %pad_add_fusion.1.info, bf16[4,256,512]{2,1,0:T(8,128)(2,1)S(1)} %bitcast.38, bf16[256,1024]{1,0:T(8,128)(2,1)S(1)} %copy-done.2, bf16[256,1024]{1,0:T(8,128)(2,1)S(1)} %collective-permute-done.9.refs_5_.refs_9_.refs_2_.refs_6_, ...), custom_call_target="tpu_custom_call" | custom-call | flops 1000 | bytes 1000 | tf_op jit(solution)/shard_map/ctx_attend/pallas_call | solution.py:179
  85.8 8.9 %mem_attend.5 = (bf16[4,256,512]{2,1,0:T(8,128)(2,1)S(1)}, f32[4,8,256]{2,1,0:T(8,128)S(1)}) custom-call(s32[5,8]{1,0:T(8,128)S(1)} %pad_add_fusion.1.info, bf16[4,256,512]{2,1,0:T(8,128)(2,1)S(1)} %bitcast.39, bf16[2,2048,128]{2,1,0:T(8,128)(2,1)S(1)} %copy-done.21, bf16[2,2048,128]{2,1,0:T(8,128)(2,1)} %collective-permute-done.12.refs_2_, ...), custom_call_target="tpu_custom_call" | custom-call | flops 1000 | bytes 1000 | tf_op jit(solution)/shard_map/mem_attend/pallas_call | solution.py:203
  95.8 4.0 %collective-permute-start.15 = (f32[2,4,8,256]{3,2,1,0:T(8,128)S(1)}, f32[2,4,8,256]{3,2,1,0:T(8,128)S(1)}, u32[]{:S(2)}, u32[]{:S(2)}) collective-permute-start(f32[2,4,8,256]{3,2,1,0:T(8,128)S(1)} %pad_maximum_fusion.1.refs_5_), channel_id=1, source_target_pairs={{0,4},{1,5},{2,6},{3,7},{4,0},{5,1},{6,2},{7,3},{8,12},{9,13},{10,... | collective-permute-start | bytes 196616 | tf_op jit(solution)/shard_map/ppermute | solution.py:325
  103.9 7.6 %ctx_attend.6 = (bf16[1,4,256,512]{3,2,1,0:T(8,128)(2,1)S(1)}, f32[1,4,8,256]{3,2,1,0:T(8,128)S(1)}) custom-call(s32[5,8]{1,0:T(8,128)S(1)} %pad_add_fusion.1.info, bf16[4,256,1024]{2,1,0:T(8,128)(2,1)S(1)} %bitcast.34, bf16[256,1024]{1,0:T(8,128)(2,1)S(1)} %copy-done.2, bf16[256,1024]{1,0:T(8,128)(2,1)S(1)} %collective-permute-done.9.refs_5_.refs_9_.refs_2_.refs_6_, ...), custom_call_target="tpu_custom_call" | custom-call | flops 1000 | bytes 1000 | tf_op jit(solution)/shard_map/ctx_attend/pallas_call | solution.py:179
  112.6 4.0 %scale_mix.3 = bf16[4,2,256,512]{3,2,1,0:T(8,128)(2,1)S(1)} custom-call(s32[5,8]{1,0:T(8,128)S(1)} %pad_add_fusion.1.info, bf16[4,256,512]{2,1,0:T(8,128)(2,1)S(1)} %copy-done.25, bf16[4,256,512]{2,1,0:T(8,128)(2,1)S(1)} %copy-done.29, bf16[1,4,256,512]{3,2,1,0:T(8,128)(2,1)S(1)} %copy-done.23, bf16[1,4,256,512]{3,2,1,0:T(8,128)(2,1)S(1)} %copy-done.27, ...), custom_call_target="tpu_custom_call" | custom-call | flops 1000 | bytes 1000 | tf_op jit(solution)/shard_map/scale_mix/pallas_call | solution.py:239
  122.4 8.9 %mem_attend.6 = (bf16[4,256,512]{2,1,0:T(8,128)(2,1)S(1)}, f32[4,8,256]{2,1,0:T(8,128)S(1)}) custom-call(s32[5,8]{1,0:T(8,128)S(1)} %pad_add_fusion.1.info, bf16[4,256,1024]{2,1,0:T(8,128)(2,1)S(1)} %bitcast.35, bf16[2,2048,128]{2,1,0:T(8,128)(2,1)} %get-tuple-element.196.refs_1_, bf16[2,2048,128]{2,1,0:T(8,128)(2,1)S(1)} %collective-permute-done.19.refs_2_, ...), custom_call_target="tpu_custom_call" | custom-call | flops 1000 | bytes 1000 | tf_op jit(solution)/shard_map/mem_attend/pallas_call | solution.py:203
  132.2 11.8 %collective-permute-done.24.refs_3_ = bf16[2,2048,128]{2,1,0:T(8,128)(2,1)} collective-permute-done((bf16[2,2048,128]{2,1,0:T(8,128)(2,1)}, bf16[2,2048,128]{2,1,0:T(8,128)(2,1)}, u32[]{:S(2)}, u32[]{:S(2)}) %collective-permute-start.24) | collective-permute-done | bytes 1048608 | tf_op jit(solution)/shard_map/ppermute | solution.py:325
  151.0 7.4 %ctx_attend.7 = (bf16[1,4,256,512]{3,2,1,0:T(8,128)(2,1)S(1)}, f32[1,4,8,256]{3,2,1,0:T(8,128)S(1)}) custom-call(s32[5,8]{1,0:T(8,128)S(1)} %pad_add_fusion.1.info, bf16[4,256,1024]{2,1,0:T(8,128)(2,1)S(1)} %bitcast.36, bf16[256,1024]{1,0:T(8,128)(2,1)S(1)} %copy-done.2, bf16[256,1024]{1,0:T(8,128)(2,1)S(1)} %copy-done.4, ...), custom_call_target="tpu_custom_call" | custom-call | flops 1000 | bytes 1000 | tf_op jit(solution)/shard_map/ctx_attend/pallas_call | solution.py:179
  158.5 4.5 %scale_mix.4 = (bf16[1,256,512]{2,1,0:T(8,128)(2,1)S(1)}, bf16[1,256,512]{2,1,0:T(8,128)(2,1)}, bf16[1,256,512]{2,1,0:T(8,128)(2,1)}, bf16[1,256,512]{2,1,0:T(8,128)(2,1)}) custom-call(s32[5,8]{1,0:T(8,128)S(1)} %pad_add_fusion.1.info, bf16[4,256,512]{2,1,0:T(8,128)(2,1)S(1)} %copy-done.16, bf16[1,4,256,512]{3,2,1,0:T(8,128)(2,1)S(1)} %copy-done.12, ...), custom_call_target="tpu_custom_call" | custom-call | flops 1000 | bytes 1000 | tf_op jit(solution)/shard_map/scale_mix/pallas_call | solution.py:239
  163.1 4.4 %collective-permute-start.27 = (bf16[1,256,512]{2,1,0:T(8,128)(2,1)}, bf16[1,256,512]{2,1,0:T(8,128)(2,1)}, u32[]{:S(2)}, u32[]{:S(2)}) collective-permute-start(bf16[1,256,512]{2,1,0:T(8,128)(2,1)} %get-tuple-element.222), channel_id=1, source_target_pairs={{0,12},{1,13},{2,14},{3,15},{4,8},{5,9},{6,10},{7,11},{8,4},{9,5},... | collective-permute-start | bytes 786440 | tf_op jit(solution)/shard_map/ppermute | solution.py:325
  167.5 9.0 %mem_attend.7 = (bf16[4,256,512]{2,1,0:T(8,128)(2,1)S(1)}, f32[4,8,256]{2,1,0:T(8,128)S(1)}) custom-call(s32[5,8]{1,0:T(8,128)S(1)} %pad_add_fusion.1.info, bf16[4,256,1024]{2,1,0:T(8,128)(2,1)S(1)} %bitcast.37, bf16[2,2048,128]{2,1,0:T(8,128)(2,1)S(1)} %copy-done.19, bf16[2,2048,128]{2,1,0:T(8,128)(2,1)} %collective-permute-done.28.refs_2_, ...), custom_call_target="tpu_custom_call" | custom-call | flops 1000 | bytes 1000 | tf_op jit(solution)/shard_map/mem_attend/pallas_call | solution.py:203
  178.0 5.6 %collective-permute-done.30.refs_4_ = f32[1,4,8,256]{3,2,1,0:T(8,128)S(1)} collective-permute-done((f32[1,4,8,256]{3,2,1,0:T(8,128)S(1)}, f32[1,4,8,256]{3,2,1,0:T(8,128)S(1)}, u32[]{:S(2)}, u32[]{:S(2)}) %collective-permute-start.30) | collective-permute-done | bytes 32800 | tf_op jit(solution)/shard_map/ppermute | solution.py:325
  185.4 6.3 %collective-permute-done.31.refs_5_ = f32[1,4,8,256]{3,2,1,0:T(8,128)S(1)} collective-permute-done((f32[1,4,8,256]{3,2,1,0:T(8,128)S(1)}, f32[1,4,8,256]{3,2,1,0:T(8,128)S(1)}, u32[]{:S(2)}, u32[]{:S(2)}) %collective-permute-start.31) | collective-permute-done | bytes 32800 | tf_op jit(solution)/shard_map/ppermute | solution.py:325
  193.0 3.6 %scale_mix.5 = (bf16[1,256,512]{2,1,0:T(8,128)(2,1)S(1)}, bf16[1,256,512]{2,1,0:T(8,128)(2,1)S(1)}, bf16[1,256,512]{2,1,0:T(8,128)(2,1)S(1)}, bf16[1,256,512]{2,1,0:T(8,128)(2,1)S(1)}) custom-call(s32[5,8]{1,0:T(8,128)S(1)} %pad_add_fusion.1.info, bf16[4,256,512]{2,1,0:T(8,128)(2,1)S(1)} %copy-done.18, bf16[1,4,256,512]{3,2,1,0:T(8,128)(2,1)S(1)} %copy-done.14, ...), custom_call_target="tpu_custom_call" | custom-call | flops 1000 | bytes 1000 | tf_op jit(solution)/shard_map/scale_mix/pallas_call | solution.py:239
  202.3 5.1 %collective-permute-done.33 = bf16[1,256,512]{2,1,0:T(8,128)(2,1)S(1)} collective-permute-done((bf16[1,256,512]{2,1,0:T(8,128)(2,1)S(1)}, bf16[1,256,512]{2,1,0:T(8,128)(2,1)S(1)}, u32[]{:S(2)}, u32[]{:S(2)}) %collective-permute-start.33) | collective-permute-done | bytes 262176 | tf_op jit(solution)/shard_map/ppermute | solution.py:325
  207.4 11.6 %collective-permute-done.34 = bf16[1,256,512]{2,1,0:T(8,128)(2,1)S(1)} collective-permute-done((bf16[1,256,512]{2,1,0:T(8,128)(2,1)S(1)}, bf16[1,256,512]{2,1,0:T(8,128)(2,1)S(1)}, u32[]{:S(2)}, u32[]{:S(2)}) %collective-permute-start.34) | collective-permute-done | bytes 262176 | tf_op jit(solution)/shard_map/ppermute | solution.py:325
  (163 shorter events, 54.8 us)
Async XLA Ops:
  6.5 69.6 %all-gather.5.cloned.1.call-start = ((), (), s32[]{:S(2)}) async-start(), calls=%async_computation.2 | async-start | bytes 1310720 | tf_op jit(solution)/shard_map/all_gather | solution.py:357
  10.5 91.8 %all-gather.7.cloned.1.call-start = ((), (), s32[]{:S(2)}) async-start(), calls=%async_computation.3 | async-start | bytes 2621440 | tf_op jit(solution)/shard_map/all_gather | solution.py:357
  10.6 29.6 %collective-permute-start.7 = (bf16[2,2048,128]{2,1,0:T(8,128)(2,1)}, bf16[2,2048,128]{2,1,0:T(8,128)(2,1)}, u32[]{:S(2)}, u32[]{:S(2)}) collective-permute-start(bf16[2,2048,128]{2,1,0:T(8,128)(2,1)} %get-tuple-element.149.refs_4_), channel_id=1, source_target_pairs={{0,2},{1,3},{2,0},{3,1},{4,6},{5,7},{6,4},{7,5},{8,10},{9,11},{10,... | collective-permute-start | bytes 3145736 | tf_op jit(solution)/shard_map/ppermute | solution.py:325
  13.6 205.5 %reduce-scatter.2.cloned.1.call-start = ((), (), s32[]{:S(2)}) async-start(), calls=%async_computation.1 | async-start | bytes 2621440 | tf_op jit(solution)/shard_map/reduce_scatter | solution.py:396
  13.7 28.5 %collective-permute-start.3 = (bf16[256,512]{1,0:T(8,128)(2,1)}, bf16[256,512]{1,0:T(8,128)(2,1)S(1)}, u32[]{:S(2)}, u32[]{:S(2)}) collective-permute-start(bf16[256,512]{1,0:T(8,128)(2,1)} %get-tuple-element.145.refs_0_), channel_id=1, source_target_pairs={{0,4},{1,5},{2,6},{3,7},{4,0},{5,1},{6,2},{7,3},{8,12},{9,13},{10,... | collective-permute-start | bytes 786440 | tf_op jit(solution)/shard_map/ppermute | solution.py:325
  15.8 17.8 %collective-permute-start.1 = (s32[32]{0:T(128)S(1)}, s32[32]{0:T(128)S(1)}, u32[]{:S(2)}, u32[]{:S(2)}) collective-permute-start(s32[32]{0:T(128)S(1)} %bitcast.57), channel_id=1, source_target_pairs={{0,8},{1,9},{2,10},{3,11},{4,12},{5,13},{6,14},{7,15},{8,0},{9,1},... | collective-permute-start | bytes 392 | tf_op jit(solution)/shard_map/ppermute | solution.py:325
  18.4 25.0 %collective-permute-start.4 = (bf16[256,512]{1,0:T(8,128)(2,1)}, bf16[256,512]{1,0:T(8,128)(2,1)S(1)}, u32[]{:S(2)}, u32[]{:S(2)}) collective-permute-start(bf16[256,512]{1,0:T(8,128)(2,1)} %get-tuple-element.145.refs_0_), channel_id=1, source_target_pairs={{0,8},{1,9},{2,10},{3,11},{4,12},{5,13},{6,14},{7,15},{8,0},{9,1},... | collective-permute-start | bytes 786440 | tf_op jit(solution)/shard_map/ppermute | solution.py:325
  33.6 31.1 %collective-permute-start.6 = (bf16[2,2048,128]{2,1,0:T(8,128)(2,1)}, bf16[2,2048,128]{2,1,0:T(8,128)(2,1)}, u32[]{:S(2)}, u32[]{:S(2)}) collective-permute-start(bf16[2,2048,128]{2,1,0:T(8,128)(2,1)} %get-tuple-element.149.refs_4_), channel_id=1, source_target_pairs={{0,1},{1,0},{2,3},{3,2},{4,5},{5,4},{6,7},{7,6},{8,9},{9,8},{10,11... | collective-permute-start | bytes 3145736 | tf_op jit(solution)/shard_map/ppermute | solution.py:325
  35.1 18.4 %collective-permute-start.10 = (bf16[256,1024]{1,0:T(8,128)(2,1)}, bf16[256,1024]{1,0:T(8,128)(2,1)S(1)}, u32[]{:S(2)}, u32[]{:S(2)}) collective-permute-start(bf16[256,1024]{1,0:T(8,128)(2,1)} %get-tuple-element.208.refs_4_.refs_8_.refs_1_.refs_5_), channel_id=1, source_target_pairs={{0,2},{1,3},{2,0},{3,1},{4,6},{5,7},{6,4},{7,5},{8,10},{9,11},{10,... | collective-permute-start | bytes 1572872 | tf_op jit(solution)/shard_map/ppermute | solution.py:325
  40.2 34.6 %collective-permute-start.13 = (bf16[2,2048,128]{2,1,0:T(8,128)(2,1)}, bf16[2,2048,128]{2,1,0:T(8,128)(2,1)}, u32[]{:S(2)}, u32[]{:S(2)}) collective-permute-start(bf16[2,2048,128]{2,1,0:T(8,128)(2,1)} %get-tuple-element.167.refs_1_), channel_id=1, source_target_pairs={{0,2},{1,3},{2,0},{3,1},{4,6},{5,7},{6,4},{7,5},{8,10},{9,11},{10,... | collective-permute-start | bytes 3145736 | tf_op jit(solution)/shard_map/ppermute | solution.py:325
  42.1 22.6 %collective-permute-start.8 = (bf16[2,2048,128]{2,1,0:T(8,128)(2,1)}, bf16[2,2048,128]{2,1,0:T(8,128)(2,1)}, u32[]{:S(2)}, u32[]{:S(2)}) collective-permute-start(bf16[2,2048,128]{2,1,0:T(8,128)(2,1)} %collective-permute-done.7.refs_6_), channel_id=1, source_target_pairs={{0,1},{1,0},{2,3},{3,2},{4,5},{5,4},{6,7},{7,6},{8,9},{9,8},{10,11... | collective-permute-start | bytes 3145736 | tf_op jit(solution)/shard_map/ppermute | solution.py:325
  55.4 30.4 %collective-permute-start.12 = (bf16[2,2048,128]{2,1,0:T(8,128)(2,1)}, bf16[2,2048,128]{2,1,0:T(8,128)(2,1)}, u32[]{:S(2)}, u32[]{:S(2)}) collective-permute-start(bf16[2,2048,128]{2,1,0:T(8,128)(2,1)} %get-tuple-element.167.refs_1_), channel_id=1, source_target_pairs={{0,1},{1,0},{2,3},{3,2},{4,5},{5,4},{6,7},{7,6},{8,9},{9,8},{10,11... | collective-permute-start | bytes 3145736 | tf_op jit(solution)/shard_map/ppermute | solution.py:325
  74.9 27.4 %collective-permute-start.18 = (bf16[2,2048,128]{2,1,0:T(8,128)(2,1)}, bf16[2,2048,128]{2,1,0:T(8,128)(2,1)}, u32[]{:S(2)}, u32[]{:S(2)}) collective-permute-start(bf16[2,2048,128]{2,1,0:T(8,128)(2,1)} %get-tuple-element.196.refs_1_), channel_id=1, source_target_pairs={{0,2},{1,3},{2,0},{3,1},{4,6},{5,7},{6,4},{7,5},{8,10},{9,11},{10,... | collective-permute-start | bytes 3145736 | tf_op jit(solution)/shard_map/ppermute | solution.py:325
  95.8 16.8 %collective-permute-start.15 = (f32[2,4,8,256]{3,2,1,0:T(8,128)S(1)}, f32[2,4,8,256]{3,2,1,0:T(8,128)S(1)}, u32[]{:S(2)}, u32[]{:S(2)}) collective-permute-start(f32[2,4,8,256]{3,2,1,0:T(8,128)S(1)} %pad_maximum_fusion.1.refs_5_), channel_id=1, source_target_pairs={{0,4},{1,5},{2,6},{3,7},{4,0},{5,1},{6,2},{7,3},{8,12},{9,13},{10,... | collective-permute-start | bytes 196616 | tf_op jit(solution)/shard_map/ppermute | solution.py:325
  118.5 25.5 %collective-permute-start.24 = (bf16[2,2048,128]{2,1,0:T(8,128)(2,1)}, bf16[2,2048,128]{2,1,0:T(8,128)(2,1)}, u32[]{:S(2)}, u32[]{:S(2)}) collective-permute-start(bf16[2,2048,128]{2,1,0:T(8,128)(2,1)} %get-tuple-element.225.refs_1_), channel_id=1, source_target_pairs={{0,2},{1,3},{2,0},{3,1},{4,6},{5,7},{6,4},{7,5},{8,10},{9,11},{10,... | collective-permute-start | bytes 3145736 | tf_op jit(solution)/shard_map/ppermute | solution.py:325
  119.6 47.8 %collective-permute-start.28 = (bf16[2,2048,128]{2,1,0:T(8,128)(2,1)}, bf16[2,2048,128]{2,1,0:T(8,128)(2,1)}, u32[]{:S(2)}, u32[]{:S(2)}) collective-permute-start(bf16[2,2048,128]{2,1,0:T(8,128)(2,1)} %get-tuple-element.225.refs_1_), channel_id=1, source_target_pairs={{0,1},{1,0},{2,3},{3,2},{4,5},{5,4},{6,7},{7,6},{8,9},{9,8},{10,11... | collective-permute-start | bytes 3145736 | tf_op jit(solution)/shard_map/ppermute | solution.py:325
  143.9 23.5 %collective-permute-start.29 = (bf16[2,2048,128]{2,1,0:T(8,128)(2,1)}, bf16[2,2048,128]{2,1,0:T(8,128)(2,1)}, u32[]{:S(2)}, u32[]{:S(2)}) collective-permute-start(bf16[2,2048,128]{2,1,0:T(8,128)(2,1)} %collective-permute-done.24.refs_3_), channel_id=1, source_target_pairs={{0,1},{1,0},{2,3},{3,2},{4,5},{5,4},{6,7},{7,6},{8,9},{9,8},{10,11... | collective-permute-start | bytes 3145736 | tf_op jit(solution)/shard_map/ppermute | solution.py:325
  144.0 14.5 %collective-permute-start.21 = (f32[1,4,8,256]{3,2,1,0:T(8,128)S(1)}, f32[1,4,8,256]{3,2,1,0:T(8,128)S(1)}, u32[]{:S(2)}, u32[]{:S(2)}) collective-permute-start(f32[1,4,8,256]{3,2,1,0:T(8,128)S(1)} %bitcast.40), channel_id=1, source_target_pairs={{0,4},{1,5},{2,6},{3,7},{4,0},{5,1},{6,2},{7,3},{8,12},{9,13},{10,... | collective-permute-start | bytes 98312 | tf_op jit(solution)/shard_map/ppermute | solution.py:325
  163.0 35.7 %collective-permute-start.25 = (bf16[1,256,512]{2,1,0:T(8,128)(2,1)}, bf16[1,256,512]{2,1,0:T(8,128)(2,1)}, u32[]{:S(2)}, u32[]{:S(2)}) collective-permute-start(bf16[1,256,512]{2,1,0:T(8,128)(2,1)} %get-tuple-element.220), channel_id=1, source_target_pairs={{0,4},{1,5},{2,6},{3,7},{4,0},{5,1},{6,2},{7,3},{8,12},{9,13},{10,... | collective-permute-start | bytes 786440 | tf_op jit(solution)/shard_map/ppermute | solution.py:325
  163.0 38.0 %collective-permute-start.26 = (bf16[1,256,512]{2,1,0:T(8,128)(2,1)}, bf16[1,256,512]{2,1,0:T(8,128)(2,1)}, u32[]{:S(2)}, u32[]{:S(2)}) collective-permute-start(bf16[1,256,512]{2,1,0:T(8,128)(2,1)} %get-tuple-element.221), channel_id=1, source_target_pairs={{0,8},{1,9},{2,10},{3,11},{4,12},{5,13},{6,14},{7,15},{8,0},{9,1},... | collective-permute-start | bytes 786440 | tf_op jit(solution)/shard_map/ppermute | solution.py:325
  163.1 38.0 %collective-permute-start.27 = (bf16[1,256,512]{2,1,0:T(8,128)(2,1)}, bf16[1,256,512]{2,1,0:T(8,128)(2,1)}, u32[]{:S(2)}, u32[]{:S(2)}) collective-permute-start(bf16[1,256,512]{2,1,0:T(8,128)(2,1)} %get-tuple-element.222), channel_id=1, source_target_pairs={{0,12},{1,13},{2,14},{3,15},{4,8},{5,9},{6,10},{7,11},{8,4},{9,5},... | collective-permute-start | bytes 786440 | tf_op jit(solution)/shard_map/ppermute | solution.py:325
  177.4 14.3 %collective-permute-start.31 = (f32[1,4,8,256]{3,2,1,0:T(8,128)S(1)}, f32[1,4,8,256]{3,2,1,0:T(8,128)S(1)}, u32[]{:S(2)}, u32[]{:S(2)}) collective-permute-start(f32[1,4,8,256]{3,2,1,0:T(8,128)S(1)} %bitcast.45), channel_id=1, source_target_pairs={{0,8},{1,9},{2,10},{3,11},{4,12},{5,13},{6,14},{7,15},{8,0},{9,1},... | collective-permute-start | bytes 98312 | tf_op jit(solution)/shard_map/ppermute | solution.py:325
  197.6 21.4 %collective-permute-start.34 = (bf16[1,256,512]{2,1,0:T(8,128)(2,1)S(1)}, bf16[1,256,512]{2,1,0:T(8,128)(2,1)S(1)}, u32[]{:S(2)}, u32[]{:S(2)}) collective-permute-start(bf16[1,256,512]{2,1,0:T(8,128)(2,1)S(1)} %get-tuple-element.241), channel_id=1, source_target_pairs={{0,8},{1,9},{2,10},{3,11},{4,12},{5,13},{6,14},{7,15},{8,0},{9,1},... | collective-permute-start | bytes 786440 | tf_op jit(solution)/shard_map/ppermute | solution.py:325
  198.7 20.3 %collective-permute-start.35 = (bf16[1,256,512]{2,1,0:T(8,128)(2,1)S(1)}, bf16[1,256,512]{2,1,0:T(8,128)(2,1)S(1)}, u32[]{:S(2)}, u32[]{:S(2)}) collective-permute-start(bf16[1,256,512]{2,1,0:T(8,128)(2,1)S(1)} %get-tuple-element.242), channel_id=1, source_target_pairs={{0,12},{1,13},{2,14},{3,15},{4,8},{5,9},{6,10},{7,11},{8,4},{9,5},... | collective-permute-start | bytes 786440 | tf_op jit(solution)/shard_map/ppermute | solution.py:325
  (48 other events, 407.3 us)
Sparse Core Ops, SparseCore 0:
  10.7 44.8 all-gather.4
  57.1 43.8 all-gather.6
  118.0 45.5 reduce-scatter.1

commit v3 on v2

v3 whole, which is shorter than its diff:
```python
import functools

import jax
import jax.numpy as jnp
from jax import lax
from jax.experimental import pallas as pl
from jax.experimental.pallas import tpu as pltpu
from jax.sharding import PartitionSpec as P

H = 16
KVH = 4
HD = 128
QBLK = 256
MROWS = 128
TOPM = 32
CAP = 2
G = H // KVH
WITHIN = 4
LOG2E = 1.4426950408889634
SCALE = HD**-0.5 * LOG2E
MASKED = -1e30
QW = G * HD
CHUNKS = ((0, 1), (2, 3))
ID_ROWS = 16
GROUPS = (((0, 1), "scatter"), ((2,), "direct"), ((3,), "direct"))


def scores_of(q, k):
    return lax.dot_general(q, k, (((1,), (1,)), ((), ())), preferred_element_type=jnp.float32)


def attend_heads(q, k, v, allowed, out_ref):
    keys = k.shape[0]
    vx = jnp.concatenate([v, jnp.ones((keys, HD), jnp.bfloat16)], axis=1)
    lane = lax.broadcasted_iota(jnp.int32, (QBLK, HD), 1)
    rows = jnp.zeros((QBLK, HD), jnp.float32)
    ahead = scores_of(q[:, :HD], k)
    for g in range(G):
        s = ahead
        if g + 1 < G:
            ahead = scores_of(q[:, (g + 1) * HD : (g + 2) * HD], k)
        if allowed is not None:
            s = jnp.where(allowed, s, MASKED)
        m = jnp.max(s, axis=1, keepdims=True)
        p = jnp.exp2((s - m) * SCALE).astype(jnp.bfloat16)
        o = jnp.dot(p, vx, preferred_element_type=jnp.float32)
        total = o[:, HD:]
        out_ref[0, :, g * HD : (g + 1) * HD] = (o[:, :HD] / total).astype(jnp.bfloat16)
        rows = jnp.where(lane == g, m * SCALE + jnp.log2(total), rows)
    return rows.T[:8]


def ctx_kernel(slot_base, info, q_ref, k0, k1, k2, k3, v0, v1, v2, v3, out_ref, lse_ref):
    slot = pl.program_id(1) + slot_base
    plane, within = info[0, 0], info[0, 1]
    target = jnp.bitwise_xor(plane, slot)

    def run(allowed):
        k = jnp.concatenate([k0[...], k1[...], k2[...], k3[...]], axis=0)
        v = jnp.concatenate([v0[...], v1[...], v2[...], v3[...]], axis=0)
        lse_ref[0, 0] = attend_heads(q_ref[0] if slot_base else q_ref[...], k, v, allowed, out_ref.at[0])

    if slot_base == 0:
        keys = WITHIN * QBLK
        col = lax.broadcasted_iota(jnp.int32, (QBLK, keys), 1)
        row = lax.broadcasted_iota(jnp.int32, (QBLK, keys), 0)
        key_pos = jnp.bitwise_xor(col // QBLK, within) * QBLK + col % QBLK
        run(key_pos <= within * QBLK + row)
        return

    @pl.when(target > plane)
    def _():
        run(None)

    @pl.when(target < plane)
    def _():
        out_ref[...] = jnp.zeros_like(out_ref)
        lse_ref[...] = jnp.full_like(lse_ref, MASKED)


def mem_kernel(masked, info, q_ref, s0, s1, s2, s3, own_lse_ref, ctx_lse_ref, out_ref, lse_ref, kbuf, vbuf):
    slot = pl.program_id(1)
    stores = (s0, s1, s2, s3)
    allowed = None
    keys = WITHIN * CAP * MROWS
    if masked:
        col = lax.broadcasted_iota(jnp.int32, (QBLK, keys), 1) // MROWS
        allowed = jnp.zeros((QBLK, keys), jnp.bool_)
    for n in range(WITHIN * CAP):
        entry = info[1 + slot, n]
        start = pl.multiple_of(jnp.maximum(entry, 0) * MROWS, MROWS)
        rows, to = pl.ds(start, MROWS), slice(n * MROWS, (n + 1) * MROWS)
        kbuf[to, :] = stores[n // CAP][rows, :HD]
        vbuf[to, :] = stores[n // CAP][rows, HD:]
        if masked:
            allowed = allowed | ((col == n) & (entry >= 0))
    lse_ref[0, 0] = attend_heads(q_ref[0], kbuf[...], vbuf[...], allowed, out_ref.at[0])
    lse_ref[0, 0, G:] = jnp.where(slot == 0, own_lse_ref[0, 0, :G], ctx_lse_ref[0, 0, :G])


def scale_kernel(planes, heads, scattered, info, um_ref, own_ref, uc_ref, gate_ref, *refs):
    lse_refs, out_refs = refs[:planes], refs[planes:]
    slot = pl.program_id(0)
    for h in range(heads):
        parts = [lse_refs[k][h, jnp.bitwise_xor(slot, k)] for k in range(planes)]
        top = functools.reduce(jnp.maximum, parts)
        total = functools.reduce(jnp.add, [jnp.exp2(p - top) for p in parts])
        weight = jnp.exp2(parts[0] - top) / total * gate_ref[h]
        wt = jnp.concatenate([weight, jnp.zeros((HD - 8, QBLK), jnp.float32)], axis=0).T
        for g in range(G):
            cols = slice(g * HD, (g + 1) * HD)
            term = wt[:, g : g + 1] * um_ref[h, 0, :, cols].astype(jnp.float32)
            ctx = jnp.where(slot == 0, own_ref[h, 0, :, cols], uc_ref[h, 0, :, cols])
            term += wt[:, G + g : G + g + 1] * ctx.astype(jnp.float32)
            term = term.astype(jnp.bfloat16)
            if scattered:
                out_refs[0][0, h, :, cols] = term
                continue
            for i, ref in enumerate(out_refs):

                @pl.when(slot == i)
                def _(ref=ref):
                    ref[h, :, cols] = term


PARAMS = pltpu.CompilerParams(vmem_limit_bytes=56 * 1024 * 1024)
PACK_PARAMS = pltpu.CompilerParams(vmem_limit_bytes=60 * 1024 * 1024)
SMALL = pl.CostEstimate(flops=1000, bytes_accessed=1000, transcendentals=0)


def place_of(head, chunks):
    return next((n, heads.index(head)) for n, heads in enumerate(chunks) if head in heads)


def whole(shape):
    return pl.BlockSpec(shape, lambda *_: (0,) * len(shape))


def query_spec(first):
    column = place_of(first, CHUNKS)[1]
    return pl.BlockSpec((1, QBLK, QW), lambda h, j, info: (jnp.bitwise_xor(info[0, 0], j), 0, column + h))


def per_head(rows, cols):
    return pl.BlockSpec((1, 1, rows, cols), lambda h, j, info: (h, j, 0, 0))


def partial_shapes(count, planes):
    return [
        jax.ShapeDtypeStruct((count, planes, QBLK, QW), jnp.bfloat16),
        jax.ShapeDtypeStruct((count, planes, 8, QBLK), jnp.float32),
    ]


def ctx_call(info, q, sources, first, count, planes):
    base = min(planes - 1, 1)
    kspec = pl.BlockSpec((QBLK, HD), lambda h, j, info: (0, first + h))
    if base:
        column = place_of(first, CHUNKS)[1]
        qspec = pl.BlockSpec((1, QBLK, QW), lambda h, j, info: (jnp.bitwise_xor(info[0, 0], j + 1), 0, column + h))
    else:
        qspec = pl.BlockSpec((QBLK, QW), lambda h, j, info: (0, first + h))
    return pl.pallas_call(
        functools.partial(ctx_kernel, base),
        grid_spec=pltpu.PrefetchScalarGridSpec(
            num_scalar_prefetch=1,
            grid=(count, planes - base),
            in_specs=[qspec] + [kspec] * (2 * WITHIN),
            out_specs=[per_head(QBLK, QW), per_head(8, QBLK)],
        ),
        out_shape=partial_shapes(count, planes - base),
        compiler_params=PARAMS,
        cost_estimate=SMALL,
        name="ctx_attend",
    )(info, q, *sources)


def mem_call(info, q, stores, own_lse, ctx_lse, first, count, chunk_first, planes, masked):
    keys = WITHIN * CAP * MROWS
    column = place_of(first, CHUNKS)[1]
    sspec = pl.BlockSpec((stores[0].shape[0], 2 * HD), lambda h, j, info: (0, column + h))
    return pl.pallas_call(
        functools.partial(mem_kernel, masked),
        grid_spec=pltpu.PrefetchScalarGridSpec(
            num_scalar_prefetch=1,
            grid=(count, planes),
            in_specs=[query_spec(first)]
            + [sspec] * WITHIN
            + [
                pl.BlockSpec((1, 1, 8, QBLK), lambda h, j, info: (first + h, 0, 0, 0)),
                pl.BlockSpec((1, 1, 8, QBLK), lambda h, j, info: (first - chunk_first + h, jnp.maximum(j - 1, 0), 0, 0)),
            ],
            out_specs=[per_head(QBLK, QW), per_head(8, QBLK)],
            scratch_shapes=[pltpu.VMEM((keys, HD), jnp.bfloat16), pltpu.VMEM((keys, HD), jnp.bfloat16)],
        ),
        out_shape=partial_shapes(count, planes),
        compiler_params=PARAMS,
        cost_estimate=SMALL,
        name="mem_attend",
    )(info, q, *stores, own_lse, ctx_lse)


def scale_call(info, um, own, uc, gate_rows, lses, first, chunk_first, scattered):
    heads, planes = um.shape[:2]
    part = pl.BlockSpec((heads, 1, QBLK, QW), lambda j, info: (0, j, 0, 0))
    own_part = pl.BlockSpec((heads, 1, QBLK, QW), lambda j, info: (first // heads, 0, 0, 0))
    nth = (first - chunk_first) // heads
    rest = pl.BlockSpec((heads, 1, QBLK, QW), lambda j, info: (nth, jnp.maximum(j - 1, 0), 0, 0))
    if scattered:
        out_specs = [pl.BlockSpec((1, heads, QBLK, QW), lambda j, info: (jnp.bitwise_xor(info[0, 0], j), 0, 0, 0))]
        shapes = [(planes, heads, QBLK, QW)]
    else:
        shapes = [(heads, QBLK, QW)] * planes
        out_specs = [whole(shape) for shape in shapes]
    return pl.pallas_call(
        functools.partial(scale_kernel, planes, heads, scattered),
        grid_spec=pltpu.PrefetchScalarGridSpec(
            num_scalar_prefetch=1,
            grid=(planes,),
            in_specs=[part, own_part, rest, whole((heads, 8, 1))] + [whole((heads, planes, 8, QBLK))] * planes,
            out_specs=out_specs,
        ),
        out_shape=[jax.ShapeDtypeStruct(shape, jnp.bfloat16) for shape in shapes],
        compiler_params=PARAMS,
        cost_estimate=SMALL,
        name="scale_mix",
    )(info, um, own, uc, gate_rows, *lses)


def route_kernel(planes, local_count, ids_ref, slot_ref, place_ref, out_ref):
    entries = slot_ref.shape[0]
    plane, within = place_ref[0], place_ref[1]
    before = lax.broadcasted_iota(jnp.int32, (TOPM, TOPM), 0) <= lax.broadcasted_iota(jnp.int32, (TOPM, TOPM), 1)
    before = before.astype(jnp.float32)
    source = lax.broadcasted_iota(jnp.int32, (8, TOPM), 0)
    holder = plane * WITHIN + jnp.bitwise_xor(within, source)
    lane = lax.broadcasted_iota(jnp.int32, (1, HD), 1)
    for k in range(planes):
        halves = ids_ref[jnp.bitwise_xor(plane, k), :8, : 2 * TOPM].astype(jnp.float32)[:1].astype(jnp.int32)
        ids = halves[:, :TOPM] * 256 + halves[:, TOPM:]
        hits = lax.broadcasted_iota(jnp.int32, (entries, TOPM), 0) == ids
        slots = jnp.sum(jnp.where(hits, slot_ref[...], 0), axis=0, keepdims=True)
        held = (slots // local_count == holder) & (source < WITHIN)
        rank = jnp.dot(held.astype(jnp.float32), before, preferred_element_type=jnp.float32)
        local = slots % local_count + 1
        row = jnp.zeros((1, HD), jnp.int32)
        for r in range(CAP):
            found = jnp.sum(jnp.where(held & (rank == r + 1), local, 0), axis=1, keepdims=True) - 1
            for s in range(WITHIN):
                row = jnp.where(lane == s * CAP + r, found[s : s + 1], row)
        out_ref[k : k + 1, :] = row[:, :8]


def route_call(place, gathered, block_slot, local_count):
    planes = gathered.shape[0]
    return pl.pallas_call(
        functools.partial(route_kernel, planes, local_count),
        grid=(1,),
        in_specs=[
            pl.BlockSpec((planes, ID_ROWS, HD), lambda i: (0, QBLK // ID_ROWS, 0)),
            whole((block_slot.shape[0], 1)),
            pl.BlockSpec(memory_space=pltpu.SMEM),
        ],
        out_specs=whole((planes, 8)),
        out_shape=jax.ShapeDtypeStruct((planes, 8), jnp.int32),
        compiler_params=PARAMS,
        cost_estimate=SMALL,
        name="route_blocks",
    )(gathered, block_slot[:, None], place)


def pack_kernel(stores, chunks, first, q, k, v, ids, *outs):
    for n, heads in enumerate(stores):
        for i, head in enumerate(heads):
            cols = slice(head * HD, (head + 1) * HD)
            outs[n][:, 2 * i * HD : (2 * i + 1) * HD] = k[:, cols]
            outs[n][:, (2 * i + 1) * HD : (2 * i + 2) * HD] = v[:, cols]

    @pl.when(pl.program_id(0) == 0)
    def _():
        for n, heads in enumerate(chunks):
            out = outs[len(stores) + n]
            out[:QBLK, :] = q[:, heads[0] * QW : (heads[-1] + 1) * QW]
            if first and n == 0:
                halves = jnp.concatenate([ids[...] // 256, ids[...] % 256], axis=1).astype(jnp.float32)
                halves = jnp.concatenate([halves, jnp.zeros((1, out.shape[1] - 2 * TOPM), jnp.float32)], axis=1)
                out[QBLK:, :] = jnp.broadcast_to(halves, (ID_ROWS, out.shape[1])).astype(jnp.bfloat16)


def pack_call(stores, chunks, first, q, k, v, ids):
    rows, steps = k.shape[0], 4
    part = rows // steps
    shapes = [(rows, 2 * len(heads) * HD) for heads in stores]
    specs = [pl.BlockSpec((part, shape[1]), lambda i: (i, 0)) for shape in shapes]
    shapes += [(QBLK + ID_ROWS * (first and n == 0), len(heads) * QW) for n, heads in enumerate(chunks)]
    specs += [whole(shape) for shape in shapes[len(stores) :]]
    width = (stores[-1][-1] + 1) * HD
    q_width = (chunks[-1][-1] + 1) * QW if chunks else QW
    return pl.pallas_call(
        functools.partial(pack_kernel, stores, chunks, first),
        grid=(steps,),
        in_specs=[whole((QBLK, q_width))]
        + [pl.BlockSpec((part, width), lambda i: (i, 0))] * 2
        + [whole(ids.shape)],
        out_specs=specs,
        out_shape=[jax.ShapeDtypeStruct(shape, jnp.bfloat16) for shape in shapes],
        compiler_params=PACK_PARAMS,
        cost_estimate=SMALL,
        name="pack_heads",
    )(q, k, v, ids)


class Order:
    def __init__(self):
        self.last = ()

    def before(self, *arrays):
        if not self.last:
            return arrays
        return lax.optimization_barrier((*arrays, *self.last))[: len(arrays)]

    def done(self, *arrays):
        self.last = arrays


def on_device(
    queries, ctx_keys, ctx_values, store_keys, store_values, block_ids, block_slot, gate_logit
):
    devices = lax.axis_size("seq")
    planes = devices // WITHIN
    me = lax.axis_index("seq")
    plane, within = me // WITHIN, me % WITHIN
    local_count = store_keys.shape[0]
    masked = devices * CAP != TOPM

    def xor(x, bits):
        return lax.ppermute(x, "seq", [(i, i ^ bits) for i in range(devices)])

    def all_planes(x):
        return [x] + [xor(x, k * WITHIN) for k in range(1, planes)]

    columns = [[p * WITHIN + w for p in range(planes)] for w in range(WITHIN)]
    keys = store_keys.reshape(local_count * MROWS, KVH * HD)
    values = store_values.reshape(local_count * MROWS, KVH * HD)
    order = Order()

    raw = (queries, keys, values, block_ids)
    ctx_far = [xor(ctx_keys, 2), xor(ctx_values, 2)]
    ctx_near = [xor(ctx_keys, 1), xor(ctx_values, 1)]
    own_first, q_first = pack_call(CHUNKS[:1], CHUNKS[:1], True, *raw)
    order.done(q_first)
    own_second, q_second = pack_call(CHUNKS[1:], CHUNKS[1:], False, *order.before(*raw))
    order.done(q_second, *ctx_far)
    own = [own_first, own_second]
    far = [xor(part, 2) for part in order.before(*own)]
    ctx_diag = [xor(part, 1) for part in ctx_far]
    near = [xor(part, 1) for part in own]
    diag = [None, None]

    gate = 1.0 / (1.0 + jnp.exp(-gate_logit))
    gate_rows = jnp.concatenate([gate.reshape(KVH, G), 1.0 - gate.reshape(KVH, G)], axis=1)[:, :, None]
    spread = [lax.all_gather(part, "seq", axis=0, axis_index_groups=columns) for part in (q_first, q_second)]

    place = jnp.stack([plane, within] + [plane] * 6).astype(jnp.int32)
    route = route_call(place, spread[0], block_slot, local_count)
    place = place[None]
    info = jnp.concatenate([place, route])
    sources = [x for kind in zip((ctx_keys, ctx_values), ctx_near, ctx_far, ctx_diag, strict=True) for x in kind]

    def fetch_step(n):
        (far[n],) = order.before(far[n])
        order.done(far[n])
        diag[n] = xor(far[n], 1)

    def ctx_step(q, first, count, slots):
        args = order.before(place, q, *sources)
        uc, lse = ctx_call(args[0], args[1], args[2:], first, count, slots)
        order.done(lse)
        return uc, lse

    def mem_step(first, count, ctx_lse):
        n = place_of(first, CHUNKS)[0]
        args = order.before(info, spread[n], own[n], near[n], far[n], diag[n], own_lse, ctx_lse)
        um, lse = mem_call(*args[:2], args[2:6], *args[6:], first, count, CHUNKS[n][0], planes, masked)
        order.done(lse)
        return um, all_planes(lse)

    def scale_step(first, um, uc, lses, scattered):
        n = place_of(first, CHUNKS)[0]
        um, uc, *lses = order.before(um, uc, *lses)
        gates = gate_rows[first : first + um.shape[0]]
        parts = scale_call(place, um, own_uc, uc, gates, lses, first, CHUNKS[n][0], scattered)
        order.done(parts[0])
        if scattered:
            return [lax.psum_scatter(parts[0], "seq", scatter_dimension=0, axis_index_groups=columns)]
        return [parts[0]] + [xor(parts[k], k * WITHIN) for k in range(1, planes)]

    def total(parts):
        return sum(part.astype(jnp.float32) for part in parts).astype(jnp.bfloat16)

    own_uc, own_lse = ctx_step(queries, 0, KVH, 1)
    uc01, ctx_lse01 = ctx_step(spread[0], 0, 2, planes)
    fetch_step(0)
    um01, lses01 = mem_step(0, 2, ctx_lse01)
    coming = [scale_step(0, um01, uc01, lses01, True)]
    uc23, ctx_lse23 = ctx_step(spread[1], 2, 2, planes)
    fetch_step(1)
    um2, lses2 = mem_step(2, 1, ctx_lse23)
    um3, lses3 = mem_step(3, 1, ctx_lse23)
    coming.append(scale_step(2, um2, uc23, lses2, True))
    coming.append(scale_step(3, um3, uc23, lses3, False))
    return jnp.concatenate([part for parts in coming for part in total(parts)], axis=1)


def solution(mesh):
    placed = (
        P(("groups", "seq"), None),
        P(("groups", "seq"), None),
        P(("groups", "seq"), None),
        P(("groups", "seq"), None, None),
        P(("groups", "seq"), None, None),
        P(("groups", "seq"), None),
        P("groups"),
        P(),
    )
    return jax.shard_map(
        on_device, mesh=mesh, in_specs=placed, out_specs=P(("groups", "seq"), None), check_vma=False
    )
```

time: 230 us -> 224 us (0.974)
  starting transfers between devices: 47.7 us -> 25.8 us
  Pallas kernels: 86.8 us -> 102 us
  local copies, waits for them, and re-layouts: 16.2 us -> 8.63 us
  waiting for transfers between devices: 59.7 us -> 66.5 us
    ppermute x36 -> x24, starting transfers between devices: 47.6 us -> 25.5 us  [xor(): return lax.ppermute(x, 'seq', [(i, i ^ bits) for i in range(devices)])]
    all_gather x2, waiting for transfers between devices: 0.01 us -> 21.5 us  [on_device(): lax.all_gather(part, 'seq', axis=0, axis_index_groups=columns)]
    pallas_call x13 -> x12, Pallas kernels: 86.8 us -> 102 us  [the longest x3 38.3 us: mem_call(): pl.pallas_call(functools.partial(mem_kernel, masked), grid_spec=pltpu.Pre...]
    ppermute x36 -> x24, waiting for transfers between devices: 59.6 us -> 44.9 us  [xor(): return lax.ppermute(x, 'seq', [(i, i ^ bits) for i in range(devices)])]
    unnamed x66 -> x46, local copies, waits for them, and re-layouts: 14.5 us -> 4.02 us
  transfers between devices with their start and end apart: 39 -> 28, of which waited for: 13 -> 12; matrix products, arithmetic and copies ran while one was open for 2% -> 3% of each run, Pallas kernels for 35% -> 44%
where the time goes in v3:
time: 224 us; the launch traced here: 221 us
  Pallas kernels  102 us (46%)
  waiting for transfers between devices  66.5 us (30%)
  starting transfers between devices  25.8 us (12%)
  between operations  13.3 us (6%)
  local copies, waits for them, and re-layouts  8.63 us (4%)
  other arithmetic  4.5 us (2%)
    ppermute x24, waiting for transfers between devices, xor(): return lax.ppermute(x, 'seq', [(i, i ^ bits) for i in range(devices)])  44.9 us
    pallas_call x3, Pallas kernels, mem_call(): pl.pallas_call(functools.partial(mem_kernel, masked), grid_spec=pltpu.Pre...  38.3 us
    pallas_call x3, Pallas kernels, ctx_call(): pl.pallas_call(functools.partial(ctx_kernel, base), grid_spec=pltpu.Prefe...  34.1 us
    ppermute x24, starting transfers between devices, xor(): return lax.ppermute(x, 'seq', [(i, i ^ bits) for i in range(devices)])  25.5 us
    all_gather x2, waiting for transfers between devices, on_device(): lax.all_gather(part, 'seq', axis=0, axis_index_groups=columns)  21.5 us
    pallas_call x3, Pallas kernels, scale_call(): pl.pallas_call(functools.partial(scale_kernel, planes, heads, scattered),...  18.6 us
    pallas_call x2, Pallas kernels, pack_call(): pl.pallas_call(functools.partial(pack_kernel, stores, chunks, first), gri...  9.27 us
  transfers between devices with their start and end apart: 28, of which 12 were waited for; matrix products, arithmetic and copies ran while one was open for 3% of the time, Pallas kernels for 44%

profile of v3, /device:TPU:0, one launch (start us, length us, event | category | flops | bytes accessed | tf_op | source)
XLA Modules:
  0.0 221.0 jit_solution(3537052867302444147)
XLA Ops:
  6.5 4.4 %pack_heads.2 = (bf16[2048,512]{1,0:T(8,128)(2,1)}, bf16[272,1024]{1,0:T(8,128)(2,1)}) custom-call(bf16[256,2048]{1,0:T(8,128)(2,1)} %q_ref, bf16[2048,512]{1,0:T(8,128)(2,1)} %bitcast.27, bf16[2048,512]{1,0:T(8,128)(2,1)} %bitcast.29, s32[1,32]{1,0:T(1,128)} %ids.2), custom_call_target="tpu_custom_call" | custom-call | flops 1000 | bytes 1000 | tf_op jit(solution)/shard_map/pack_heads/pallas_call | solution.py:299
  11.0 3.0 %collective-permute-start.1 = (bf16[256,512]{1,0:T(8,128)(2,1)S(1)}, bf16[256,512]{1,0:T(8,128)(2,1)S(1)}, u32[]{:S(2)}, u32[]{:S(2)}) collective-permute-start(bf16[256,512]{1,0:T(8,128)(2,1)S(1)} %copy-done.2), channel_id=1, source_target_pairs={{0,2},{1,3},{2,0},{3,1},{4,6},{5,7},{6,4},{7,5},{8,10},{9,11},{10,... | collective-permute-start | bytes 786440 | tf_op jit(solution)/shard_map/ppermute | solution.py:337
  14.2 4.9 %pack_heads.3 = (bf16[2048,512]{1,0:T(8,128)(2,1)}, bf16[256,1024]{1,0:T(8,128)(2,1)}) custom-call(bf16[256,2048]{1,0:T(8,128)(2,1)} %q_ref, bf16[2048,512]{1,0:T(8,128)(2,1)} %bitcast.28, bf16[2048,512]{1,0:T(8,128)(2,1)} %bitcast.30, s32[1,32]{1,0:T(1,128)} %ids.2), custom_call_target="tpu_custom_call" | custom-call | flops 1000 | bytes 1000 | tf_op jit(solution)/shard_map/pack_heads/pallas_call | solution.py:299
  19.0 2.2 collective-permute-done.1.k2
  21.2 4.8 %collective-permute-done.2.v2 = bf16[256,512]{1,0:T(8,128)(2,1)S(1)} collective-permute-done((bf16[256,512]{1,0:T(8,128)(2,1)S(1)}, bf16[256,512]{1,0:T(8,128)(2,1)S(1)}, u32[]{:S(2)}, u32[]{:S(2)}) %collective-permute-start.2) | collective-permute-done | bytes 262176 | tf_op jit(solution)/shard_map/ppermute | solution.py:337
  31.2 9.4 %ctx_attend.3 = (bf16[4,1,256,512]{3,2,1,0:T(8,128)(2,1)}, f32[4,1,8,256]{3,2,1,0:T(8,128)}) custom-call(s32[1,8]{1,0:T(1,128)} %bitcast.32, bf16[256,2048]{1,0:T(8,128)(2,1)} %q_ref, bf16[256,512]{1,0:T(8,128)(2,1)} %k0.2, bf16[256,512]{1,0:T(8,128)(2,1)} %copy-done.6, bf16[256,512]{1,0:T(8,128)(2,1)} %copy-done.4, bf16[256,512]{1,0:T(8,128)(2,1)} %copy-done.8, ...), custom_call_target="tpu_custom_call" | custom-call | flops 1000 | bytes 1000 | tf_op jit(solution)/shard_map/ctx_attend/pallas_call | solution.py:163
  40.7 21.5 %all-gather.5.cloned.1.call-done = bf16[1088,1024]{1,0:T(8,128)(2,1)} async-done(((bf16[272,1024]{1,0:T(8,128)(2,1)}), bf16[1088,1024]{1,0:T(8,128)(2,1)}) %all-gather.5.cloned.1.call-update) | async-done | bytes 2228240 | tf_op jit(solution)/shard_map/all_gather | solution.py:362
  62.2 12.4 %ctx_attend.4 = (bf16[2,3,256,512]{3,2,1,0:T(8,128)(2,1)}, f32[2,3,8,256]{3,2,1,0:T(8,128)}) custom-call(s32[1,8]{1,0:T(1,128)} %bitcast.33, bf16[4,272,1024]{2,1,0:T(8,128)(2,1)} %bitcast.21, bf16[256,512]{1,0:T(8,128)(2,1)} %k0.2, bf16[256,512]{1,0:T(8,128)(2,1)} %copy-done.6, bf16[256,512]{1,0:T(8,128)(2,1)} %copy-done.4, bf16[256,512]{1,0:T(8,128)(2,1)} %copy-done.8, ...), custom_call_target="tpu_custom_call" | custom-call | flops 1000 | bytes 1000 | tf_op jit(solution)/shard_map/ctx_attend/pallas_call | solution.py:163
  80.4 17.7 %mem_attend.3 = (bf16[2,4,256,512]{3,2,1,0:T(8,128)(2,1)}, f32[2,4,8,256]{3,2,1,0:T(8,128)}) custom-call(s32[5,8]{1,0:T(8,128)} %pad_add_fusion.info, bf16[4,272,1024]{2,1,0:T(8,128)(2,1)} %bitcast.23, bf16[2048,512]{1,0:T(8,128)(2,1)} %get-tuple-element.139.s0, bf16[2048,512]{1,0:T(8,128)(2,1)} %collective-permute-done.s1, ...), custom_call_target="tpu_custom_call" | custom-call | flops 1000 | bytes 1000 | tf_op jit(solution)/shard_map/mem_attend/pallas_call | solution.py:182
  102.2 7.0 %collective-permute-done.10.refs_2_ = f32[2,4,8,256]{3,2,1,0:T(8,128)S(1)} collective-permute-done((f32[2,4,8,256]{3,2,1,0:T(8,128)}, f32[2,4,8,256]{3,2,1,0:T(8,128)S(1)}, u32[]{:S(2)}, u32[]{:S(2)}) %collective-permute-start.10) | collective-permute-done | bytes 65568 | tf_op jit(solution)/shard_map/ppermute | solution.py:337
  109.9 6.9 %scale_mix.3 = bf16[4,2,256,512]{3,2,1,0:T(8,128)(2,1)} custom-call(s32[1,8]{1,0:T(1,128)} %bitcast.34, bf16[2,4,256,512]{3,2,1,0:T(8,128)(2,1)} %get-tuple-element.148.um_ref, bf16[4,1,256,512]{3,2,1,0:T(8,128)(2,1)} %get-tuple-element.149.own_ref, bf16[2,3,256,512]{3,2,1,0:T(8,128)(2,1)} %get-tuple-element.150.uc_ref, f32[2,8,1]{2,1,0:T(8,128)} %copy.13.gate_ref, ...), custom_call_target="tpu_custom_call" | custom-call | flops 1000 | bytes 1000 | tf_op jit(solution)/shard_map/scale_mix/pallas_call | solution.py:215
  117.2 12.3 %ctx_attend.5 = (bf16[2,3,256,512]{3,2,1,0:T(8,128)(2,1)}, f32[2,3,8,256]{3,2,1,0:T(8,128)}) custom-call(s32[1,8]{1,0:T(1,128)} %bitcast.35, bf16[4,256,1024]{2,1,0:T(8,128)(2,1)} %bitcast.24, bf16[256,512]{1,0:T(8,128)(2,1)} %k0.2, bf16[256,512]{1,0:T(8,128)(2,1)} %copy-done.6, bf16[256,512]{1,0:T(8,128)(2,1)} %copy-done.4, bf16[256,512]{1,0:T(8,128)(2,1)} %copy-done.8, ...), custom_call_target="tpu_custom_call" | custom-call | flops 1000 | bytes 1000 | tf_op jit(solution)/shard_map/ctx_attend/pallas_call | solution.py:163
  130.0 4.0 %collective-permute-done.14.s3 = bf16[2048,512]{1,0:T(8,128)(2,1)S(1)} collective-permute-done((bf16[2048,512]{1,0:T(8,128)(2,1)}, bf16[2048,512]{1,0:T(8,128)(2,1)S(1)}, u32[]{:S(2)}, u32[]{:S(2)}) %collective-permute-start.14) | collective-permute-done | bytes 2097184 | tf_op jit(solution)/shard_map/ppermute | solution.py:337
  135.4 10.4 %mem_attend.4 = (bf16[1,4,256,512]{3,2,1,0:T(8,128)(2,1)}, f32[1,4,8,256]{3,2,1,0:T(8,128)}) custom-call(s32[5,8]{1,0:T(8,128)} %pad_add_fusion.info, bf16[4,256,1024]{2,1,0:T(8,128)(2,1)} %bitcast.25, bf16[2048,512]{1,0:T(8,128)(2,1)} %get-tuple-element.181.s0, bf16[2048,512]{1,0:T(8,128)(2,1)} %collective-permute-done.12.s1, ...), custom_call_target="tpu_custom_call" | custom-call | flops 1000 | bytes 1000 | tf_op jit(solution)/shard_map/mem_attend/pallas_call | solution.py:182
  145.8 2.6 %collective-permute-start.15 = (f32[1,4,8,256]{3,2,1,0:T(8,128)}, f32[1,4,8,256]{3,2,1,0:T(8,128)S(1)}, u32[]{:S(2)}, u32[]{:S(2)}) collective-permute-start(f32[1,4,8,256]{3,2,1,0:T(8,128)} %get-tuple-element.190.refs_0_), channel_id=1, source_target_pairs={{0,4},{1,5},{2,6},{3,7},{4,0},{5,1},{6,2},{7,3},{8,12},{9,13},{10,... | collective-permute-start | bytes 98312 | tf_op jit(solution)/shard_map/ppermute | solution.py:337
  148.3 2.4 %collective-permute-start.17 = (f32[1,4,8,256]{3,2,1,0:T(8,128)}, f32[1,4,8,256]{3,2,1,0:T(8,128)S(1)}, u32[]{:S(2)}, u32[]{:S(2)}) collective-permute-start(f32[1,4,8,256]{3,2,1,0:T(8,128)} %get-tuple-element.190.refs_0_), channel_id=1, source_target_pairs={{0,12},{1,13},{2,14},{3,15},{4,8},{5,9},{6,10},{7,11},{8,4},{9,5},... | collective-permute-start | bytes 98312 | tf_op jit(solution)/shard_map/ppermute | solution.py:337
  151.4 10.3 %mem_attend.5 = (bf16[1,4,256,512]{3,2,1,0:T(8,128)(2,1)}, f32[1,4,8,256]{3,2,1,0:T(8,128)}) custom-call(s32[5,8]{1,0:T(8,128)} %pad_add_fusion.info, bf16[4,256,1024]{2,1,0:T(8,128)(2,1)} %bitcast.26, bf16[2048,512]{1,0:T(8,128)(2,1)} %get-tuple-element.181.s0, bf16[2048,512]{1,0:T(8,128)(2,1)} %collective-permute-done.12.s1, ...), custom_call_target="tpu_custom_call" | custom-call | flops 1000 | bytes 1000 | tf_op jit(solution)/shard_map/mem_attend/pallas_call | solution.py:182
  162.4 5.5 %scale_mix.4 = bf16[4,1,256,512]{3,2,1,0:T(8,128)(2,1)} custom-call(s32[1,8]{1,0:T(1,128)} %bitcast.36, bf16[1,4,256,512]{3,2,1,0:T(8,128)(2,1)} %get-tuple-element.188.um_ref, bf16[4,1,256,512]{3,2,1,0:T(8,128)(2,1)} %get-tuple-element.149.own_ref, bf16[2,3,256,512]{3,2,1,0:T(8,128)(2,1)} %get-tuple-element.196.uc_ref, f32[1,8,1]{2,1,0:T(8,128)} %copy.14.gate_ref, ...), custom_call_target="tpu_custom_call" | custom-call | flops 1000 | bytes 1000 | tf_op jit(solution)/shard_map/scale_mix/pallas_call | solution.py:215
  169.9 2.4 %collective-permute-start.20 = (f32[1,4,8,256]{3,2,1,0:T(8,128)S(1)}, f32[1,4,8,256]{3,2,1,0:T(8,128)S(1)}, u32[]{:S(2)}, u32[]{:S(2)}) collective-permute-start(f32[1,4,8,256]{3,2,1,0:T(8,128)S(1)} %copy-done.14), channel_id=1, source_target_pairs={{0,12},{1,13},{2,14},{3,15},{4,8},{5,9},{6,10},{7,11},{8,4},{9,5},... | collective-permute-start | bytes 98312 | tf_op jit(solution)/shard_map/ppermute | solution.py:337
  176.3 6.2 %scale_mix.5 = (bf16[1,256,512]{2,1,0:T(8,128)(2,1)}, bf16[1,256,512]{2,1,0:T(8,128)(2,1)}, bf16[1,256,512]{2,1,0:T(8,128)(2,1)}, bf16[1,256,512]{2,1,0:T(8,128)(2,1)}) custom-call(s32[1,8]{1,0:T(1,128)} %bitcast.37, bf16[1,4,256,512]{3,2,1,0:T(8,128)(2,1)} %get-tuple-element.195.um_ref, bf16[4,1,256,512]{3,2,1,0:T(8,128)(2,1)} %get-tuple-element.149.own_ref, ...), custom_call_target="tpu_custom_call" | custom-call | flops 1000 | bytes 1000 | tf_op jit(solution)/shard_map/scale_mix/pallas_call | solution.py:215
  182.5 3.4 %collective-permute-start.22 = (bf16[1,256,512]{2,1,0:T(8,128)(2,1)}, bf16[1,256,512]{2,1,0:T(8,128)(2,1)S(1)}, u32[]{:S(2)}, u32[]{:S(2)}) collective-permute-start(bf16[1,256,512]{2,1,0:T(8,128)(2,1)} %get-tuple-element.203), channel_id=1, source_target_pairs={{0,8},{1,9},{2,10},{3,11},{4,12},{5,13},{6,14},{7,15},{8,0},{9,1},... | collective-permute-start | bytes 786440 | tf_op jit(solution)/shard_map/ppermute | solution.py:337
  186.9 16.1 %collective-permute-done.21 = bf16[1,256,512]{2,1,0:T(8,128)(2,1)S(1)} collective-permute-done((bf16[1,256,512]{2,1,0:T(8,128)(2,1)}, bf16[1,256,512]{2,1,0:T(8,128)(2,1)S(1)}, u32[]{:S(2)}, u32[]{:S(2)}) %collective-permute-start.21) | collective-permute-done | bytes 262176 | tf_op jit(solution)/shard_map/ppermute | solution.py:337
  203.0 7.2 %collective-permute-done.23 = bf16[1,256,512]{2,1,0:T(8,128)(2,1)S(1)} collective-permute-done((bf16[1,256,512]{2,1,0:T(8,128)(2,1)}, bf16[1,256,512]{2,1,0:T(8,128)(2,1)S(1)}, u32[]{:S(2)}, u32[]{:S(2)}) %collective-permute-start.23) | collective-permute-done | bytes 262176 | tf_op jit(solution)/shard_map/ppermute | solution.py:337
  212.4 2.1 pad_maximum_fusion
  (109 shorter events, 28.7 us)
Async XLA Ops:
  6.5 55.6 %all-gather.5.cloned.1.call-start = ((), (), s32[]{:S(2)}) async-start(), calls=%async_computation.4 | async-start | bytes 2785280 | tf_op jit(solution)/shard_map/all_gather | solution.py:362
  11.0 106.2 %all-gather.7.cloned.1.call-start = ((), (), s32[]{:S(2)}) async-start(), calls=%async_computation.5 | async-start | bytes 2621440 | tf_op jit(solution)/shard_map/all_gather | solution.py:362
  11.0 10.2 %collective-permute-start.1 = (bf16[256,512]{1,0:T(8,128)(2,1)S(1)}, bf16[256,512]{1,0:T(8,128)(2,1)S(1)}, u32[]{:S(2)}, u32[]{:S(2)}) collective-permute-start(bf16[256,512]{1,0:T(8,128)(2,1)S(1)} %copy-done.2), channel_id=1, source_target_pairs={{0,2},{1,3},{2,0},{3,1},{4,6},{5,7},{6,4},{7,5},{8,10},{9,11},{10,... | collective-permute-start | bytes 786440 | tf_op jit(solution)/shard_map/ppermute | solution.py:337
  14.1 11.9 %collective-permute-start.2 = (bf16[256,512]{1,0:T(8,128)(2,1)S(1)}, bf16[256,512]{1,0:T(8,128)(2,1)S(1)}, u32[]{:S(2)}, u32[]{:S(2)}) collective-permute-start(bf16[256,512]{1,0:T(8,128)(2,1)S(1)} %copy-done.3), channel_id=1, source_target_pairs={{0,2},{1,3},{2,0},{3,1},{4,6},{5,7},{6,4},{7,5},{8,10},{9,11},{10,... | collective-permute-start | bytes 786440 | tf_op jit(solution)/shard_map/ppermute | solution.py:337
  26.0 48.6 %collective-permute-start.3 = (bf16[2048,512]{1,0:T(8,128)(2,1)}, bf16[2048,512]{1,0:T(8,128)(2,1)}, u32[]{:S(2)}, u32[]{:S(2)}) collective-permute-start(bf16[2048,512]{1,0:T(8,128)(2,1)} %get-tuple-element.139.s0), channel_id=1, source_target_pairs={{0,2},{1,3},{2,0},{3,1},{4,6},{5,7},{6,4},{7,5},{8,10},{9,11},{10,... | collective-permute-start | bytes 6291464 | tf_op jit(solution)/shard_map/ppermute | solution.py:337
  27.8 183.5 %reduce-scatter.3.cloned.1.call-start = ((), (), s32[]{:S(2)}) async-start(), calls=%async_computation.2 | async-start | bytes 2621440 | tf_op jit(solution)/shard_map/reduce_scatter | solution.py:395
  29.5 50.8 %collective-permute-start = (bf16[2048,512]{1,0:T(8,128)(2,1)}, bf16[2048,512]{1,0:T(8,128)(2,1)}, u32[]{:S(2)}, u32[]{:S(2)}) collective-permute-start(bf16[2048,512]{1,0:T(8,128)(2,1)} %get-tuple-element.139.s0), channel_id=1, source_target_pairs={{0,1},{1,0},{2,3},{3,2},{4,5},{5,4},{6,7},{7,6},{8,9},{9,8},{10,11... | collective-permute-start | bytes 6291464 | tf_op jit(solution)/shard_map/ppermute | solution.py:337
  74.6 5.8 %collective-permute-start.8 = (bf16[2048,512]{1,0:T(8,128)(2,1)}, bf16[2048,512]{1,0:T(8,128)(2,1)}, u32[]{:S(2)}, u32[]{:S(2)}) collective-permute-start(bf16[2048,512]{1,0:T(8,128)(2,1)} %collective-permute-done.3.s2), channel_id=1, source_target_pairs={{0,1},{1,0},{2,3},{3,2},{4,5},{5,4},{6,7},{7,6},{8,9},{9,8},{10,11... | collective-permute-start | bytes 6291464 | tf_op jit(solution)/shard_map/ppermute | solution.py:337
  75.6 53.8 %collective-permute-start.13 = (bf16[2048,512]{1,0:T(8,128)(2,1)S(1)}, bf16[2048,512]{1,0:T(8,128)(2,1)}, u32[]{:S(2)}, u32[]{:S(2)}) collective-permute-start(bf16[2048,512]{1,0:T(8,128)(2,1)S(1)} %copy-done), channel_id=1, source_target_pairs={{0,2},{1,3},{2,0},{3,1},{4,6},{5,7},{6,4},{7,5},{8,10},{9,11},{10,... | collective-permute-start | bytes 6291464 | tf_op jit(solution)/shard_map/ppermute | solution.py:337
  98.0 11.2 %collective-permute-start.10 = (f32[2,4,8,256]{3,2,1,0:T(8,128)}, f32[2,4,8,256]{3,2,1,0:T(8,128)S(1)}, u32[]{:S(2)}, u32[]{:S(2)}) collective-permute-start(f32[2,4,8,256]{3,2,1,0:T(8,128)} %get-tuple-element.151.refs_0_), channel_id=1, source_target_pairs={{0,8},{1,9},{2,10},{3,11},{4,12},{5,13},{6,14},{7,15},{8,0},{9,1},... | collective-permute-start | bytes 196616 | tf_op jit(solution)/shard_map/ppermute | solution.py:337
  99.0 10.1 %collective-permute-start.11 = (f32[2,4,8,256]{3,2,1,0:T(8,128)}, f32[2,4,8,256]{3,2,1,0:T(8,128)S(1)}, u32[]{:S(2)}, u32[]{:S(2)}) collective-permute-start(f32[2,4,8,256]{3,2,1,0:T(8,128)} %get-tuple-element.151.refs_0_), channel_id=1, source_target_pairs={{0,12},{1,13},{2,14},{3,15},{4,8},{5,9},{6,10},{7,11},{8,4},{9,5},... | collective-permute-start | bytes 196616 | tf_op jit(solution)/shard_map/ppermute | solution.py:337
  100.5 8.7 %collective-permute-start.9 = (f32[2,4,8,256]{3,2,1,0:T(8,128)}, f32[2,4,8,256]{3,2,1,0:T(8,128)S(1)}, u32[]{:S(2)}, u32[]{:S(2)}) collective-permute-start(f32[2,4,8,256]{3,2,1,0:T(8,128)} %get-tuple-element.151.refs_0_), channel_id=1, source_target_pairs={{0,4},{1,5},{2,6},{3,7},{4,0},{5,1},{6,2},{7,3},{8,12},{9,13},{10,... | collective-permute-start | bytes 196616 | tf_op jit(solution)/shard_map/ppermute | solution.py:337
  116.8 95.6 %reduce-scatter.5.cloned.1.call-start = ((), (), s32[]{:S(2)}) async-start(), calls=%async_computation.3 | async-start | bytes 1310720 | tf_op jit(solution)/shard_map/reduce_scatter | solution.py:395
  117.1 12.9 %collective-permute-start.12 = (bf16[2048,512]{1,0:T(8,128)(2,1)S(1)}, bf16[2048,512]{1,0:T(8,128)(2,1)}, u32[]{:S(2)}, u32[]{:S(2)}) collective-permute-start(bf16[2048,512]{1,0:T(8,128)(2,1)S(1)} %copy-done), channel_id=1, source_target_pairs={{0,1},{1,0},{2,3},{3,2},{4,5},{5,4},{6,7},{7,6},{8,9},{9,8},{10,11... | collective-permute-start | bytes 6291464 | tf_op jit(solution)/shard_map/ppermute | solution.py:337
  129.4 4.5 %collective-permute-start.14 = (bf16[2048,512]{1,0:T(8,128)(2,1)}, bf16[2048,512]{1,0:T(8,128)(2,1)S(1)}, u32[]{:S(2)}, u32[]{:S(2)}) collective-permute-start(bf16[2048,512]{1,0:T(8,128)(2,1)} %collective-permute-done.13.s2), channel_id=1, source_target_pairs={{0,1},{1,0},{2,3},{3,2},{4,5},{5,4},{6,7},{7,6},{8,9},{9,8},{10,11... | collective-permute-start | bytes 6291464 | tf_op jit(solution)/shard_map/ppermute | solution.py:337
  145.8 16.0 %collective-permute-start.15 = (f32[1,4,8,256]{3,2,1,0:T(8,128)}, f32[1,4,8,256]{3,2,1,0:T(8,128)S(1)}, u32[]{:S(2)}, u32[]{:S(2)}) collective-permute-start(f32[1,4,8,256]{3,2,1,0:T(8,128)} %get-tuple-element.190.refs_0_), channel_id=1, source_target_pairs={{0,4},{1,5},{2,6},{3,7},{4,0},{5,1},{6,2},{7,3},{8,12},{9,13},{10,... | collective-permute-start | bytes 98312 | tf_op jit(solution)/shard_map/ppermute | solution.py:337
  148.3 13.4 %collective-permute-start.16 = (f32[1,4,8,256]{3,2,1,0:T(8,128)}, f32[1,4,8,256]{3,2,1,0:T(8,128)S(1)}, u32[]{:S(2)}, u32[]{:S(2)}) collective-permute-start(f32[1,4,8,256]{3,2,1,0:T(8,128)} %get-tuple-element.190.refs_0_), channel_id=1, source_target_pairs={{0,8},{1,9},{2,10},{3,11},{4,12},{5,13},{6,14},{7,15},{8,0},{9,1},... | collective-permute-start | bytes 98312 | tf_op jit(solution)/shard_map/ppermute | solution.py:337
  148.3 13.5 %collective-permute-start.17 = (f32[1,4,8,256]{3,2,1,0:T(8,128)}, f32[1,4,8,256]{3,2,1,0:T(8,128)S(1)}, u32[]{:S(2)}, u32[]{:S(2)}) collective-permute-start(f32[1,4,8,256]{3,2,1,0:T(8,128)} %get-tuple-element.190.refs_0_), channel_id=1, source_target_pairs={{0,12},{1,13},{2,14},{3,15},{4,8},{5,9},{6,10},{7,11},{8,4},{9,5},... | collective-permute-start | bytes 98312 | tf_op jit(solution)/shard_map/ppermute | solution.py:337
  167.9 5.1 %collective-permute-start.18 = (f32[1,4,8,256]{3,2,1,0:T(8,128)S(1)}, f32[1,4,8,256]{3,2,1,0:T(8,128)S(1)}, u32[]{:S(2)}, u32[]{:S(2)}) collective-permute-start(f32[1,4,8,256]{3,2,1,0:T(8,128)S(1)} %copy-done.14), channel_id=1, source_target_pairs={{0,4},{1,5},{2,6},{3,7},{4,0},{5,1},{6,2},{7,3},{8,12},{9,13},{10,... | collective-permute-start | bytes 98312 | tf_op jit(solution)/shard_map/ppermute | solution.py:337
  169.0 5.5 %collective-permute-start.19 = (f32[1,4,8,256]{3,2,1,0:T(8,128)S(1)}, f32[1,4,8,256]{3,2,1,0:T(8,128)S(1)}, u32[]{:S(2)}, u32[]{:S(2)}) collective-permute-start(f32[1,4,8,256]{3,2,1,0:T(8,128)S(1)} %copy-done.14), channel_id=1, source_target_pairs={{0,8},{1,9},{2,10},{3,11},{4,12},{5,13},{6,14},{7,15},{8,0},{9,1},... | collective-permute-start | bytes 98312 | tf_op jit(solution)/shard_map/ppermute | solution.py:337
  169.9 5.8 %collective-permute-start.20 = (f32[1,4,8,256]{3,2,1,0:T(8,128)S(1)}, f32[1,4,8,256]{3,2,1,0:T(8,128)S(1)}, u32[]{:S(2)}, u32[]{:S(2)}) collective-permute-start(f32[1,4,8,256]{3,2,1,0:T(8,128)S(1)} %copy-done.14), channel_id=1, source_target_pairs={{0,12},{1,13},{2,14},{3,15},{4,8},{5,9},{6,10},{7,11},{8,4},{9,5},... | collective-permute-start | bytes 98312 | tf_op jit(solution)/shard_map/ppermute | solution.py:337
  182.5 20.5 %collective-permute-start.21 = (bf16[1,256,512]{2,1,0:T(8,128)(2,1)}, bf16[1,256,512]{2,1,0:T(8,128)(2,1)S(1)}, u32[]{:S(2)}, u32[]{:S(2)}) collective-permute-start(bf16[1,256,512]{2,1,0:T(8,128)(2,1)} %get-tuple-element.202), channel_id=1, source_target_pairs={{0,4},{1,5},{2,6},{3,7},{4,0},{5,1},{6,2},{7,3},{8,12},{9,13},{10,... | collective-permute-start | bytes 786440 | tf_op jit(solution)/shard_map/ppermute | solution.py:337
  182.5 20.5 %collective-permute-start.22 = (bf16[1,256,512]{2,1,0:T(8,128)(2,1)}, bf16[1,256,512]{2,1,0:T(8,128)(2,1)S(1)}, u32[]{:S(2)}, u32[]{:S(2)}) collective-permute-start(bf16[1,256,512]{2,1,0:T(8,128)(2,1)} %get-tuple-element.203), channel_id=1, source_target_pairs={{0,8},{1,9},{2,10},{3,11},{4,12},{5,13},{6,14},{7,15},{8,0},{9,1},... | collective-permute-start | bytes 786440 | tf_op jit(solution)/shard_map/ppermute | solution.py:337
  185.9 24.2 %collective-permute-start.23 = (bf16[1,256,512]{2,1,0:T(8,128)(2,1)}, bf16[1,256,512]{2,1,0:T(8,128)(2,1)S(1)}, u32[]{:S(2)}, u32[]{:S(2)}) collective-permute-start(bf16[1,256,512]{2,1,0:T(8,128)(2,1)} %get-tuple-element.204), channel_id=1, source_target_pairs={{0,12},{1,13},{2,14},{3,15},{4,8},{5,9},{6,10},{7,11},{8,4},{9,5},... | collective-permute-start | bytes 786440 | tf_op jit(solution)/shard_map/ppermute | solution.py:337
  (27 other events, 95.6 us)
Sparse Core Ops, SparseCore 0:
  11.1 51.0 all-gather.4
  63.7 50.3 all-gather.6
  116.9 47.8 reduce-scatter.2
  168.0 33.2 reduce-scatter.4

commit v4 on v3

--- a/solution.py
+++ b/solution.py
@@ -21,7 +21,6 @@
 MASKED = -1e30
 QW = G * HD
 CHUNKS = ((0, 1), (2, 3))
-ID_ROWS = 16
 GROUPS = (((0, 1), "scatter"), ((2,), "direct"), ((3,), "direct"))
 
 
@@ -101,17 +100,23 @@
 def scale_kernel(planes, heads, scattered, info, um_ref, own_ref, uc_ref, gate_ref, *refs):
     lse_refs, out_refs = refs[:planes], refs[planes:]
     slot = pl.program_id(0)
+    row = lax.broadcasted_iota(jnp.int32, (16, 2 * QW), 0) % 8
+    spread = (row == lax.broadcasted_iota(jnp.int32, (16, 2 * QW), 1) // HD).astype(jnp.bfloat16)
     for h in range(heads):
         parts = [lse_refs[k][h, jnp.bitwise_xor(slot, k)] for k in range(planes)]
         top = functools.reduce(jnp.maximum, parts)
         total = functools.reduce(jnp.add, [jnp.exp2(p - top) for p in parts])
         weight = jnp.exp2(parts[0] - top) / total * gate_ref[h]
-        wt = jnp.concatenate([weight, jnp.zeros((HD - 8, QBLK), jnp.float32)], axis=0).T
+        high = weight.astype(jnp.bfloat16)
+        low = (weight - high.astype(jnp.float32)).astype(jnp.bfloat16)
+        wide = lax.dot_general(
+            jnp.concatenate([high, low], axis=0), spread, (((0,), (0,)), ((), ())), preferred_element_type=jnp.float32
+        )
         for g in range(G):
             cols = slice(g * HD, (g + 1) * HD)
-            term = wt[:, g : g + 1] * um_ref[h, 0, :, cols].astype(jnp.float32)
+            term = wide[:, cols] * um_ref[h, 0, :, cols].astype(jnp.float32)
             ctx = jnp.where(slot == 0, own_ref[h, 0, :, cols], uc_ref[h, 0, :, cols])
-            term += wt[:, G + g : G + g + 1] * ctx.astype(jnp.float32)
+            term += wide[:, QW + g * HD : QW + (g + 1) * HD] * ctx.astype(jnp.float32)
             term = term.astype(jnp.bfloat16)
             if scattered:
                 out_refs[0][0, h, :, cols] = term
@@ -227,7 +232,8 @@
     )(info, um, own, uc, gate_rows, *lses)
 
 
-def route_kernel(planes, local_count, ids_ref, slot_ref, place_ref, out_ref):
+def route_kernel(planes, local_count, *refs):
+    ids_refs, (slot_ref, place_ref, out_ref) = refs[:planes], refs[planes:]
     entries = slot_ref.shape[0]
     plane, within = place_ref[0], place_ref[1]
     before = lax.broadcasted_iota(jnp.int32, (TOPM, TOPM), 0) <= lax.broadcasted_iota(jnp.int32, (TOPM, TOPM), 1)
@@ -236,9 +242,7 @@
     holder = plane * WITHIN + jnp.bitwise_xor(within, source)
     lane = lax.broadcasted_iota(jnp.int32, (1, HD), 1)
     for k in range(planes):
-        halves = ids_ref[jnp.bitwise_xor(plane, k), :8, : 2 * TOPM].astype(jnp.float32)[:1].astype(jnp.int32)
-        ids = halves[:, :TOPM] * 256 + halves[:, TOPM:]
-        hits = lax.broadcasted_iota(jnp.int32, (entries, TOPM), 0) == ids
+        hits = lax.broadcasted_iota(jnp.int32, (entries, TOPM), 0) == ids_refs[k][...]
         slots = jnp.sum(jnp.where(hits, slot_ref[...], 0), axis=0, keepdims=True)
         held = (slots // local_count == holder) & (source < WITHIN)
         rank = jnp.dot(held.astype(jnp.float32), before, preferred_element_type=jnp.float32)
@@ -251,63 +255,87 @@
         out_ref[k : k + 1, :] = row[:, :8]
 
 
-def route_call(place, gathered, block_slot, local_count):
-    planes = gathered.shape[0]
+def route_call(place, ids, block_slot, local_count):
+    planes = len(ids)
     return pl.pallas_call(
         functools.partial(route_kernel, planes, local_count),
         grid=(1,),
-        in_specs=[
-            pl.BlockSpec((planes, ID_ROWS, HD), lambda i: (0, QBLK // ID_ROWS, 0)),
-            whole((block_slot.shape[0], 1)),
-            pl.BlockSpec(memory_space=pltpu.SMEM),
-        ],
+        in_specs=[whole((1, TOPM))] * planes
+        + [whole((block_slot.shape[0], 1)), pl.BlockSpec(memory_space=pltpu.SMEM)],
         out_specs=whole((planes, 8)),
         out_shape=jax.ShapeDtypeStruct((planes, 8), jnp.int32),
         compiler_params=PARAMS,
         cost_estimate=SMALL,
         name="route_blocks",
-    )(gathered, block_slot[:, None], place)
-
-
-def pack_kernel(stores, chunks, first, q, k, v, ids, *outs):
-    for n, heads in enumerate(stores):
-        for i, head in enumerate(heads):
-            cols = slice(head * HD, (head + 1) * HD)
-            outs[n][:, 2 * i * HD : (2 * i + 1) * HD] = k[:, cols]
-            outs[n][:, (2 * i + 1) * HD : (2 * i + 2) * HD] = v[:, cols]
-
-    @pl.when(pl.program_id(0) == 0)
-    def _():
-        for n, heads in enumerate(chunks):
-            out = outs[len(stores) + n]
-            out[:QBLK, :] = q[:, heads[0] * QW : (heads[-1] + 1) * QW]
-            if first and n == 0:
-                halves = jnp.concatenate([ids[...] // 256, ids[...] % 256], axis=1).astype(jnp.float32)
-                halves = jnp.concatenate([halves, jnp.zeros((1, out.shape[1] - 2 * TOPM), jnp.float32)], axis=1)
-                out[QBLK:, :] = jnp.broadcast_to(halves, (ID_ROWS, out.shape[1])).astype(jnp.bfloat16)
-
-
-def pack_call(stores, chunks, first, q, k, v, ids):
-    rows, steps = k.shape[0], 4
-    part = rows // steps
-    shapes = [(rows, 2 * len(heads) * HD) for heads in stores]
-    specs = [pl.BlockSpec((part, shape[1]), lambda i: (i, 0)) for shape in shapes]
-    shapes += [(QBLK + ID_ROWS * (first and n == 0), len(heads) * QW) for n, heads in enumerate(chunks)]
-    specs += [whole(shape) for shape in shapes[len(stores) :]]
-    width = (stores[-1][-1] + 1) * HD
-    q_width = (chunks[-1][-1] + 1) * QW if chunks else QW
-    return pl.pallas_call(
-        functools.partial(pack_kernel, stores, chunks, first),
-        grid=(steps,),
-        in_specs=[whole((QBLK, q_width))]
-        + [pl.BlockSpec((part, width), lambda i: (i, 0))] * 2
-        + [whole(ids.shape)],
-        out_specs=specs,
+    )(*ids, block_slot[:, None], place)
+
+
+def pack_queries_kernel(q, *outs):
+    for out, heads in zip(outs, CHUNKS, strict=True):
+        out[...] = q[:, heads[0] * QW : (heads[-1] + 1) * QW]
+
+
+def pack_queries(q):
+    shapes = [(QBLK, len(heads) * QW) for heads in CHUNKS]
+    return pl.pallas_call(
+        pack_queries_kernel,
+        grid=(1,),
+        in_specs=[whole(q.shape)],
+        out_specs=[whole(shape) for shape in shapes],
         out_shape=[jax.ShapeDtypeStruct(shape, jnp.bfloat16) for shape in shapes],
         compiler_params=PACK_PARAMS,
         cost_estimate=SMALL,
-        name="pack_heads",
-    )(q, k, v, ids)
+        name="pack_queries",
+    )(q)
+
+
+def pack_stores_kernel(k, v, out):
+    for i in range(k.shape[1] // HD):
+        cols = slice(i * HD, (i + 1) * HD)
+        out[:, 2 * i * HD : (2 * i + 1) * HD] = k[:, cols]
+        out[:, (2 * i + 1) * HD : (2 * i + 2) * HD] = v[:, cols]
+
+
+def pack_stores(k, v, n):
+    rows, steps = k.shape[0], 4
+    part, width = rows // steps, len(CHUNKS[n]) * HD
+    return pl.pallas_call(
+        pack_stores_kernel,
+        grid=(steps,),
+        in_specs=[pl.BlockSpec((part, width), lambda i: (i, n))] * 2,
+        out_specs=pl.BlockSpec((part, 2 * width), lambda i: (i, 0)),
+        out_shape=jax.ShapeDtypeStruct((rows, 2 * width), jnp.bfloat16),
+        compiler_params=PACK_PARAMS,
+        cost_estimate=SMALL,
+        name="pack_stores",
+    )(k, v)
+
+
+def finish_kernel(counts, *refs):
+    *parts, out_ref = refs
+    head = 0
+    for count, heads in counts:
+        group, parts = parts[:count], parts[count:]
+        for h in range(heads):
+            total = group[0][h]
+            if count > 1:
+                total = sum(part[h].astype(jnp.float32) for part in group).astype(jnp.bfloat16)
+            out_ref[:, (head + h) * QW : (head + h + 1) * QW] = total
+        head += heads
+
+
+def finish_call(groups):
+    flat = [part for parts in groups for part in parts]
+    return pl.pallas_call(
+        functools.partial(finish_kernel, [(len(parts), parts[0].shape[0]) for parts in groups]),
+        grid=(1,),
+        in_specs=[whole(part.shape) for part in flat],
+        out_specs=whole((QBLK, KVH * QW)),
+        out_shape=jax.ShapeDtypeStruct((QBLK, KVH * QW), jnp.bfloat16),
+        compiler_params=PARAMS,
+        cost_estimate=SMALL,
+        name="finish_heads",
+    )(*flat)
 
 
 class Order:
@@ -344,15 +372,17 @@
     values = store_values.reshape(local_count * MROWS, KVH * HD)
     order = Order()
 
-    raw = (queries, keys, values, block_ids)
     ctx_far = [xor(ctx_keys, 2), xor(ctx_values, 2)]
     ctx_near = [xor(ctx_keys, 1), xor(ctx_values, 1)]
-    own_first, q_first = pack_call(CHUNKS[:1], CHUNKS[:1], True, *raw)
+    ids = all_planes(block_ids)
+    q_first, q_second = pack_queries(queries)
     order.done(q_first)
-    own_second, q_second = pack_call(CHUNKS[1:], CHUNKS[1:], False, *order.before(*raw))
-    order.done(q_second, *ctx_far)
-    own = [own_first, own_second]
-    far = [xor(part, 2) for part in order.before(*own)]
+    own = [pack_stores(*order.before(keys, values), 0)]
+    order.done(own[0], *ctx_far)
+    far = [xor(order.before(own[0])[0], 2)]
+    own.append(pack_stores(*order.before(keys, values), 1))
+    order.done(own[1])
+    far.append(xor(own[1], 2))
     ctx_diag = [xor(part, 1) for part in ctx_far]
     near = [xor(part, 1) for part in own]
     diag = [None, None]
@@ -362,7 +392,8 @@
     spread = [lax.all_gather(part, "seq", axis=0, axis_index_groups=columns) for part in (q_first, q_second)]
 
     place = jnp.stack([plane, within] + [plane] * 6).astype(jnp.int32)
-    route = route_call(place, spread[0], block_slot, local_count)
+    route = route_call(place, order.before(*ids), block_slot, local_count)
+    order.done(route)
     place = place[None]
     info = jnp.concatenate([place, route])
     sources = [x for kind in zip((ctx_keys, ctx_values), ctx_near, ctx_far, ctx_diag, strict=True) for x in kind]
@@ -381,7 +412,7 @@
     def mem_step(first, count, ctx_lse):
         n = place_of(first, CHUNKS)[0]
         args = order.before(info, spread[n], own[n], near[n], far[n], diag[n], own_lse, ctx_lse)
-        um, lse = mem_call(*args[:2], args[2:6], *args[6:], first, count, CHUNKS[n][0], planes, masked)
+        um, lse = mem_call(*args[:2], args[2:6], *args[6:], first, count, CHUNKS[n][0] if count > 1 else first, planes, masked)
         order.done(lse)
         return um, all_planes(lse)
 
@@ -389,27 +420,25 @@
         n = place_of(first, CHUNKS)[0]
         um, uc, *lses = order.before(um, uc, *lses)
         gates = gate_rows[first : first + um.shape[0]]
-        parts = scale_call(place, um, own_uc, uc, gates, lses, first, CHUNKS[n][0], scattered)
+        parts = scale_call(place, um, own_uc, uc, gates, lses, first, first, scattered)
         order.done(parts[0])
         if scattered:
             return [lax.psum_scatter(parts[0], "seq", scatter_dimension=0, axis_index_groups=columns)]
         return [parts[0]] + [xor(parts[k], k * WITHIN) for k in range(1, planes)]
-
-    def total(parts):
-        return sum(part.astype(jnp.float32) for part in parts).astype(jnp.bfloat16)
 
     own_uc, own_lse = ctx_step(queries, 0, KVH, 1)
     uc01, ctx_lse01 = ctx_step(spread[0], 0, 2, planes)
     fetch_step(0)
     um01, lses01 = mem_step(0, 2, ctx_lse01)
     coming = [scale_step(0, um01, uc01, lses01, True)]
-    uc23, ctx_lse23 = ctx_step(spread[1], 2, 2, planes)
+    uc2, ctx_lse2 = ctx_step(spread[1], 2, 1, planes)
     fetch_step(1)
-    um2, lses2 = mem_step(2, 1, ctx_lse23)
-    um3, lses3 = mem_step(3, 1, ctx_lse23)
-    coming.append(scale_step(2, um2, uc23, lses2, True))
-    coming.append(scale_step(3, um3, uc23, lses3, False))
-    return jnp.concatenate([part for parts in coming for part in total(parts)], axis=1)
+    uc3, ctx_lse3 = ctx_step(spread[1], 3, 1, planes)
+    um2, lses2 = mem_step(2, 1, ctx_lse2)
+    um3, lses3 = mem_step(3, 1, ctx_lse3)
+    coming.append(scale_step(2, um2, uc2, lses2, True))
+    coming.append(scale_step(3, um3, uc3, lses3, False))
+    return finish_call(coming)
 
 
 def solution(mesh):

time: 224 us -> 219 us (0.978)
  waiting for transfers between devices: 66.5 us -> 55.7 us
  Pallas kernels: 102 us -> 107 us
  starting transfers between devices: 25.8 us -> 30.4 us
  other arithmetic: 4.5 us -> 0.68 us
    all_gather x2, waiting for transfers between devices: 21.5 us -> 4.03 us  [on_device(): lax.all_gather(part, 'seq', axis=0, axis_index_groups=columns)]
    ppermute x24 -> x27, waiting for transfers between devices: 44.9 us -> 51.6 us  [xor(): return lax.ppermute(x, 'seq', [(i, i ^ bits) for i in range(devices)])]
    ppermute x24 -> x27, starting transfers between devices: 25.5 us -> 30.1 us  [xor(): return lax.ppermute(x, 'seq', [(i, i ^ bits) for i in range(devices)])]
    pallas_call x2 -> x4, Pallas kernels: 9.27 us -> 12.7 us  [the longest x2 7.86 us: pack_stores(): pl.pallas_call(pack_stores_kernel, grid=(steps,), in_specs=[pl.BlockSpec(...]
    pallas_call x3 -> x4, Pallas kernels: 34.1 us -> 36.5 us  [ctx_call(): pl.pallas_call(functools.partial(ctx_kernel, base), grid_spec=pltpu.Prefe...]
    unnamed x46 -> x62, local copies, waits for them, and re-layouts: 4.02 us -> 4.91 us
  transfers between devices with their start and end apart: 28 -> 31, of which waited for: 12 -> 12; matrix products, arithmetic and copies ran while one was open for 3% -> 2% of each run, Pallas kernels for 44% -> 47%
where the time goes in v4:
time: 219 us; the launch traced here: 215 us
  Pallas kernels  107 us (49%)
  waiting for transfers between devices  55.7 us (25%)
  starting transfers between devices  30.4 us (14%)
  between operations  13.4 us (6%)
  local copies, waits for them, and re-layouts  8.5 us (4%)
    ppermute x27, waiting for transfers between devices, xor(): return lax.ppermute(x, 'seq', [(i, i ^ bits) for i in range(devices)])  51.6 us
    pallas_call x3, Pallas kernels, mem_call(): pl.pallas_call(functools.partial(mem_kernel, masked), grid_spec=pltpu.Pre...  38.4 us
    pallas_call x4, Pallas kernels, ctx_call(): pl.pallas_call(functools.partial(ctx_kernel, base), grid_spec=pltpu.Prefe...  36.5 us
    ppermute x27, starting transfers between devices, xor(): return lax.ppermute(x, 'seq', [(i, i ^ bits) for i in range(devices)])  30.1 us
    pallas_call x3, Pallas kernels, scale_call(): pl.pallas_call(functools.partial(scale_kernel, planes, heads, scattered),...  17.3 us
    pallas_call x2, Pallas kernels, pack_stores(): pl.pallas_call(pack_stores_kernel, grid=(steps,), in_specs=[pl.BlockSpec(...  7.86 us
    unnamed x62, local copies, waits for them, and re-layouts  4.91 us
  transfers between devices with their start and end apart: 31, of which 12 were waited for; matrix products, arithmetic and copies ran while one was open for 2% of the time, Pallas kernels for 47%

profile of v4, /device:TPU:0, one launch (start us, length us, event | category | flops | bytes accessed | tf_op | source)
XLA Modules:
  0.0 215.4 jit_solution(7849378772681371651)
XLA Ops:
  8.8 3.0 %collective-permute-start.3 = (bf16[256,512]{1,0:T(8,128)(2,1)}, bf16[256,512]{1,0:T(8,128)(2,1)S(1)}, u32[]{:S(2)}, u32[]{:S(2)}) collective-permute-start(bf16[256,512]{1,0:T(8,128)(2,1)} %k0.3), channel_id=1, source_target_pairs={{0,2},{1,3},{2,0},{3,1},{4,6},{5,7},{6,4},{7,5},{8,10},{9,11},{10,... | collective-permute-start | bytes 786440 | tf_op jit(solution)/shard_map/ppermute | solution.py:365
  12.0 3.9 %pack_stores.2.s0 = bf16[2048,512]{1,0:T(8,128)(2,1)} custom-call(bf16[2048,512]{1,0:T(8,128)(2,1)} %bitcast.20, bf16[2048,512]{1,0:T(8,128)(2,1)} %bitcast.22), custom_call_target="tpu_custom_call" | custom-call | flops 1000 | bytes 1000 | tf_op jit(solution)/shard_map/pack_stores/pallas_call | solution.py:302
  15.9 3.3 %collective-permute-done.3.k2 = bf16[256,512]{1,0:T(8,128)(2,1)S(1)} collective-permute-done((bf16[256,512]{1,0:T(8,128)(2,1)}, bf16[256,512]{1,0:T(8,128)(2,1)S(1)}, u32[]{:S(2)}, u32[]{:S(2)}) %collective-permute-start.3) | collective-permute-done | bytes 262176 | tf_op jit(solution)/shard_map/ppermute | solution.py:365
  19.2 4.8 %collective-permute-done.4.v2 = bf16[256,512]{1,0:T(8,128)(2,1)S(1)} collective-permute-done((bf16[256,512]{1,0:T(8,128)(2,1)}, bf16[256,512]{1,0:T(8,128)(2,1)S(1)}, u32[]{:S(2)}, u32[]{:S(2)}) %collective-permute-start.4) | collective-permute-done | bytes 262176 | tf_op jit(solution)/shard_map/ppermute | solution.py:365
  32.0 3.4 %collective-permute-done.2.refs_3_ = s32[1,32]{1,0:T(1,128)S(1)} collective-permute-done((s32[1,32]{1,0:T(1,128)S(1)}, s32[1,32]{1,0:T(1,128)S(1)}, u32[]{:S(2)}, u32[]{:S(2)}) %collective-permute-start.2) | collective-permute-done | bytes 160 | tf_op jit(solution)/shard_map/ppermute | solution.py:365
  36.9 3.9 %pack_stores.3.s0 = bf16[2048,512]{1,0:T(8,128)(2,1)} custom-call(bf16[2048,512]{1,0:T(8,128)(2,1)} %bitcast.21, bf16[2048,512]{1,0:T(8,128)(2,1)} %bitcast.23), custom_call_target="tpu_custom_call" | custom-call | flops 1000 | bytes 1000 | tf_op jit(solution)/shard_map/pack_stores/pallas_call | solution.py:302
  44.2 9.4 %ctx_attend.4 = (bf16[4,1,256,512]{3,2,1,0:T(8,128)(2,1)}, f32[4,1,8,256]{3,2,1,0:T(8,128)}) custom-call(s32[1,8]{1,0:T(1,128)} %bitcast.28, bf16[256,2048]{1,0:T(8,128)(2,1)} %q_ref, bf16[256,512]{1,0:T(8,128)(2,1)} %k0.3, bf16[256,512]{1,0:T(8,128)(2,1)} %copy-done.6, bf16[256,512]{1,0:T(8,128)(2,1)} %copy-done.4, bf16[256,512]{1,0:T(8,128)(2,1)} %copy-done.9, ...), custom_call_target="tpu_custom_call" | custom-call | flops 1000 | bytes 1000 | tf_op jit(solution)/shard_map/ctx_attend/pallas_call | solution.py:168
  53.6 4.0 %all-gather.5.cloned.1.call-done = bf16[1024,1024]{1,0:T(8,128)(2,1)} async-done(((bf16[256,1024]{1,0:T(8,128)(2,1)}), bf16[1024,1024]{1,0:T(8,128)(2,1)}) %all-gather.5.cloned.1.call-update) | async-done | bytes 2097168 | tf_op jit(solution)/shard_map/all_gather | solution.py:392
  57.6 12.4 %ctx_attend.5 = (bf16[2,3,256,512]{3,2,1,0:T(8,128)(2,1)}, f32[2,3,8,256]{3,2,1,0:T(8,128)}) custom-call(s32[1,8]{1,0:T(1,128)} %bitcast.29, bf16[4,256,1024]{2,1,0:T(8,128)(2,1)} %bitcast.24, bf16[256,512]{1,0:T(8,128)(2,1)} %k0.3, bf16[256,512]{1,0:T(8,128)(2,1)} %copy-done.6, bf16[256,512]{1,0:T(8,128)(2,1)} %copy-done.4, bf16[256,512]{1,0:T(8,128)(2,1)} %copy-done.9, ...), custom_call_target="tpu_custom_call" | custom-call | flops 1000 | bytes 1000 | tf_op jit(solution)/shard_map/ctx_attend/pallas_call | solution.py:168
  75.8 17.7 %mem_attend.3 = (bf16[2,4,256,512]{3,2,1,0:T(8,128)(2,1)}, f32[2,4,8,256]{3,2,1,0:T(8,128)}) custom-call(s32[5,8]{1,0:T(8,128)} %pad_add_fusion.info, bf16[4,256,1024]{2,1,0:T(8,128)(2,1)} %bitcast.25, bf16[2048,512]{1,0:T(8,128)(2,1)} %pack_stores.2.s0, bf16[2048,512]{1,0:T(8,128)(2,1)} %collective-permute-done.5.s1, ...), custom_call_target="tpu_custom_call" | custom-call | flops 1000 | bytes 1000 | tf_op jit(solution)/shard_map/mem_attend/pallas_call | solution.py:187
  98.5 5.0 %collective-permute-done.12.refs_1_ = f32[2,4,8,256]{3,2,1,0:T(8,128)S(1)} collective-permute-done((f32[2,4,8,256]{3,2,1,0:T(8,128)}, f32[2,4,8,256]{3,2,1,0:T(8,128)S(1)}, u32[]{:S(2)}, u32[]{:S(2)}) %collective-permute-start.12) | collective-permute-done | bytes 65568 | tf_op jit(solution)/shard_map/ppermute | solution.py:365
  103.5 3.8 %collective-permute-done.13.refs_2_ = f32[2,4,8,256]{3,2,1,0:T(8,128)S(1)} collective-permute-done((f32[2,4,8,256]{3,2,1,0:T(8,128)}, f32[2,4,8,256]{3,2,1,0:T(8,128)S(1)}, u32[]{:S(2)}, u32[]{:S(2)}) %collective-permute-start.13) | collective-permute-done | bytes 65568 | tf_op jit(solution)/shard_map/ppermute | solution.py:365
  107.9 6.3 %scale_mix.3 = bf16[4,2,256,512]{3,2,1,0:T(8,128)(2,1)} custom-call(s32[1,8]{1,0:T(1,128)} %bitcast.30, bf16[2,4,256,512]{3,2,1,0:T(8,128)(2,1)} %get-tuple-element.162.um_ref, bf16[4,1,256,512]{3,2,1,0:T(8,128)(2,1)} %get-tuple-element.163.own_ref, bf16[2,3,256,512]{3,2,1,0:T(8,128)(2,1)} %get-tuple-element.164.uc_ref, f32[2,8,1]{2,1,0:T(8,128)} %copy.13.gate_ref, ...), custom_call_target="tpu_custom_call" | custom-call | flops 1000 | bytes 1000 | tf_op jit(solution)/shard_map/scale_mix/pallas_call | solution.py:220
  114.7 7.3 %ctx_attend.6 = (bf16[1,3,256,512]{3,2,1,0:T(8,128)(2,1)}, f32[1,3,8,256]{3,2,1,0:T(8,128)}) custom-call(s32[1,8]{1,0:T(1,128)} %bitcast.31, bf16[4,256,1024]{2,1,0:T(8,128)(2,1)} %bitcast.16, bf16[256,512]{1,0:T(8,128)(2,1)} %k0.3, bf16[256,512]{1,0:T(8,128)(2,1)} %copy-done.6, bf16[256,512]{1,0:T(8,128)(2,1)} %copy-done.4, bf16[256,512]{1,0:T(8,128)(2,1)} %copy-done.9, ...), custom_call_target="tpu_custom_call" | custom-call | flops 1000 | bytes 1000 | tf_op jit(solution)/shard_map/ctx_attend/pallas_call | solution.py:168
  122.5 7.3 %ctx_attend.7 = (bf16[1,3,256,512]{3,2,1,0:T(8,128)(2,1)}, f32[1,3,8,256]{3,2,1,0:T(8,128)}) custom-call(s32[1,8]{1,0:T(1,128)} %bitcast.32, bf16[4,256,1024]{2,1,0:T(8,128)(2,1)} %bitcast.17, bf16[256,512]{1,0:T(8,128)(2,1)} %k0.3, bf16[256,512]{1,0:T(8,128)(2,1)} %copy-done.6, bf16[256,512]{1,0:T(8,128)(2,1)} %copy-done.4, bf16[256,512]{1,0:T(8,128)(2,1)} %copy-done.9, ...), custom_call_target="tpu_custom_call" | custom-call | flops 1000 | bytes 1000 | tf_op jit(solution)/shard_map/ctx_attend/pallas_call | solution.py:168
  131.3 10.3 %mem_attend.4 = (bf16[1,4,256,512]{3,2,1,0:T(8,128)(2,1)}, f32[1,4,8,256]{3,2,1,0:T(8,128)}) custom-call(s32[5,8]{1,0:T(8,128)} %pad_add_fusion.info, bf16[4,256,1024]{2,1,0:T(8,128)(2,1)} %bitcast.18, bf16[2048,512]{1,0:T(8,128)(2,1)} %pack_stores.3.s0, bf16[2048,512]{1,0:T(8,128)(2,1)} %collective-permute-done.15.s1, ...), custom_call_target="tpu_custom_call" | custom-call | flops 1000 | bytes 1000 | tf_op jit(solution)/shard_map/mem_attend/pallas_call | solution.py:187
  141.7 4.3 %collective-permute-start.20 = (f32[1,4,8,256]{3,2,1,0:T(8,128)}, f32[1,4,8,256]{3,2,1,0:T(8,128)S(1)}, u32[]{:S(2)}, u32[]{:S(2)}) collective-permute-start(f32[1,4,8,256]{3,2,1,0:T(8,128)} %get-tuple-element.215.refs_0_), channel_id=1, source_target_pairs={{0,12},{1,13},{2,14},{3,15},{4,8},{5,9},{6,10},{7,11},{8,4},{9,5},... | collective-permute-start | bytes 98312 | tf_op jit(solution)/shard_map/ppermute | solution.py:365
  146.7 10.3 %mem_attend.5 = (bf16[1,4,256,512]{3,2,1,0:T(8,128)(2,1)}, f32[1,4,8,256]{3,2,1,0:T(8,128)}) custom-call(s32[5,8]{1,0:T(8,128)} %pad_add_fusion.info, bf16[4,256,1024]{2,1,0:T(8,128)(2,1)} %bitcast.19, bf16[2048,512]{1,0:T(8,128)(2,1)} %pack_stores.3.s0, bf16[2048,512]{1,0:T(8,128)(2,1)} %collective-permute-done.15.s1, ...), custom_call_target="tpu_custom_call" | custom-call | flops 1000 | bytes 1000 | tf_op jit(solution)/shard_map/mem_attend/pallas_call | solution.py:187
  157.7 5.3 %scale_mix.4 = bf16[4,1,256,512]{3,2,1,0:T(8,128)(2,1)} custom-call(s32[1,8]{1,0:T(1,128)} %bitcast.33, bf16[1,4,256,512]{3,2,1,0:T(8,128)(2,1)} %get-tuple-element.213.um_ref, bf16[4,1,256,512]{3,2,1,0:T(8,128)(2,1)} %get-tuple-element.163.own_ref, bf16[1,3,256,512]{3,2,1,0:T(8,128)(2,1)} %get-tuple-element.214.uc_ref, f32[1,8,1]{2,1,0:T(8,128)} %copy.14.gate_ref, ...), custom_call_target="tpu_custom_call" | custom-call | flops 1000 | bytes 1000 | tf_op jit(solution)/shard_map/scale_mix/pallas_call | solution.py:220
  163.7 3.8 %collective-permute-start.23 = (f32[1,4,8,256]{3,2,1,0:T(8,128)S(1)}, f32[1,4,8,256]{3,2,1,0:T(8,128)S(1)}, u32[]{:S(2)}, u32[]{:S(2)}) collective-permute-start(f32[1,4,8,256]{3,2,1,0:T(8,128)S(1)} %copy-done.17), channel_id=1, source_target_pairs={{0,12},{1,13},{2,14},{3,15},{4,8},{5,9},{6,10},{7,11},{8,4},{9,5},... | collective-permute-start | bytes 98312 | tf_op jit(solution)/shard_map/ppermute | solution.py:365
  170.3 5.7 %scale_mix.5 = (bf16[1,256,512]{2,1,0:T(8,128)(2,1)}, bf16[1,256,512]{2,1,0:T(8,128)(2,1)}, bf16[1,256,512]{2,1,0:T(8,128)(2,1)}, bf16[1,256,512]{2,1,0:T(8,128)(2,1)}) custom-call(s32[1,8]{1,0:T(1,128)} %bitcast.34, bf16[1,4,256,512]{3,2,1,0:T(8,128)(2,1)} %get-tuple-element.221.um_ref, bf16[4,1,256,512]{3,2,1,0:T(8,128)(2,1)} %get-tuple-element.163.own_ref, ...), custom_call_target="tpu_custom_call" | custom-call | flops 1000 | bytes 1000 | tf_op jit(solution)/shard_map/scale_mix/pallas_call | solution.py:220
  176.2 4.3 %collective-permute-start.25 = (bf16[1,256,512]{2,1,0:T(8,128)(2,1)}, bf16[1,256,512]{2,1,0:T(8,128)(2,1)S(1)}, u32[]{:S(2)}, u32[]{:S(2)}) collective-permute-start(bf16[1,256,512]{2,1,0:T(8,128)(2,1)} %get-tuple-element.229), channel_id=1, source_target_pairs={{0,8},{1,9},{2,10},{3,11},{4,12},{5,13},{6,14},{7,15},{8,0},{9,1},... | collective-permute-start | bytes 786440 | tf_op jit(solution)/shard_map/ppermute | solution.py:365
  180.5 17.6 %collective-permute-done.24.refs_3_ = bf16[1,256,512]{2,1,0:T(8,128)(2,1)S(1)} collective-permute-done((bf16[1,256,512]{2,1,0:T(8,128)(2,1)}, bf16[1,256,512]{2,1,0:T(8,128)(2,1)S(1)}, u32[]{:S(2)}, u32[]{:S(2)}) %collective-permute-start.24) | collective-permute-done | bytes 262176 | tf_op jit(solution)/shard_map/ppermute | solution.py:365
  198.1 7.5 %collective-permute-done.26.refs_5_ = bf16[1,256,512]{2,1,0:T(8,128)(2,1)S(1)} collective-permute-done((bf16[1,256,512]{2,1,0:T(8,128)(2,1)}, bf16[1,256,512]{2,1,0:T(8,128)(2,1)S(1)}, u32[]{:S(2)}, u32[]{:S(2)}) %collective-permute-start.26) | collective-permute-done | bytes 262176 | tf_op jit(solution)/shard_map/ppermute | solution.py:365
  (131 shorter events, 37.3 us)
Async XLA Ops:
  6.5 51.1 %all-gather.5.cloned.1.call-start = ((), (), s32[]{:S(2)}) async-start(), calls=%async_computation.4 | async-start | bytes 2621440 | tf_op jit(solution)/shard_map/all_gather | solution.py:392
  8.8 105.8 %all-gather.7.cloned.1.call-start = ((), (), s32[]{:S(2)}) async-start(), calls=%async_computation.5 | async-start | bytes 2621440 | tf_op jit(solution)/shard_map/all_gather | solution.py:392
  8.8 10.4 %collective-permute-start.3 = (bf16[256,512]{1,0:T(8,128)(2,1)}, bf16[256,512]{1,0:T(8,128)(2,1)S(1)}, u32[]{:S(2)}, u32[]{:S(2)}) collective-permute-start(bf16[256,512]{1,0:T(8,128)(2,1)} %k0.3), channel_id=1, source_target_pairs={{0,2},{1,3},{2,0},{3,1},{4,6},{5,7},{6,4},{7,5},{8,10},{9,11},{10,... | collective-permute-start | bytes 786440 | tf_op jit(solution)/shard_map/ppermute | solution.py:365
  11.9 12.1 %collective-permute-start.4 = (bf16[256,512]{1,0:T(8,128)(2,1)}, bf16[256,512]{1,0:T(8,128)(2,1)S(1)}, u32[]{:S(2)}, u32[]{:S(2)}) collective-permute-start(bf16[256,512]{1,0:T(8,128)(2,1)} %v0.3), channel_id=1, source_target_pairs={{0,2},{1,3},{2,0},{3,1},{4,6},{5,7},{6,4},{7,5},{8,10},{9,11},{10,... | collective-permute-start | bytes 786440 | tf_op jit(solution)/shard_map/ppermute | solution.py:365
  24.0 47.2 %collective-permute-start.6 = (bf16[2048,512]{1,0:T(8,128)(2,1)}, bf16[2048,512]{1,0:T(8,128)(2,1)}, u32[]{:S(2)}, u32[]{:S(2)}) collective-permute-start(bf16[2048,512]{1,0:T(8,128)(2,1)} %pack_stores.2.s0), channel_id=1, source_target_pairs={{0,2},{1,3},{2,0},{3,1},{4,6},{5,7},{6,4},{7,5},{8,10},{9,11},{10,... | collective-permute-start | bytes 6291464 | tf_op jit(solution)/shard_map/ppermute | solution.py:365
  25.8 179.8 %reduce-scatter.3.cloned.1.call-start = ((), (), s32[]{:S(2)}) async-start(), calls=%async_computation.2 | async-start | bytes 2621440 | tf_op jit(solution)/shard_map/reduce_scatter | solution.py:426
  30.3 12.5 %collective-permute-start.7 = (bf16[256,512]{1,0:T(8,128)(2,1)S(1)}, bf16[256,512]{1,0:T(8,128)(2,1)S(1)}, u32[]{:S(2)}, u32[]{:S(2)}) collective-permute-start(bf16[256,512]{1,0:T(8,128)(2,1)S(1)} %copy-done.2), channel_id=1, source_target_pairs={{0,1},{1,0},{2,3},{3,2},{4,5},{5,4},{6,7},{7,6},{8,9},{9,8},{10,11... | collective-permute-start | bytes 786440 | tf_op jit(solution)/shard_map/ppermute | solution.py:365
  30.3 13.0 %collective-permute-start.9 = (bf16[256,512]{1,0:T(8,128)(2,1)S(1)}, bf16[256,512]{1,0:T(8,128)(2,1)S(1)}, u32[]{:S(2)}, u32[]{:S(2)}) collective-permute-start(bf16[256,512]{1,0:T(8,128)(2,1)S(1)} %copy-done.3), channel_id=1, source_target_pairs={{0,1},{1,0},{2,3},{3,2},{4,5},{5,4},{6,7},{7,6},{8,9},{9,8},{10,11... | collective-permute-start | bytes 786440 | tf_op jit(solution)/shard_map/ppermute | solution.py:365
  32.0 11.3 %collective-permute-start.10 = (bf16[256,512]{1,0:T(8,128)(2,1)S(1)}, bf16[256,512]{1,0:T(8,128)(2,1)S(1)}, u32[]{:S(2)}, u32[]{:S(2)}) collective-permute-start(bf16[256,512]{1,0:T(8,128)(2,1)S(1)} %collective-permute-done.4.v2), channel_id=1, source_target_pairs={{0,1},{1,0},{2,3},{3,2},{4,5},{5,4},{6,7},{7,6},{8,9},{9,8},{10,11... | collective-permute-start | bytes 786440 | tf_op jit(solution)/shard_map/ppermute | solution.py:365
  35.4 7.9 %collective-permute-start.8 = (bf16[256,512]{1,0:T(8,128)(2,1)S(1)}, bf16[256,512]{1,0:T(8,128)(2,1)S(1)}, u32[]{:S(2)}, u32[]{:S(2)}) collective-permute-start(bf16[256,512]{1,0:T(8,128)(2,1)S(1)} %collective-permute-done.3.k2), channel_id=1, source_target_pairs={{0,1},{1,0},{2,3},{3,2},{4,5},{5,4},{6,7},{7,6},{8,9},{9,8},{10,11... | collective-permute-start | bytes 786440 | tf_op jit(solution)/shard_map/ppermute | solution.py:365
  42.8 30.7 %collective-permute-start.5 = (bf16[2048,512]{1,0:T(8,128)(2,1)}, bf16[2048,512]{1,0:T(8,128)(2,1)}, u32[]{:S(2)}, u32[]{:S(2)}) collective-permute-start(bf16[2048,512]{1,0:T(8,128)(2,1)} %pack_stores.2.s0), channel_id=1, source_target_pairs={{0,1},{1,0},{2,3},{3,2},{4,5},{5,4},{6,7},{7,6},{8,9},{9,8},{10,11... | collective-permute-start | bytes 6291464 | tf_op jit(solution)/shard_map/ppermute | solution.py:365
  71.4 50.6 %collective-permute-start.16 = (bf16[2048,512]{1,0:T(8,128)(2,1)S(1)}, bf16[2048,512]{1,0:T(8,128)(2,1)}, u32[]{:S(2)}, u32[]{:S(2)}) collective-permute-start(bf16[2048,512]{1,0:T(8,128)(2,1)S(1)} %copy-done), channel_id=1, source_target_pairs={{0,2},{1,3},{2,0},{3,1},{4,6},{5,7},{6,4},{7,5},{8,10},{9,11},{10,... | collective-permute-start | bytes 6291464 | tf_op jit(solution)/shard_map/ppermute | solution.py:365
  93.5 10.1 %collective-permute-start.12 = (f32[2,4,8,256]{3,2,1,0:T(8,128)}, f32[2,4,8,256]{3,2,1,0:T(8,128)S(1)}, u32[]{:S(2)}, u32[]{:S(2)}) collective-permute-start(f32[2,4,8,256]{3,2,1,0:T(8,128)} %get-tuple-element.165.refs_0_), channel_id=1, source_target_pairs={{0,4},{1,5},{2,6},{3,7},{4,0},{5,1},{6,2},{7,3},{8,12},{9,13},{10,... | collective-permute-start | bytes 196616 | tf_op jit(solution)/shard_map/ppermute | solution.py:365
  94.9 12.4 %collective-permute-start.13 = (f32[2,4,8,256]{3,2,1,0:T(8,128)}, f32[2,4,8,256]{3,2,1,0:T(8,128)S(1)}, u32[]{:S(2)}, u32[]{:S(2)}) collective-permute-start(f32[2,4,8,256]{3,2,1,0:T(8,128)} %get-tuple-element.165.refs_0_), channel_id=1, source_target_pairs={{0,8},{1,9},{2,10},{3,11},{4,12},{5,13},{6,14},{7,15},{8,0},{9,1},... | collective-permute-start | bytes 196616 | tf_op jit(solution)/shard_map/ppermute | solution.py:365
  97.5 9.8 %collective-permute-start.14 = (f32[2,4,8,256]{3,2,1,0:T(8,128)}, f32[2,4,8,256]{3,2,1,0:T(8,128)S(1)}, u32[]{:S(2)}, u32[]{:S(2)}) collective-permute-start(f32[2,4,8,256]{3,2,1,0:T(8,128)} %get-tuple-element.165.refs_0_), channel_id=1, source_target_pairs={{0,12},{1,13},{2,14},{3,15},{4,8},{5,9},{6,10},{7,11},{8,4},{9,5},... | collective-permute-start | bytes 196616 | tf_op jit(solution)/shard_map/ppermute | solution.py:365
  114.3 91.3 %reduce-scatter.5.cloned.1.call-start = ((), (), s32[]{:S(2)}) async-start(), calls=%async_computation.3 | async-start | bytes 1310720 | tf_op jit(solution)/shard_map/reduce_scatter | solution.py:426
  114.5 15.3 %collective-permute-start.15 = (bf16[2048,512]{1,0:T(8,128)(2,1)S(1)}, bf16[2048,512]{1,0:T(8,128)(2,1)}, u32[]{:S(2)}, u32[]{:S(2)}) collective-permute-start(bf16[2048,512]{1,0:T(8,128)(2,1)S(1)} %copy-done), channel_id=1, source_target_pairs={{0,1},{1,0},{2,3},{3,2},{4,5},{5,4},{6,7},{7,6},{8,9},{9,8},{10,11... | collective-permute-start | bytes 6291464 | tf_op jit(solution)/shard_map/ppermute | solution.py:365
  122.0 7.9 %collective-permute-start.17 = (bf16[2048,512]{1,0:T(8,128)(2,1)}, bf16[2048,512]{1,0:T(8,128)(2,1)S(1)}, u32[]{:S(2)}, u32[]{:S(2)}) collective-permute-start(bf16[2048,512]{1,0:T(8,128)(2,1)} %collective-permute-done.16.s2), channel_id=1, source_target_pairs={{0,1},{1,0},{2,3},{3,2},{4,5},{5,4},{6,7},{7,6},{8,9},{9,8},{10,11... | collective-permute-start | bytes 6291464 | tf_op jit(solution)/shard_map/ppermute | solution.py:365
  141.7 15.4 %collective-permute-start.18 = (f32[1,4,8,256]{3,2,1,0:T(8,128)}, f32[1,4,8,256]{3,2,1,0:T(8,128)S(1)}, u32[]{:S(2)}, u32[]{:S(2)}) collective-permute-start(f32[1,4,8,256]{3,2,1,0:T(8,128)} %get-tuple-element.215.refs_0_), channel_id=1, source_target_pairs={{0,4},{1,5},{2,6},{3,7},{4,0},{5,1},{6,2},{7,3},{8,12},{9,13},{10,... | collective-permute-start | bytes 98312 | tf_op jit(solution)/shard_map/ppermute | solution.py:365
  141.7 15.4 %collective-permute-start.19 = (f32[1,4,8,256]{3,2,1,0:T(8,128)}, f32[1,4,8,256]{3,2,1,0:T(8,128)S(1)}, u32[]{:S(2)}, u32[]{:S(2)}) collective-permute-start(f32[1,4,8,256]{3,2,1,0:T(8,128)} %get-tuple-element.215.refs_0_), channel_id=1, source_target_pairs={{0,8},{1,9},{2,10},{3,11},{4,12},{5,13},{6,14},{7,15},{8,0},{9,1},... | collective-permute-start | bytes 98312 | tf_op jit(solution)/shard_map/ppermute | solution.py:365
  141.7 15.3 %collective-permute-start.20 = (f32[1,4,8,256]{3,2,1,0:T(8,128)}, f32[1,4,8,256]{3,2,1,0:T(8,128)S(1)}, u32[]{:S(2)}, u32[]{:S(2)}) collective-permute-start(f32[1,4,8,256]{3,2,1,0:T(8,128)} %get-tuple-element.215.refs_0_), channel_id=1, source_target_pairs={{0,12},{1,13},{2,14},{3,15},{4,8},{5,9},{6,10},{7,11},{8,4},{9,5},... | collective-permute-start | bytes 98312 | tf_op jit(solution)/shard_map/ppermute | solution.py:365
  176.0 22.1 %collective-permute-start.24 = (bf16[1,256,512]{2,1,0:T(8,128)(2,1)}, bf16[1,256,512]{2,1,0:T(8,128)(2,1)S(1)}, u32[]{:S(2)}, u32[]{:S(2)}) collective-permute-start(bf16[1,256,512]{2,1,0:T(8,128)(2,1)} %get-tuple-element.228), channel_id=1, source_target_pairs={{0,4},{1,5},{2,6},{3,7},{4,0},{5,1},{6,2},{7,3},{8,12},{9,13},{10,... | collective-permute-start | bytes 786440 | tf_op jit(solution)/shard_map/ppermute | solution.py:365
  176.2 21.9 %collective-permute-start.25 = (bf16[1,256,512]{2,1,0:T(8,128)(2,1)}, bf16[1,256,512]{2,1,0:T(8,128)(2,1)S(1)}, u32[]{:S(2)}, u32[]{:S(2)}) collective-permute-start(bf16[1,256,512]{2,1,0:T(8,128)(2,1)} %get-tuple-element.229), channel_id=1, source_target_pairs={{0,8},{1,9},{2,10},{3,11},{4,12},{5,13},{6,14},{7,15},{8,0},{9,1},... | collective-permute-start | bytes 786440 | tf_op jit(solution)/shard_map/ppermute | solution.py:365
  180.5 25.1 %collective-permute-start.26 = (bf16[1,256,512]{2,1,0:T(8,128)(2,1)}, bf16[1,256,512]{2,1,0:T(8,128)(2,1)S(1)}, u32[]{:S(2)}, u32[]{:S(2)}) collective-permute-start(bf16[1,256,512]{2,1,0:T(8,128)(2,1)} %get-tuple-element.230), channel_id=1, source_target_pairs={{0,12},{1,13},{2,14},{3,15},{4,8},{5,9},{6,10},{7,11},{8,4},{9,5},... | collective-permute-start | bytes 786440 | tf_op jit(solution)/shard_map/ppermute | solution.py:365
  (38 other events, 266.3 us)
Sparse Core Ops, SparseCore 0:
  8.9 48.6 all-gather.4
  59.2 49.8 all-gather.6
  114.4 45.9 reduce-scatter.2
  163.1 34.7 reduce-scatter.4

commit v5 on v4

--- a/solution.py
+++ b/solution.py
@@ -97,16 +97,21 @@
     lse_ref[0, 0, G:] = jnp.where(slot == 0, own_lse_ref[0, 0, :G], ctx_lse_ref[0, 0, :G])
 
 
-def scale_kernel(planes, heads, scattered, info, um_ref, own_ref, uc_ref, gate_ref, *refs):
+def scale_kernel(planes, heads, first, scattered, info, um_ref, own_ref, uc_ref, gate_ref, *refs):
     lse_refs, out_refs = refs[:planes], refs[planes:]
     slot = pl.program_id(0)
+    part_row = lax.broadcasted_iota(jnp.int32, (8, QBLK), 0)
     row = lax.broadcasted_iota(jnp.int32, (16, 2 * QW), 0) % 8
     spread = (row == lax.broadcasted_iota(jnp.int32, (16, 2 * QW), 1) // HD).astype(jnp.bfloat16)
     for h in range(heads):
         parts = [lse_refs[k][h, jnp.bitwise_xor(slot, k)] for k in range(planes)]
         top = functools.reduce(jnp.maximum, parts)
         total = functools.reduce(jnp.add, [jnp.exp2(p - top) for p in parts])
-        weight = jnp.exp2(parts[0] - top) / total * gate_ref[h]
+        weight = jnp.exp2(parts[0] - top) / total
+        for g in range(G):
+            gate = gate_ref[(first + h) * G + g]
+            weight = jnp.where(part_row == g, weight * gate, weight)
+            weight = jnp.where(part_row == G + g, weight * (1.0 - gate), weight)
         high = weight.astype(jnp.bfloat16)
         low = (weight - high.astype(jnp.float32)).astype(jnp.bfloat16)
         wide = lax.dot_general(
@@ -128,7 +133,7 @@
                     ref[h, :, cols] = term
 
 
-PARAMS = pltpu.CompilerParams(vmem_limit_bytes=56 * 1024 * 1024)
+PARAMS = pltpu.CompilerParams(vmem_limit_bytes=24 * 1024 * 1024)
 PACK_PARAMS = pltpu.CompilerParams(vmem_limit_bytes=60 * 1024 * 1024)
 SMALL = pl.CostEstimate(flops=1000, bytes_accessed=1000, transcendentals=0)
 
@@ -174,7 +179,7 @@
             out_specs=[per_head(QBLK, QW), per_head(8, QBLK)],
         ),
         out_shape=partial_shapes(count, planes - base),
-        compiler_params=PARAMS,
+        compiler_params=PACK_PARAMS,
         cost_estimate=SMALL,
         name="ctx_attend",
     )(info, q, *sources)
@@ -205,7 +210,7 @@
     )(info, q, *stores, own_lse, ctx_lse)
 
 
-def scale_call(info, um, own, uc, gate_rows, lses, first, chunk_first, scattered):
+def scale_call(info, um, own, uc, gate, lses, first, chunk_first, scattered):
     heads, planes = um.shape[:2]
     part = pl.BlockSpec((heads, 1, QBLK, QW), lambda j, info: (0, j, 0, 0))
     own_part = pl.BlockSpec((heads, 1, QBLK, QW), lambda j, info: (first // heads, 0, 0, 0))
@@ -218,18 +223,18 @@
         shapes = [(heads, QBLK, QW)] * planes
         out_specs = [whole(shape) for shape in shapes]
     return pl.pallas_call(
-        functools.partial(scale_kernel, planes, heads, scattered),
+        functools.partial(scale_kernel, planes, heads, first, scattered),
         grid_spec=pltpu.PrefetchScalarGridSpec(
             num_scalar_prefetch=1,
             grid=(planes,),
-            in_specs=[part, own_part, rest, whole((heads, 8, 1))] + [whole((heads, planes, 8, QBLK))] * planes,
+            in_specs=[part, own_part, rest, pl.BlockSpec(memory_space=pltpu.SMEM)] + [whole((heads, planes, 8, QBLK))] * planes,
             out_specs=out_specs,
         ),
         out_shape=[jax.ShapeDtypeStruct(shape, jnp.bfloat16) for shape in shapes],
         compiler_params=PARAMS,
         cost_estimate=SMALL,
         name="scale_mix",
-    )(info, um, own, uc, gate_rows, *lses)
+    )(info, um, own, uc, gate, *lses)
 
 
 def route_kernel(planes, local_count, *refs):
@@ -388,7 +393,6 @@
     diag = [None, None]
 
     gate = 1.0 / (1.0 + jnp.exp(-gate_logit))
-    gate_rows = jnp.concatenate([gate.reshape(KVH, G), 1.0 - gate.reshape(KVH, G)], axis=1)[:, :, None]
     spread = [lax.all_gather(part, "seq", axis=0, axis_index_groups=columns) for part in (q_first, q_second)]
 
     place = jnp.stack([plane, within] + [plane] * 6).astype(jnp.int32)
@@ -419,8 +423,7 @@
     def scale_step(first, um, uc, lses, scattered):
         n = place_of(first, CHUNKS)[0]
         um, uc, *lses = order.before(um, uc, *lses)
-        gates = gate_rows[first : first + um.shape[0]]
-        parts = scale_call(place, um, own_uc, uc, gates, lses, first, first, scattered)
+        parts = scale_call(place, um, own_uc, uc, gate, lses, first, first, scattered)
         order.done(parts[0])
         if scattered:
             return [lax.psum_scatter(parts[0], "seq", scatter_dimension=0, axis_index_groups=columns)]

time: 219 us -> 215 us (0.982)
  waiting for transfers between devices: 55.7 us -> 67.8 us
  Pallas kernels: 107 us -> 95.3 us
  local copies, waits for them, and re-layouts: 8.5 us -> 5 us
    ppermute x27, waiting for transfers between devices: 51.6 us -> 61 us  [xor(): return lax.ppermute(x, 'seq', [(i, i ^ bits) for i in range(devices)])]
    pallas_call x3, Pallas kernels: 17.3 us -> 11.9 us  [scale_call(): pl.pallas_call(functools.partial(scale_kernel, planes, heads, first, scat...]
    pallas_call x3, Pallas kernels: 38.4 us -> 34.7 us  [mem_call(): pl.pallas_call(functools.partial(mem_kernel, masked), grid_spec=pltpu.Pre...]
    unnamed x62 -> x56, local copies, waits for them, and re-layouts: 4.91 us -> 4.78 us
  transfers between devices with their start and end apart: 31 -> 31, of which waited for: 12 -> 16; matrix products, arithmetic and copies ran while one was open for 2% -> 0% of each run, Pallas kernels for 47% -> 43%
where the time goes in v5:
time: 215 us; the launch traced here: 212 us
  Pallas kernels  95.3 us (44%)
  waiting for transfers between devices  67.8 us (32%)
  starting transfers between devices  30 us (14%)
  between operations  13.4 us (6%)
  local copies, waits for them, and re-layouts  5 us (2%)
    ppermute x27, waiting for transfers between devices, xor(): return lax.ppermute(x, 'seq', [(i, i ^ bits) for i in range(devices)])  61 us
    pallas_call x4, Pallas kernels, ctx_call(): pl.pallas_call(functools.partial(ctx_kernel, base), grid_spec=pltpu.Prefe...  36.6 us
    pallas_call x3, Pallas kernels, mem_call(): pl.pallas_call(functools.partial(mem_kernel, masked), grid_spec=pltpu.Pre...  34.7 us
    ppermute x27, starting transfers between devices, xor(): return lax.ppermute(x, 'seq', [(i, i ^ bits) for i in range(devices)])  29.7 us
    pallas_call x3, Pallas kernels, scale_call(): pl.pallas_call(functools.partial(scale_kernel, planes, heads, first, scat...  11.9 us
    pallas_call x2, Pallas kernels, pack_stores(): pl.pallas_call(pack_stores_kernel, grid=(steps,), in_specs=[pl.BlockSpec(...  7.84 us
    all_gather x2, waiting for transfers between devices, on_device(): lax.all_gather(part, 'seq', axis=0, axis_index_groups=columns)  6.2 us
    unnamed x56, local copies, waits for them, and re-layouts  4.78 us
  transfers between devices with their start and end apart: 31, of which 16 were waited for; matrix products, arithmetic and copies ran while one was open for 0% of the time, Pallas kernels for 43%

profile of v5, /device:TPU:0, one launch (start us, length us, event | category | flops | bytes accessed | tf_op | source)
XLA Modules:
  0.0 211.6 jit_solution(10343148584542785245)
XLA Ops:
  8.8 3.0 %collective-permute-start.3 = (bf16[256,512]{1,0:T(8,128)(2,1)}, bf16[256,512]{1,0:T(8,128)(2,1)S(1)}, u32[]{:S(2)}, u32[]{:S(2)}) collective-permute-start(bf16[256,512]{1,0:T(8,128)(2,1)} %k0.3), channel_id=1, source_target_pairs={{0,2},{1,3},{2,0},{3,1},{4,6},{5,7},{6,4},{7,5},{8,10},{9,11},{10,... | collective-permute-start | bytes 786440 | tf_op jit(solution)/shard_map/ppermute | solution.py:370
  12.0 4.0 %pack_stores.2.s0 = bf16[2048,512]{1,0:T(8,128)(2,1)} custom-call(bf16[2048,512]{1,0:T(8,128)(2,1)} %bitcast.26, bf16[2048,512]{1,0:T(8,128)(2,1)} %bitcast.28), custom_call_target="tpu_custom_call" | custom-call | flops 1000 | bytes 1000 | tf_op jit(solution)/shard_map/pack_stores/pallas_call | solution.py:307
  15.9 3.3 %collective-permute-done.3.k2 = bf16[256,512]{1,0:T(8,128)(2,1)S(1)} collective-permute-done((bf16[256,512]{1,0:T(8,128)(2,1)}, bf16[256,512]{1,0:T(8,128)(2,1)S(1)}, u32[]{:S(2)}, u32[]{:S(2)}) %collective-permute-start.3) | collective-permute-done | bytes 262176 | tf_op jit(solution)/shard_map/ppermute | solution.py:370
  19.2 4.8 %collective-permute-done.4.v2 = bf16[256,512]{1,0:T(8,128)(2,1)S(1)} collective-permute-done((bf16[256,512]{1,0:T(8,128)(2,1)}, bf16[256,512]{1,0:T(8,128)(2,1)S(1)}, u32[]{:S(2)}, u32[]{:S(2)}) %collective-permute-start.4) | collective-permute-done | bytes 262176 | tf_op jit(solution)/shard_map/ppermute | solution.py:370
  32.0 3.4 %collective-permute-done.2.refs_3_ = s32[1,32]{1,0:T(1,128)S(1)} collective-permute-done((s32[1,32]{1,0:T(1,128)S(1)}, s32[1,32]{1,0:T(1,128)S(1)}, u32[]{:S(2)}, u32[]{:S(2)}) %collective-permute-start.2) | collective-permute-done | bytes 160 | tf_op jit(solution)/shard_map/ppermute | solution.py:370
  35.7 3.9 %pack_stores.3.s0 = bf16[2048,512]{1,0:T(8,128)(2,1)} custom-call(bf16[2048,512]{1,0:T(8,128)(2,1)} %bitcast.27, bf16[2048,512]{1,0:T(8,128)(2,1)} %bitcast.29), custom_call_target="tpu_custom_call" | custom-call | flops 1000 | bytes 1000 | tf_op jit(solution)/shard_map/pack_stores/pallas_call | solution.py:307
  42.0 9.4 %ctx_attend.4 = (bf16[4,1,256,512]{3,2,1,0:T(8,128)(2,1)}, f32[4,1,8,256]{3,2,1,0:T(8,128)}) custom-call(s32[1,8]{1,0:T(1,128)} %bitcast.18, bf16[256,2048]{1,0:T(8,128)(2,1)} %q_ref, bf16[256,512]{1,0:T(8,128)(2,1)} %k0.3, bf16[256,512]{1,0:T(8,128)(2,1)} %copy-done.22, bf16[256,512]{1,0:T(8,128)(2,1)} %copy-done.20, bf16[256,512]{1,0:T(8,128)(2,1)} %copy-done.25, ...), custom_call_target="tpu_custom_call" | custom-call | flops 1000 | bytes 1000 | tf_op jit(solution)/shard_map/ctx_attend/pallas_call | solution.py:173
  51.5 6.2 %all-gather.5.cloned.1.call-done = bf16[1024,1024]{1,0:T(8,128)(2,1)} async-done(((bf16[256,1024]{1,0:T(8,128)(2,1)}), bf16[1024,1024]{1,0:T(8,128)(2,1)}) %all-gather.5.cloned.1.call-update) | async-done | bytes 2097168 | tf_op jit(solution)/shard_map/all_gather | solution.py:396
  57.6 12.4 %ctx_attend.5 = (bf16[2,3,256,512]{3,2,1,0:T(8,128)(2,1)}, f32[2,3,8,256]{3,2,1,0:T(8,128)}) custom-call(s32[1,8]{1,0:T(1,128)} %bitcast.19, bf16[4,256,1024]{2,1,0:T(8,128)(2,1)} %bitcast.14, bf16[256,512]{1,0:T(8,128)(2,1)} %k0.3, bf16[256,512]{1,0:T(8,128)(2,1)} %copy-done.22, bf16[256,512]{1,0:T(8,128)(2,1)} %copy-done.20, bf16[256,512]{1,0:T(8,128)(2,1)} %copy-done.25, ...), custom_call_target="tpu_custom_call" | custom-call | flops 1000 | bytes 1000 | tf_op jit(solution)/shard_map/ctx_attend/pallas_call | solution.py:173
  76.4 15.9 %mem_attend.3 = (bf16[2,4,256,512]{3,2,1,0:T(8,128)(2,1)S(1)}, f32[2,4,8,256]{3,2,1,0:T(8,128)S(1)}) custom-call(s32[5,8]{1,0:T(8,128)S(1)} %pad_add_fusion.info, bf16[4,256,1024]{2,1,0:T(8,128)(2,1)S(1)} %bitcast.15, bf16[2048,512]{1,0:T(8,128)(2,1)} %pack_stores.2.s0, bf16[2048,512]{1,0:T(8,128)(2,1)} %collective-permute-done.5.s1, ...), custom_call_target="tpu_custom_call" | custom-call | flops 1000 | bytes 1000 | tf_op jit(solution)/shard_map/mem_attend/pallas_call | solution.py:192
  96.8 4.6 %collective-permute-done.12.refs_1_ = f32[2,4,8,256]{3,2,1,0:T(8,128)S(1)} collective-permute-done((f32[2,4,8,256]{3,2,1,0:T(8,128)S(1)}, f32[2,4,8,256]{3,2,1,0:T(8,128)S(1)}, u32[]{:S(2)}, u32[]{:S(2)}) %collective-permute-start.12) | collective-permute-done | bytes 65568 | tf_op jit(solution)/shard_map/ppermute | solution.py:370
  101.4 3.9 %collective-permute-done.13.refs_2_ = f32[2,4,8,256]{3,2,1,0:T(8,128)S(1)} collective-permute-done((f32[2,4,8,256]{3,2,1,0:T(8,128)S(1)}, f32[2,4,8,256]{3,2,1,0:T(8,128)S(1)}, u32[]{:S(2)}, u32[]{:S(2)}) %collective-permute-start.13) | collective-permute-done | bytes 65568 | tf_op jit(solution)/shard_map/ppermute | solution.py:370
  105.9 4.7 %scale_mix.3 = bf16[4,2,256,512]{3,2,1,0:T(8,128)(2,1)} custom-call(s32[1,8]{1,0:T(1,128)S(1)} %bitcast.23, bf16[2,4,256,512]{3,2,1,0:T(8,128)(2,1)S(1)} %get-tuple-element.162.um_ref, bf16[4,1,256,512]{3,2,1,0:T(8,128)(2,1)S(1)} %copy-done.1, bf16[2,3,256,512]{3,2,1,0:T(8,128)(2,1)S(1)} %copy-done.3, f32[16]{0:T(128)S(1)} %add_divide_fusion.gate_ref, ...), custom_call_target="tpu_custom_call" | custom-call | flops 1000 | bytes 1000 | tf_op jit(solution)/shard_map/scale_mix/pallas_call | solution.py:225
  111.0 7.3 %ctx_attend.6 = (bf16[1,3,256,512]{3,2,1,0:T(8,128)(2,1)}, f32[1,3,8,256]{3,2,1,0:T(8,128)}) custom-call(s32[1,8]{1,0:T(1,128)} %bitcast.20, bf16[4,256,1024]{2,1,0:T(8,128)(2,1)} %bitcast.10, bf16[256,512]{1,0:T(8,128)(2,1)} %k0.3, bf16[256,512]{1,0:T(8,128)(2,1)} %copy-done.22, bf16[256,512]{1,0:T(8,128)(2,1)} %copy-done.20, bf16[256,512]{1,0:T(8,128)(2,1)} %copy-done.25, ...), custom_call_target="tpu_custom_call" | custom-call | flops 1000 | bytes 1000 | tf_op jit(solution)/shard_map/ctx_attend/pallas_call | solution.py:173
  119.6 7.5 %ctx_attend.7 = (bf16[1,3,256,512]{3,2,1,0:T(8,128)(2,1)}, f32[1,3,8,256]{3,2,1,0:T(8,128)}) custom-call(s32[1,8]{1,0:T(1,128)} %bitcast.21, bf16[4,256,1024]{2,1,0:T(8,128)(2,1)} %bitcast.11, bf16[256,512]{1,0:T(8,128)(2,1)} %k0.3, bf16[256,512]{1,0:T(8,128)(2,1)} %copy-done.22, bf16[256,512]{1,0:T(8,128)(2,1)} %copy-done.20, bf16[256,512]{1,0:T(8,128)(2,1)} %copy-done.25, ...), custom_call_target="tpu_custom_call" | custom-call | flops 1000 | bytes 1000 | tf_op jit(solution)/shard_map/ctx_attend/pallas_call | solution.py:173
  127.1 9.4 %mem_attend.4 = (bf16[1,4,256,512]{3,2,1,0:T(8,128)(2,1)S(1)}, f32[1,4,8,256]{3,2,1,0:T(8,128)S(1)}) custom-call(s32[5,8]{1,0:T(8,128)S(1)} %pad_add_fusion.info, bf16[4,256,1024]{2,1,0:T(8,128)(2,1)S(1)} %bitcast.12, bf16[2048,512]{1,0:T(8,128)(2,1)} %pack_stores.3.s0, bf16[2048,512]{1,0:T(8,128)(2,1)} %collective-permute-done.15.s1, ...), custom_call_target="tpu_custom_call" | custom-call | flops 1000 | bytes 1000 | tf_op jit(solution)/shard_map/mem_attend/pallas_call | solution.py:192
  137.7 3.3 %collective-permute-start.20 = (f32[1,4,8,256]{3,2,1,0:T(8,128)S(1)}, f32[1,4,8,256]{3,2,1,0:T(8,128)S(1)}, u32[]{:S(2)}, u32[]{:S(2)}) collective-permute-start(f32[1,4,8,256]{3,2,1,0:T(8,128)S(1)} %get-tuple-element.215.refs_0_), channel_id=1, source_target_pairs={{0,12},{1,13},{2,14},{3,15},{4,8},{5,9},{6,10},{7,11},{8,4},{9,5},... | collective-permute-start | bytes 98312 | tf_op jit(solution)/shard_map/ppermute | solution.py:370
  141.0 9.4 %mem_attend.5 = (bf16[1,4,256,512]{3,2,1,0:T(8,128)(2,1)S(1)}, f32[1,4,8,256]{3,2,1,0:T(8,128)S(1)}) custom-call(s32[5,8]{1,0:T(8,128)S(1)} %pad_add_fusion.info, bf16[4,256,1024]{2,1,0:T(8,128)(2,1)S(1)} %bitcast.13, bf16[2048,512]{1,0:T(8,128)(2,1)} %pack_stores.3.s0, bf16[2048,512]{1,0:T(8,128)(2,1)} %collective-permute-done.15.s1, ...), custom_call_target="tpu_custom_call" | custom-call | flops 1000 | bytes 1000 | tf_op jit(solution)/shard_map/mem_attend/pallas_call | solution.py:192
  151.5 3.8 %scale_mix.4 = bf16[4,1,256,512]{3,2,1,0:T(8,128)(2,1)} custom-call(s32[1,8]{1,0:T(1,128)S(1)} %bitcast.24, bf16[1,4,256,512]{3,2,1,0:T(8,128)(2,1)S(1)} %get-tuple-element.213.um_ref, bf16[4,1,256,512]{3,2,1,0:T(8,128)(2,1)S(1)} %copy-done.1, bf16[1,3,256,512]{3,2,1,0:T(8,128)(2,1)S(1)} %copy-done.6, f32[16]{0:T(128)S(1)} %add_divide_fusion.gate_ref, ...), custom_call_target="tpu_custom_call" | custom-call | flops 1000 | bytes 1000 | tf_op jit(solution)/shard_map/scale_mix/pallas_call | solution.py:225
  156.5 3.3 %collective-permute-start.23 = (f32[1,4,8,256]{3,2,1,0:T(8,128)S(1)}, f32[1,4,8,256]{3,2,1,0:T(8,128)S(1)}, u32[]{:S(2)}, u32[]{:S(2)}) collective-permute-start(f32[1,4,8,256]{3,2,1,0:T(8,128)S(1)} %get-tuple-element.223.refs_0_), channel_id=1, source_target_pairs={{0,12},{1,13},{2,14},{3,15},{4,8},{5,9},{6,10},{7,11},{8,4},{9,5},... | collective-permute-start | bytes 98312 | tf_op jit(solution)/shard_map/ppermute | solution.py:370
  162.2 3.3 %scale_mix.5 = (bf16[1,256,512]{2,1,0:T(8,128)(2,1)S(1)}, bf16[1,256,512]{2,1,0:T(8,128)(2,1)S(1)}, bf16[1,256,512]{2,1,0:T(8,128)(2,1)S(1)}, bf16[1,256,512]{2,1,0:T(8,128)(2,1)S(1)}) custom-call(s32[1,8]{1,0:T(1,128)S(1)} %bitcast.25, bf16[1,4,256,512]{3,2,1,0:T(8,128)(2,1)S(1)} %copy-done.5, bf16[4,1,256,512]{3,2,1,0:T(8,128)(2,1)S(1)} %copy-done.1, ...), custom_call_target="tpu_custom_call" | custom-call | flops 1000 | bytes 1000 | tf_op jit(solution)/shard_map/scale_mix/pallas_call | solution.py:225
  165.7 3.8 %collective-permute-start.25 = (bf16[1,256,512]{2,1,0:T(8,128)(2,1)S(1)}, bf16[1,256,512]{2,1,0:T(8,128)(2,1)S(1)}, u32[]{:S(2)}, u32[]{:S(2)}) collective-permute-start(bf16[1,256,512]{2,1,0:T(8,128)(2,1)S(1)} %get-tuple-element.229), channel_id=1, source_target_pairs={{0,8},{1,9},{2,10},{3,11},{4,12},{5,13},{6,14},{7,15},{8,0},{9,1},... | collective-permute-start | bytes 786440 | tf_op jit(solution)/shard_map/ppermute | solution.py:370
  170.0 17.9 %collective-permute-done.24.refs_3_ = bf16[1,256,512]{2,1,0:T(8,128)(2,1)S(1)} collective-permute-done((bf16[1,256,512]{2,1,0:T(8,128)(2,1)S(1)}, bf16[1,256,512]{2,1,0:T(8,128)(2,1)S(1)}, u32[]{:S(2)}, u32[]{:S(2)}) %collective-permute-start.24) | collective-permute-done | bytes 262176 | tf_op jit(solution)/shard_map/ppermute | solution.py:370
  188.0 13.4 %collective-permute-done.25.refs_4_ = bf16[1,256,512]{2,1,0:T(8,128)(2,1)S(1)} collective-permute-done((bf16[1,256,512]{2,1,0:T(8,128)(2,1)S(1)}, bf16[1,256,512]{2,1,0:T(8,128)(2,1)S(1)}, u32[]{:S(2)}, u32[]{:S(2)}) %collective-permute-start.25) | collective-permute-done | bytes 262176 | tf_op jit(solution)/shard_map/ppermute | solution.py:370
  (117 shorter events, 36.3 us)
Async XLA Ops:
  6.5 51.1 %all-gather.5.cloned.1.call-start = ((), (), s32[]{:S(2)}) async-start(), calls=%async_computation.4 | async-start | bytes 2621440 | tf_op jit(solution)/shard_map/all_gather | solution.py:396
  8.8 102.2 %all-gather.7.cloned.1.call-start = ((), (), s32[]{:S(2)}) async-start(), calls=%async_computation.5 | async-start | bytes 2621440 | tf_op jit(solution)/shard_map/all_gather | solution.py:396
  8.8 10.4 %collective-permute-start.3 = (bf16[256,512]{1,0:T(8,128)(2,1)}, bf16[256,512]{1,0:T(8,128)(2,1)S(1)}, u32[]{:S(2)}, u32[]{:S(2)}) collective-permute-start(bf16[256,512]{1,0:T(8,128)(2,1)} %k0.3), channel_id=1, source_target_pairs={{0,2},{1,3},{2,0},{3,1},{4,6},{5,7},{6,4},{7,5},{8,10},{9,11},{10,... | collective-permute-start | bytes 786440 | tf_op jit(solution)/shard_map/ppermute | solution.py:370
  11.9 12.1 %collective-permute-start.4 = (bf16[256,512]{1,0:T(8,128)(2,1)}, bf16[256,512]{1,0:T(8,128)(2,1)S(1)}, u32[]{:S(2)}, u32[]{:S(2)}) collective-permute-start(bf16[256,512]{1,0:T(8,128)(2,1)} %v0.3), channel_id=1, source_target_pairs={{0,2},{1,3},{2,0},{3,1},{4,6},{5,7},{6,4},{7,5},{8,10},{9,11},{10,... | collective-permute-start | bytes 786440 | tf_op jit(solution)/shard_map/ppermute | solution.py:370
  24.0 47.2 %collective-permute-start.6 = (bf16[2048,512]{1,0:T(8,128)(2,1)}, bf16[2048,512]{1,0:T(8,128)(2,1)}, u32[]{:S(2)}, u32[]{:S(2)}) collective-permute-start(bf16[2048,512]{1,0:T(8,128)(2,1)} %pack_stores.2.s0), channel_id=1, source_target_pairs={{0,2},{1,3},{2,0},{3,1},{4,6},{5,7},{6,4},{7,5},{8,10},{9,11},{10,... | collective-permute-start | bytes 6291464 | tf_op jit(solution)/shard_map/ppermute | solution.py:370
  25.8 175.6 %reduce-scatter.3.cloned.1.call-start = ((), (), s32[]{:S(2)}) async-start(), calls=%async_computation.2 | async-start | bytes 2621440 | tf_op jit(solution)/shard_map/reduce_scatter | solution.py:429
  30.3 10.2 %collective-permute-start.7 = (bf16[256,512]{1,0:T(8,128)(2,1)S(1)}, bf16[256,512]{1,0:T(8,128)(2,1)S(1)}, u32[]{:S(2)}, u32[]{:S(2)}) collective-permute-start(bf16[256,512]{1,0:T(8,128)(2,1)S(1)} %copy-done.18), channel_id=1, source_target_pairs={{0,1},{1,0},{2,3},{3,2},{4,5},{5,4},{6,7},{7,6},{8,9},{9,8},{10,11... | collective-permute-start | bytes 786440 | tf_op jit(solution)/shard_map/ppermute | solution.py:370
  30.3 10.8 %collective-permute-start.9 = (bf16[256,512]{1,0:T(8,128)(2,1)S(1)}, bf16[256,512]{1,0:T(8,128)(2,1)S(1)}, u32[]{:S(2)}, u32[]{:S(2)}) collective-permute-start(bf16[256,512]{1,0:T(8,128)(2,1)S(1)} %copy-done.19), channel_id=1, source_target_pairs={{0,1},{1,0},{2,3},{3,2},{4,5},{5,4},{6,7},{7,6},{8,9},{9,8},{10,11... | collective-permute-start | bytes 786440 | tf_op jit(solution)/shard_map/ppermute | solution.py:370
  32.0 9.1 %collective-permute-start.10 = (bf16[256,512]{1,0:T(8,128)(2,1)S(1)}, bf16[256,512]{1,0:T(8,128)(2,1)S(1)}, u32[]{:S(2)}, u32[]{:S(2)}) collective-permute-start(bf16[256,512]{1,0:T(8,128)(2,1)S(1)} %collective-permute-done.4.v2), channel_id=1, source_target_pairs={{0,1},{1,0},{2,3},{3,2},{4,5},{5,4},{6,7},{7,6},{8,9},{9,8},{10,11... | collective-permute-start | bytes 786440 | tf_op jit(solution)/shard_map/ppermute | solution.py:370
  35.4 5.7 %collective-permute-start.8 = (bf16[256,512]{1,0:T(8,128)(2,1)S(1)}, bf16[256,512]{1,0:T(8,128)(2,1)S(1)}, u32[]{:S(2)}, u32[]{:S(2)}) collective-permute-start(bf16[256,512]{1,0:T(8,128)(2,1)S(1)} %collective-permute-done.3.k2), channel_id=1, source_target_pairs={{0,1},{1,0},{2,3},{3,2},{4,5},{5,4},{6,7},{7,6},{8,9},{9,8},{10,11... | collective-permute-start | bytes 786440 | tf_op jit(solution)/shard_map/ppermute | solution.py:370
  40.6 32.2 %collective-permute-start.5 = (bf16[2048,512]{1,0:T(8,128)(2,1)}, bf16[2048,512]{1,0:T(8,128)(2,1)}, u32[]{:S(2)}, u32[]{:S(2)}) collective-permute-start(bf16[2048,512]{1,0:T(8,128)(2,1)} %pack_stores.2.s0), channel_id=1, source_target_pairs={{0,1},{1,0},{2,3},{3,2},{4,5},{5,4},{6,7},{7,6},{8,9},{9,8},{10,11... | collective-permute-start | bytes 6291464 | tf_op jit(solution)/shard_map/ppermute | solution.py:370
  71.3 48.4 %collective-permute-start.16 = (bf16[2048,512]{1,0:T(8,128)(2,1)}, bf16[2048,512]{1,0:T(8,128)(2,1)}, u32[]{:S(2)}, u32[]{:S(2)}) collective-permute-start(bf16[2048,512]{1,0:T(8,128)(2,1)} %pack_stores.3.s0), channel_id=1, source_target_pairs={{0,2},{1,3},{2,0},{3,1},{4,6},{5,7},{6,4},{7,5},{8,10},{9,11},{10,... | collective-permute-start | bytes 6291464 | tf_op jit(solution)/shard_map/ppermute | solution.py:370
  92.3 9.1 %collective-permute-start.12 = (f32[2,4,8,256]{3,2,1,0:T(8,128)S(1)}, f32[2,4,8,256]{3,2,1,0:T(8,128)S(1)}, u32[]{:S(2)}, u32[]{:S(2)}) collective-permute-start(f32[2,4,8,256]{3,2,1,0:T(8,128)S(1)} %get-tuple-element.165.refs_0_), channel_id=1, source_target_pairs={{0,4},{1,5},{2,6},{3,7},{4,0},{5,1},{6,2},{7,3},{8,12},{9,13},{10,... | collective-permute-start | bytes 196616 | tf_op jit(solution)/shard_map/ppermute | solution.py:370
  93.9 11.4 %collective-permute-start.13 = (f32[2,4,8,256]{3,2,1,0:T(8,128)S(1)}, f32[2,4,8,256]{3,2,1,0:T(8,128)S(1)}, u32[]{:S(2)}, u32[]{:S(2)}) collective-permute-start(f32[2,4,8,256]{3,2,1,0:T(8,128)S(1)} %get-tuple-element.165.refs_0_), channel_id=1, source_target_pairs={{0,8},{1,9},{2,10},{3,11},{4,12},{5,13},{6,14},{7,15},{8,0},{9,1},... | collective-permute-start | bytes 196616 | tf_op jit(solution)/shard_map/ppermute | solution.py:370
  96.4 9.5 %collective-permute-start.14 = (f32[2,4,8,256]{3,2,1,0:T(8,128)S(1)}, f32[2,4,8,256]{3,2,1,0:T(8,128)S(1)}, u32[]{:S(2)}, u32[]{:S(2)}) collective-permute-start(f32[2,4,8,256]{3,2,1,0:T(8,128)S(1)} %get-tuple-element.165.refs_0_), channel_id=1, source_target_pairs={{0,12},{1,13},{2,14},{3,15},{4,8},{5,9},{6,10},{7,11},{8,4},{9,5},... | collective-permute-start | bytes 196616 | tf_op jit(solution)/shard_map/ppermute | solution.py:370
  110.6 91.2 %reduce-scatter.5.cloned.1.call-start = ((), (), s32[]{:S(2)}) async-start(), calls=%async_computation.3 | async-start | bytes 1310720 | tf_op jit(solution)/shard_map/reduce_scatter | solution.py:429
  110.9 16.2 %collective-permute-start.15 = (bf16[2048,512]{1,0:T(8,128)(2,1)}, bf16[2048,512]{1,0:T(8,128)(2,1)}, u32[]{:S(2)}, u32[]{:S(2)}) collective-permute-start(bf16[2048,512]{1,0:T(8,128)(2,1)} %pack_stores.3.s0), channel_id=1, source_target_pairs={{0,1},{1,0},{2,3},{3,2},{4,5},{5,4},{6,7},{7,6},{8,9},{9,8},{10,11... | collective-permute-start | bytes 6291464 | tf_op jit(solution)/shard_map/ppermute | solution.py:370
  119.6 7.5 %collective-permute-start.17 = (bf16[2048,512]{1,0:T(8,128)(2,1)}, bf16[2048,512]{1,0:T(8,128)(2,1)}, u32[]{:S(2)}, u32[]{:S(2)}) collective-permute-start(bf16[2048,512]{1,0:T(8,128)(2,1)} %collective-permute-done.16.s2), channel_id=1, source_target_pairs={{0,1},{1,0},{2,3},{3,2},{4,5},{5,4},{6,7},{7,6},{8,9},{9,8},{10,11... | collective-permute-start | bytes 6291464 | tf_op jit(solution)/shard_map/ppermute | solution.py:370
  136.5 14.9 %collective-permute-start.18 = (f32[1,4,8,256]{3,2,1,0:T(8,128)S(1)}, f32[1,4,8,256]{3,2,1,0:T(8,128)S(1)}, u32[]{:S(2)}, u32[]{:S(2)}) collective-permute-start(f32[1,4,8,256]{3,2,1,0:T(8,128)S(1)} %get-tuple-element.215.refs_0_), channel_id=1, source_target_pairs={{0,4},{1,5},{2,6},{3,7},{4,0},{5,1},{6,2},{7,3},{8,12},{9,13},{10,... | collective-permute-start | bytes 98312 | tf_op jit(solution)/shard_map/ppermute | solution.py:370
  136.7 14.8 %collective-permute-start.19 = (f32[1,4,8,256]{3,2,1,0:T(8,128)S(1)}, f32[1,4,8,256]{3,2,1,0:T(8,128)S(1)}, u32[]{:S(2)}, u32[]{:S(2)}) collective-permute-start(f32[1,4,8,256]{3,2,1,0:T(8,128)S(1)} %get-tuple-element.215.refs_0_), channel_id=1, source_target_pairs={{0,8},{1,9},{2,10},{3,11},{4,12},{5,13},{6,14},{7,15},{8,0},{9,1},... | collective-permute-start | bytes 98312 | tf_op jit(solution)/shard_map/ppermute | solution.py:370
  137.7 13.7 %collective-permute-start.20 = (f32[1,4,8,256]{3,2,1,0:T(8,128)S(1)}, f32[1,4,8,256]{3,2,1,0:T(8,128)S(1)}, u32[]{:S(2)}, u32[]{:S(2)}) collective-permute-start(f32[1,4,8,256]{3,2,1,0:T(8,128)S(1)} %get-tuple-element.215.refs_0_), channel_id=1, source_target_pairs={{0,12},{1,13},{2,14},{3,15},{4,8},{5,9},{6,10},{7,11},{8,4},{9,5},... | collective-permute-start | bytes 98312 | tf_op jit(solution)/shard_map/ppermute | solution.py:370
  165.6 22.4 %collective-permute-start.24 = (bf16[1,256,512]{2,1,0:T(8,128)(2,1)S(1)}, bf16[1,256,512]{2,1,0:T(8,128)(2,1)S(1)}, u32[]{:S(2)}, u32[]{:S(2)}) collective-permute-start(bf16[1,256,512]{2,1,0:T(8,128)(2,1)S(1)} %get-tuple-element.228), channel_id=1, source_target_pairs={{0,4},{1,5},{2,6},{3,7},{4,0},{5,1},{6,2},{7,3},{8,12},{9,13},{10,... | collective-permute-start | bytes 786440 | tf_op jit(solution)/shard_map/ppermute | solution.py:370
  165.7 35.7 %collective-permute-start.25 = (bf16[1,256,512]{2,1,0:T(8,128)(2,1)S(1)}, bf16[1,256,512]{2,1,0:T(8,128)(2,1)S(1)}, u32[]{:S(2)}, u32[]{:S(2)}) collective-permute-start(bf16[1,256,512]{2,1,0:T(8,128)(2,1)S(1)} %get-tuple-element.229), channel_id=1, source_target_pairs={{0,8},{1,9},{2,10},{3,11},{4,12},{5,13},{6,14},{7,15},{8,0},{9,1},... | collective-permute-start | bytes 786440 | tf_op jit(solution)/shard_map/ppermute | solution.py:370
  169.5 31.9 %collective-permute-start.26 = (bf16[1,256,512]{2,1,0:T(8,128)(2,1)S(1)}, bf16[1,256,512]{2,1,0:T(8,128)(2,1)S(1)}, u32[]{:S(2)}, u32[]{:S(2)}) collective-permute-start(bf16[1,256,512]{2,1,0:T(8,128)(2,1)S(1)} %get-tuple-element.230), channel_id=1, source_target_pairs={{0,12},{1,13},{2,14},{3,15},{4,8},{5,9},{6,10},{7,11},{8,4},{9,5},... | collective-permute-start | bytes 786440 | tf_op jit(solution)/shard_map/ppermute | solution.py:370
  (35 other events, 376.5 us)
Sparse Core Ops, SparseCore 0:
  8.9 48.6 all-gather.4
  59.2 50.2 all-gather.6
  111.8 46.3 reduce-scatter.2
  160.4 41.3 reduce-scatter.4

commit v6 on v5

--- a/solution.py
+++ b/solution.py
@@ -275,19 +275,18 @@
     )(*ids, block_slot[:, None], place)
 
 
-def pack_queries_kernel(q, *outs):
-    for out, heads in zip(outs, CHUNKS, strict=True):
-        out[...] = q[:, heads[0] * QW : (heads[-1] + 1) * QW]
-
-
-def pack_queries(q):
-    shapes = [(QBLK, len(heads) * QW) for heads in CHUNKS]
+def pack_queries_kernel(q, out):
+    out[...] = q[...]
+
+
+def pack_queries(q, n):
+    shape = (q.shape[0], len(CHUNKS[n]) * QW)
     return pl.pallas_call(
         pack_queries_kernel,
         grid=(1,),
-        in_specs=[whole(q.shape)],
-        out_specs=[whole(shape) for shape in shapes],
-        out_shape=[jax.ShapeDtypeStruct(shape, jnp.bfloat16) for shape in shapes],
+        in_specs=[pl.BlockSpec(shape, lambda i: (0, n))],
+        out_specs=whole(shape),
+        out_shape=jax.ShapeDtypeStruct(shape, jnp.bfloat16),
         compiler_params=PACK_PARAMS,
         cost_estimate=SMALL,
         name="pack_queries",
@@ -329,18 +328,25 @@
         head += heads
 
 
-def finish_call(groups):
+def finish_call(groups, half, base=None):
     flat = [part for parts in groups for part in parts]
-    return pl.pallas_call(
-        functools.partial(finish_kernel, [(len(parts), parts[0].shape[0]) for parts in groups]),
+    counts = [(len(parts), parts[0].shape[0]) for parts in groups]
+    given = [] if base is None else [base]
+
+    def body(*refs):
+        finish_kernel(counts, *refs[len(given) :])
+
+    return pl.pallas_call(
+        body,
         grid=(1,),
-        in_specs=[whole(part.shape) for part in flat],
-        out_specs=whole((QBLK, KVH * QW)),
+        in_specs=[pl.BlockSpec(memory_space=pl.ANY)] * len(given) + [whole(part.shape) for part in flat],
+        out_specs=pl.BlockSpec((QBLK, KVH // 2 * QW), lambda i: (0, half)),
         out_shape=jax.ShapeDtypeStruct((QBLK, KVH * QW), jnp.bfloat16),
-        compiler_params=PARAMS,
+        input_output_aliases={0: 0} if given else {},
+        compiler_params=PACK_PARAMS,
         cost_estimate=SMALL,
         name="finish_heads",
-    )(*flat)
+    )(*given, *flat)
 
 
 class Order:
@@ -372,6 +378,11 @@
     def all_planes(x):
         return [x] + [xor(x, k * WITHIN) for k in range(1, planes)]
 
+    def between(x, plane_pairs):
+        return lax.ppermute(
+            x, "seq", [(a * WITHIN + w, b * WITHIN + w) for a, b in plane_pairs for w in range(WITHIN)]
+        )
+
     columns = [[p * WITHIN + w for p in range(planes)] for w in range(WITHIN)]
     keys = store_keys.reshape(local_count * MROWS, KVH * HD)
     values = store_values.reshape(local_count * MROWS, KVH * HD)
@@ -380,13 +391,15 @@
     ctx_far = [xor(ctx_keys, 2), xor(ctx_values, 2)]
     ctx_near = [xor(ctx_keys, 1), xor(ctx_values, 1)]
     ids = all_planes(block_ids)
-    q_first, q_second = pack_queries(queries)
+    q_first = pack_queries(queries, 0)
     order.done(q_first)
     own = [pack_stores(*order.before(keys, values), 0)]
     order.done(own[0], *ctx_far)
     far = [xor(order.before(own[0])[0], 2)]
     own.append(pack_stores(*order.before(keys, values), 1))
     order.done(own[1])
+    q_second = pack_queries(*order.before(queries), 1)
+    order.done(q_second)
     far.append(xor(own[1], 2))
     ctx_diag = [xor(part, 1) for part in ctx_far]
     near = [xor(part, 1) for part in own]
@@ -427,7 +440,15 @@
         order.done(parts[0])
         if scattered:
             return [lax.psum_scatter(parts[0], "seq", scatter_dimension=0, axis_index_groups=columns)]
-        return [parts[0]] + [xor(parts[k], k * WITHIN) for k in range(1, planes)]
+        if planes != 4:
+            return [parts[0]] + [xor(parts[k], k * WITHIN) for k in range(1, planes)]
+        handed = [between(parts[k], [(0, 1), (3, 2)]) for k in (3, 2)]
+        summed = [
+            (parts[k].astype(jnp.float32) + part.astype(jnp.float32)).astype(jnp.bfloat16)
+            for k, part in zip((2, 3), handed, strict=True)
+        ]
+        far_parts = [between(summed[0], [(1, 3), (2, 0)]), between(summed[1], [(1, 2), (2, 1)])]
+        return [parts[0], xor(parts[1], WITHIN), *far_parts]
 
     own_uc, own_lse = ctx_step(queries, 0, KVH, 1)
     uc01, ctx_lse01 = ctx_step(spread[0], 0, 2, planes)
@@ -441,7 +462,7 @@
     um3, lses3 = mem_step(3, 1, ctx_lse3)
     coming.append(scale_step(2, um2, uc2, lses2, True))
     coming.append(scale_step(3, um3, uc3, lses3, False))
-    return finish_call(coming)
+    return finish_call(coming[1:], 1, finish_call(coming[:1], 0))
 
 
 def solution(mesh):

time: 215 us -> 212 us (0.986); the launches traced: 212 us -> 211 us
  waiting for transfers between devices: 67.8 us -> 63.2 us
  Pallas kernels: 95.3 us -> 99.8 us
    ppermute x27 -> x25, waiting for transfers between devices: 61 us -> 34.3 us  [xor(): return lax.ppermute(x, 'seq', [(i, i ^ bits) for i in range(devices)])]
    ppermute x0 -> x4, waiting for transfers between devices: none -> 23.8 us  [between(): lax.ppermute(x, 'seq', [(a * WITHIN + w, b * WITHIN + w) for a, b in plan...]
    ppermute x0 -> x4, starting transfers between devices: none -> 5.21 us  [between(): lax.ppermute(x, 'seq', [(a * WITHIN + w, b * WITHIN + w) for a, b in plan...]
    pallas_call x2 -> x4, Pallas kernels: 3.39 us -> 7.9 us  [the longest x2 4.08 us: finish_call(): pl.pallas_call(body, grid=(1,), in_specs=[pl.BlockSpec(memory_space=pl.AN...]
    ppermute x27 -> x25, starting transfers between devices: 29.7 us -> 25.3 us  [xor(): return lax.ppermute(x, 'seq', [(i, i ^ bits) for i in range(devices)])]
    unnamed x56 -> x60, local copies, waits for them, and re-layouts: 4.78 us -> 3.08 us
  transfers between devices with their start and end apart: 31 -> 33, of which waited for: 16 -> 18; matrix products, arithmetic and copies ran while one was open for 0% -> 0% of each run, Pallas kernels for 43% -> 45%
where the time goes in v6:
time: 212 us; the launch traced here: 211 us
  Pallas kernels  99.8 us (47%)
  waiting for transfers between devices  63.2 us (30%)
  starting transfers between devices  30.8 us (15%)
  between operations  13.5 us (6%)
  local copies, waits for them, and re-layouts  3.3 us (2%)
    pallas_call x4, Pallas kernels, ctx_call(): pl.pallas_call(functools.partial(ctx_kernel, base), grid_spec=pltpu.Prefe...  36.6 us
    pallas_call x3, Pallas kernels, mem_call(): pl.pallas_call(functools.partial(mem_kernel, masked), grid_spec=pltpu.Pre...  34.7 us
    ppermute x25, waiting for transfers between devices, xor(): return lax.ppermute(x, 'seq', [(i, i ^ bits) for i in range(devices)])  34.3 us
    ppermute x25, starting transfers between devices, xor(): return lax.ppermute(x, 'seq', [(i, i ^ bits) for i in range(devices)])  25.3 us
    ppermute x4, waiting for transfers between devices, between(): lax.ppermute(x, 'seq', [(a * WITHIN + w, b * WITHIN + w) for a, b in plan...  23.8 us
    pallas_call x3, Pallas kernels, scale_call(): pl.pallas_call(functools.partial(scale_kernel, planes, heads, first, scat...  11.9 us
    pallas_call x2, Pallas kernels, pack_stores(): pl.pallas_call(pack_stores_kernel, grid=(steps,), in_specs=[pl.BlockSpec(...  7.8 us
    ppermute x4, starting transfers between devices, between(): lax.ppermute(x, 'seq', [(a * WITHIN + w, b * WITHIN + w) for a, b in plan...  5.21 us
  transfers between devices with their start and end apart: 33, of which 18 were waited for; matrix products, arithmetic and copies ran while one was open for 0% of the time, Pallas kernels for 45%

profile of v6, /device:TPU:0, one launch (start us, length us, event | category | flops | bytes accessed | tf_op | source)
XLA Modules:
  0.0 210.8 jit_solution(14366398881681990476)
XLA Ops:
  8.6 3.0 %collective-permute-start.3 = (bf16[256,512]{1,0:T(8,128)(2,1)S(1)}, bf16[256,512]{1,0:T(8,128)(2,1)S(1)}, u32[]{:S(2)}, u32[]{:S(2)}) collective-permute-start(bf16[256,512]{1,0:T(8,128)(2,1)S(1)} %copy-done.17), channel_id=1, source_target_pairs={{0,2},{1,3},{2,0},{3,1},{4,6},{5,7},{6,4},{7,5},{8,10},{9,11},{10,... | collective-permute-start | bytes 786440 | tf_op jit(solution)/shard_map/ppermute | solution.py:376
  11.7 3.9 %pack_stores.2.s0 = bf16[2048,512]{1,0:T(8,128)(2,1)} custom-call(bf16[2048,512]{1,0:T(8,128)(2,1)} %bitcast.24, bf16[2048,512]{1,0:T(8,128)(2,1)} %bitcast.26), custom_call_target="tpu_custom_call" | custom-call | flops 1000 | bytes 1000 | tf_op jit(solution)/shard_map/pack_stores/pallas_call | solution.py:306
  15.6 3.1 %collective-permute-done.3.k2 = bf16[256,512]{1,0:T(8,128)(2,1)S(1)} collective-permute-done((bf16[256,512]{1,0:T(8,128)(2,1)S(1)}, bf16[256,512]{1,0:T(8,128)(2,1)S(1)}, u32[]{:S(2)}, u32[]{:S(2)}) %collective-permute-start.3) | collective-permute-done | bytes 262176 | tf_op jit(solution)/shard_map/ppermute | solution.py:376
  18.7 4.8 %collective-permute-done.4.v2 = bf16[256,512]{1,0:T(8,128)(2,1)S(1)} collective-permute-done((bf16[256,512]{1,0:T(8,128)(2,1)S(1)}, bf16[256,512]{1,0:T(8,128)(2,1)S(1)}, u32[]{:S(2)}, u32[]{:S(2)}) %collective-permute-start.4) | collective-permute-done | bytes 262176 | tf_op jit(solution)/shard_map/ppermute | solution.py:376
  25.3 3.9 %pack_stores.3.s0 = bf16[2048,512]{1,0:T(8,128)(2,1)} custom-call(bf16[2048,512]{1,0:T(8,128)(2,1)} %bitcast.25, bf16[2048,512]{1,0:T(8,128)(2,1)} %bitcast.27), custom_call_target="tpu_custom_call" | custom-call | flops 1000 | bytes 1000 | tf_op jit(solution)/shard_map/pack_stores/pallas_call | solution.py:306
  37.3 3.5 %collective-permute-done.2.refs_3_ = s32[1,32]{1,0:T(1,128)S(1)} collective-permute-done((s32[1,32]{1,0:T(1,128)S(1)}, s32[1,32]{1,0:T(1,128)S(1)}, u32[]{:S(2)}, u32[]{:S(2)}) %collective-permute-start.2) | collective-permute-done | bytes 160 | tf_op jit(solution)/shard_map/ppermute | solution.py:376
  43.5 9.4 %ctx_attend.4 = (bf16[4,1,256,512]{3,2,1,0:T(8,128)(2,1)}, f32[4,1,8,256]{3,2,1,0:T(8,128)}) custom-call(s32[1,8]{1,0:T(1,128)} %bitcast.16, bf16[256,2048]{1,0:T(8,128)(2,1)} %q_ref, bf16[256,512]{1,0:T(8,128)(2,1)} %k0.3, bf16[256,512]{1,0:T(8,128)(2,1)} %copy-done.21, bf16[256,512]{1,0:T(8,128)(2,1)} %copy-done.19, bf16[256,512]{1,0:T(8,128)(2,1)} %copy-done.24, ...), custom_call_target="tpu_custom_call" | custom-call | flops 1000 | bytes 1000 | tf_op jit(solution)/shard_map/ctx_attend/pallas_call | solution.py:173
  53.0 4.7 %all-gather.5.cloned.1.call-done = bf16[1024,1024]{1,0:T(8,128)(2,1)} async-done(((bf16[256,1024]{1,0:T(8,128)(2,1)}), bf16[1024,1024]{1,0:T(8,128)(2,1)}) %all-gather.5.cloned.1.call-update) | async-done | bytes 2097168 | tf_op jit(solution)/shard_map/all_gather | solution.py:409
  57.6 12.4 %ctx_attend.5 = (bf16[2,3,256,512]{3,2,1,0:T(8,128)(2,1)}, f32[2,3,8,256]{3,2,1,0:T(8,128)}) custom-call(s32[1,8]{1,0:T(1,128)} %bitcast.17, bf16[4,256,1024]{2,1,0:T(8,128)(2,1)} %bitcast.14, bf16[256,512]{1,0:T(8,128)(2,1)} %k0.3, bf16[256,512]{1,0:T(8,128)(2,1)} %copy-done.21, bf16[256,512]{1,0:T(8,128)(2,1)} %copy-done.19, bf16[256,512]{1,0:T(8,128)(2,1)} %copy-done.24, ...), custom_call_target="tpu_custom_call" | custom-call | flops 1000 | bytes 1000 | tf_op jit(solution)/shard_map/ctx_attend/pallas_call | solution.py:173
  75.9 15.9 %mem_attend.3 = (bf16[2,4,256,512]{3,2,1,0:T(8,128)(2,1)S(1)}, f32[2,4,8,256]{3,2,1,0:T(8,128)S(1)}) custom-call(s32[5,8]{1,0:T(8,128)S(1)} %pad_add_fusion.info, bf16[4,256,1024]{2,1,0:T(8,128)(2,1)S(1)} %bitcast.15, bf16[2048,512]{1,0:T(8,128)(2,1)} %pack_stores.2.s0, bf16[2048,512]{1,0:T(8,128)(2,1)} %collective-permute-done.5.s1, ...), custom_call_target="tpu_custom_call" | custom-call | flops 1000 | bytes 1000 | tf_op jit(solution)/shard_map/mem_attend/pallas_call | solution.py:192
  96.3 4.8 %collective-permute-done.12.refs_1_ = f32[2,4,8,256]{3,2,1,0:T(8,128)S(1)} collective-permute-done((f32[2,4,8,256]{3,2,1,0:T(8,128)S(1)}, f32[2,4,8,256]{3,2,1,0:T(8,128)S(1)}, u32[]{:S(2)}, u32[]{:S(2)}) %collective-permute-start.12) | collective-permute-done | bytes 65568 | tf_op jit(solution)/shard_map/ppermute | solution.py:376
  101.1 3.4 %collective-permute-done.13.refs_2_ = f32[2,4,8,256]{3,2,1,0:T(8,128)S(1)} collective-permute-done((f32[2,4,8,256]{3,2,1,0:T(8,128)S(1)}, f32[2,4,8,256]{3,2,1,0:T(8,128)S(1)}, u32[]{:S(2)}, u32[]{:S(2)}) %collective-permute-start.13) | collective-permute-done | bytes 65568 | tf_op jit(solution)/shard_map/ppermute | solution.py:376
  105.4 4.7 %scale_mix.3 = bf16[4,2,256,512]{3,2,1,0:T(8,128)(2,1)} custom-call(s32[1,8]{1,0:T(1,128)S(1)} %bitcast.21, bf16[2,4,256,512]{3,2,1,0:T(8,128)(2,1)S(1)} %get-tuple-element.161.um_ref, bf16[4,1,256,512]{3,2,1,0:T(8,128)(2,1)S(1)} %copy-done.1, bf16[2,3,256,512]{3,2,1,0:T(8,128)(2,1)S(1)} %copy-done.3, f32[16]{0:T(128)S(1)} %add_divide_fusion.gate_ref, ...), custom_call_target="tpu_custom_call" | custom-call | flops 1000 | bytes 1000 | tf_op jit(solution)/shard_map/scale_mix/pallas_call | solution.py:225
  110.5 7.3 %ctx_attend.6 = (bf16[1,3,256,512]{3,2,1,0:T(8,128)(2,1)}, f32[1,3,8,256]{3,2,1,0:T(8,128)}) custom-call(s32[1,8]{1,0:T(1,128)} %bitcast.18, bf16[4,256,1024]{2,1,0:T(8,128)(2,1)} %bitcast.10, bf16[256,512]{1,0:T(8,128)(2,1)} %k0.3, bf16[256,512]{1,0:T(8,128)(2,1)} %copy-done.21, bf16[256,512]{1,0:T(8,128)(2,1)} %copy-done.19, bf16[256,512]{1,0:T(8,128)(2,1)} %copy-done.24, ...), custom_call_target="tpu_custom_call" | custom-call | flops 1000 | bytes 1000 | tf_op jit(solution)/shard_map/ctx_attend/pallas_call | solution.py:173
  119.1 7.5 %ctx_attend.7 = (bf16[1,3,256,512]{3,2,1,0:T(8,128)(2,1)}, f32[1,3,8,256]{3,2,1,0:T(8,128)}) custom-call(s32[1,8]{1,0:T(1,128)} %bitcast.19, bf16[4,256,1024]{2,1,0:T(8,128)(2,1)} %bitcast.11, bf16[256,512]{1,0:T(8,128)(2,1)} %k0.3, bf16[256,512]{1,0:T(8,128)(2,1)} %copy-done.21, bf16[256,512]{1,0:T(8,128)(2,1)} %copy-done.19, bf16[256,512]{1,0:T(8,128)(2,1)} %copy-done.24, ...), custom_call_target="tpu_custom_call" | custom-call | flops 1000 | bytes 1000 | tf_op jit(solution)/shard_map/ctx_attend/pallas_call | solution.py:173
  126.6 9.4 %mem_attend.4 = (bf16[1,4,256,512]{3,2,1,0:T(8,128)(2,1)S(1)}, f32[1,4,8,256]{3,2,1,0:T(8,128)S(1)}) custom-call(s32[5,8]{1,0:T(8,128)S(1)} %pad_add_fusion.info, bf16[4,256,1024]{2,1,0:T(8,128)(2,1)S(1)} %bitcast.12, bf16[2048,512]{1,0:T(8,128)(2,1)} %pack_stores.3.s0, bf16[2048,512]{1,0:T(8,128)(2,1)} %collective-permute-done.15.s1, ...), custom_call_target="tpu_custom_call" | custom-call | flops 1000 | bytes 1000 | tf_op jit(solution)/shard_map/mem_attend/pallas_call | solution.py:192
  137.2 3.3 %collective-permute-start.20 = (f32[1,4,8,256]{3,2,1,0:T(8,128)S(1)}, f32[1,4,8,256]{3,2,1,0:T(8,128)S(1)}, u32[]{:S(2)}, u32[]{:S(2)}) collective-permute-start(f32[1,4,8,256]{3,2,1,0:T(8,128)S(1)} %get-tuple-element.213.refs_0_), channel_id=1, source_target_pairs={{0,12},{1,13},{2,14},{3,15},{4,8},{5,9},{6,10},{7,11},{8,4},{9,5},... | collective-permute-start | bytes 98312 | tf_op jit(solution)/shard_map/ppermute | solution.py:376
  140.5 9.4 %mem_attend.5 = (bf16[1,4,256,512]{3,2,1,0:T(8,128)(2,1)S(1)}, f32[1,4,8,256]{3,2,1,0:T(8,128)S(1)}) custom-call(s32[5,8]{1,0:T(8,128)S(1)} %pad_add_fusion.info, bf16[4,256,1024]{2,1,0:T(8,128)(2,1)S(1)} %bitcast.13, bf16[2048,512]{1,0:T(8,128)(2,1)} %pack_stores.3.s0, bf16[2048,512]{1,0:T(8,128)(2,1)} %collective-permute-done.15.s1, ...), custom_call_target="tpu_custom_call" | custom-call | flops 1000 | bytes 1000 | tf_op jit(solution)/shard_map/mem_attend/pallas_call | solution.py:192
  150.9 3.8 %scale_mix.4 = bf16[4,1,256,512]{3,2,1,0:T(8,128)(2,1)} custom-call(s32[1,8]{1,0:T(1,128)S(1)} %bitcast.22, bf16[1,4,256,512]{3,2,1,0:T(8,128)(2,1)S(1)} %get-tuple-element.211.um_ref, bf16[4,1,256,512]{3,2,1,0:T(8,128)(2,1)S(1)} %copy-done.1, bf16[1,3,256,512]{3,2,1,0:T(8,128)(2,1)S(1)} %copy-done.6, f32[16]{0:T(128)S(1)} %add_divide_fusion.gate_ref, ...), custom_call_target="tpu_custom_call" | custom-call | flops 1000 | bytes 1000 | tf_op jit(solution)/shard_map/scale_mix/pallas_call | solution.py:225
  155.9 3.3 %collective-permute-start.23 = (f32[1,4,8,256]{3,2,1,0:T(8,128)S(1)}, f32[1,4,8,256]{3,2,1,0:T(8,128)S(1)}, u32[]{:S(2)}, u32[]{:S(2)}) collective-permute-start(f32[1,4,8,256]{3,2,1,0:T(8,128)S(1)} %get-tuple-element.221.refs_0_), channel_id=1, source_target_pairs={{0,12},{1,13},{2,14},{3,15},{4,8},{5,9},{6,10},{7,11},{8,4},{9,5},... | collective-permute-start | bytes 98312 | tf_op jit(solution)/shard_map/ppermute | solution.py:376
  161.6 3.4 %scale_mix.5 = (bf16[1,256,512]{2,1,0:T(8,128)(2,1)S(1)}, bf16[1,256,512]{2,1,0:T(8,128)(2,1)S(1)}, bf16[1,256,512]{2,1,0:T(8,128)(2,1)S(1)}, bf16[1,256,512]{2,1,0:T(8,128)(2,1)S(1)}) custom-call(s32[1,8]{1,0:T(1,128)S(1)} %bitcast.23, bf16[1,4,256,512]{3,2,1,0:T(8,128)(2,1)S(1)} %copy-done.5, bf16[4,1,256,512]{3,2,1,0:T(8,128)(2,1)S(1)} %copy-done.1, ...), custom_call_target="tpu_custom_call" | custom-call | flops 1000 | bytes 1000 | tf_op jit(solution)/shard_map/scale_mix/pallas_call | solution.py:225
  168.4 10.8 %collective-permute-done.27 = bf16[1,256,512]{2,1,0:T(8,128)(2,1)S(1)} collective-permute-done((bf16[1,256,512]{2,1,0:T(8,128)(2,1)S(1)}, bf16[1,256,512]{2,1,0:T(8,128)(2,1)S(1)}, u32[]{:S(2)}, u32[]{:S(2)}) %collective-permute-start.27) | collective-permute-done | bytes 262176 | tf_op jit(solution)/shard_map/ppermute | solution.py:382
  179.9 10.5 %collective-permute-done.25 = bf16[1,256,512]{2,1,0:T(8,128)(2,1)S(1)} collective-permute-done((bf16[1,256,512]{2,1,0:T(8,128)(2,1)S(1)}, bf16[1,256,512]{2,1,0:T(8,128)(2,1)S(1)}, u32[]{:S(2)}, u32[]{:S(2)}) %collective-permute-start.25) | collective-permute-done | bytes 262176 | tf_op jit(solution)/shard_map/ppermute | solution.py:382
  193.7 5.1 %collective-permute-done.24.refs_3_ = bf16[1,256,512]{2,1,0:T(8,128)(2,1)S(1)} collective-permute-done((bf16[1,256,512]{2,1,0:T(8,128)(2,1)S(1)}, bf16[1,256,512]{2,1,0:T(8,128)(2,1)S(1)}, u32[]{:S(2)}, u32[]{:S(2)}) %collective-permute-start.24) | collective-permute-done | bytes 262176 | tf_op jit(solution)/shard_map/ppermute | solution.py:376
  (129 shorter events, 46.0 us)
Async XLA Ops:
  6.5 51.1 %all-gather.5.cloned.1.call-start = ((), (), s32[]{:S(2)}) async-start(), calls=%async_computation.4 | async-start | bytes 2621440 | tf_op jit(solution)/shard_map/all_gather | solution.py:409
  8.5 102.0 %all-gather.7.cloned.1.call-start = ((), (), s32[]{:S(2)}) async-start(), calls=%async_computation.5 | async-start | bytes 2621440 | tf_op jit(solution)/shard_map/all_gather | solution.py:409
  8.6 10.2 %collective-permute-start.3 = (bf16[256,512]{1,0:T(8,128)(2,1)S(1)}, bf16[256,512]{1,0:T(8,128)(2,1)S(1)}, u32[]{:S(2)}, u32[]{:S(2)}) collective-permute-start(bf16[256,512]{1,0:T(8,128)(2,1)S(1)} %copy-done.17), channel_id=1, source_target_pairs={{0,2},{1,3},{2,0},{3,1},{4,6},{5,7},{6,4},{7,5},{8,10},{9,11},{10,... | collective-permute-start | bytes 786440 | tf_op jit(solution)/shard_map/ppermute | solution.py:376
  11.6 11.9 %collective-permute-start.4 = (bf16[256,512]{1,0:T(8,128)(2,1)S(1)}, bf16[256,512]{1,0:T(8,128)(2,1)S(1)}, u32[]{:S(2)}, u32[]{:S(2)}) collective-permute-start(bf16[256,512]{1,0:T(8,128)(2,1)S(1)} %copy-done.18), channel_id=1, source_target_pairs={{0,2},{1,3},{2,0},{3,1},{4,6},{5,7},{6,4},{7,5},{8,10},{9,11},{10,... | collective-permute-start | bytes 786440 | tf_op jit(solution)/shard_map/ppermute | solution.py:376
  23.5 47.2 %collective-permute-start.6 = (bf16[2048,512]{1,0:T(8,128)(2,1)}, bf16[2048,512]{1,0:T(8,128)(2,1)}, u32[]{:S(2)}, u32[]{:S(2)}) collective-permute-start(bf16[2048,512]{1,0:T(8,128)(2,1)} %pack_stores.2.s0), channel_id=1, source_target_pairs={{0,2},{1,3},{2,0},{3,1},{4,6},{5,7},{6,4},{7,5},{8,10},{9,11},{10,... | collective-permute-start | bytes 6291464 | tf_op jit(solution)/shard_map/ppermute | solution.py:376
  31.1 160.8 %reduce-scatter.3.cloned.1.call-start = ((), (), s32[]{:S(2)}) async-start(), calls=%async_computation.2 | async-start | bytes 2621440 | tf_op jit(solution)/shard_map/reduce_scatter | solution.py:442
  35.6 6.5 %collective-permute-start.7 = (bf16[256,512]{1,0:T(8,128)(2,1)S(1)}, bf16[256,512]{1,0:T(8,128)(2,1)S(1)}, u32[]{:S(2)}, u32[]{:S(2)}) collective-permute-start(bf16[256,512]{1,0:T(8,128)(2,1)S(1)} %copy-done.17), channel_id=1, source_target_pairs={{0,1},{1,0},{2,3},{3,2},{4,5},{5,4},{6,7},{7,6},{8,9},{9,8},{10,11... | collective-permute-start | bytes 786440 | tf_op jit(solution)/shard_map/ppermute | solution.py:376
  35.6 7.0 %collective-permute-start.9 = (bf16[256,512]{1,0:T(8,128)(2,1)S(1)}, bf16[256,512]{1,0:T(8,128)(2,1)S(1)}, u32[]{:S(2)}, u32[]{:S(2)}) collective-permute-start(bf16[256,512]{1,0:T(8,128)(2,1)S(1)} %copy-done.18), channel_id=1, source_target_pairs={{0,1},{1,0},{2,3},{3,2},{4,5},{5,4},{6,7},{7,6},{8,9},{9,8},{10,11... | collective-permute-start | bytes 786440 | tf_op jit(solution)/shard_map/ppermute | solution.py:376
  42.1 30.2 %collective-permute-start.5 = (bf16[2048,512]{1,0:T(8,128)(2,1)}, bf16[2048,512]{1,0:T(8,128)(2,1)}, u32[]{:S(2)}, u32[]{:S(2)}) collective-permute-start(bf16[2048,512]{1,0:T(8,128)(2,1)} %pack_stores.2.s0), channel_id=1, source_target_pairs={{0,1},{1,0},{2,3},{3,2},{4,5},{5,4},{6,7},{7,6},{8,9},{9,8},{10,11... | collective-permute-start | bytes 6291464 | tf_op jit(solution)/shard_map/ppermute | solution.py:376
  70.8 48.4 %collective-permute-start.16 = (bf16[2048,512]{1,0:T(8,128)(2,1)}, bf16[2048,512]{1,0:T(8,128)(2,1)}, u32[]{:S(2)}, u32[]{:S(2)}) collective-permute-start(bf16[2048,512]{1,0:T(8,128)(2,1)} %pack_stores.3.s0), channel_id=1, source_target_pairs={{0,2},{1,3},{2,0},{3,1},{4,6},{5,7},{6,4},{7,5},{8,10},{9,11},{10,... | collective-permute-start | bytes 6291464 | tf_op jit(solution)/shard_map/ppermute | solution.py:376
  91.8 9.3 %collective-permute-start.12 = (f32[2,4,8,256]{3,2,1,0:T(8,128)S(1)}, f32[2,4,8,256]{3,2,1,0:T(8,128)S(1)}, u32[]{:S(2)}, u32[]{:S(2)}) collective-permute-start(f32[2,4,8,256]{3,2,1,0:T(8,128)S(1)} %get-tuple-element.164.refs_0_), channel_id=1, source_target_pairs={{0,4},{1,5},{2,6},{3,7},{4,0},{5,1},{6,2},{7,3},{8,12},{9,13},{10,... | collective-permute-start | bytes 196616 | tf_op jit(solution)/shard_map/ppermute | solution.py:376
  93.4 11.1 %collective-permute-start.13 = (f32[2,4,8,256]{3,2,1,0:T(8,128)S(1)}, f32[2,4,8,256]{3,2,1,0:T(8,128)S(1)}, u32[]{:S(2)}, u32[]{:S(2)}) collective-permute-start(f32[2,4,8,256]{3,2,1,0:T(8,128)S(1)} %get-tuple-element.164.refs_0_), channel_id=1, source_target_pairs={{0,8},{1,9},{2,10},{3,11},{4,12},{5,13},{6,14},{7,15},{8,0},{9,1},... | collective-permute-start | bytes 196616 | tf_op jit(solution)/shard_map/ppermute | solution.py:376
  96.0 9.4 %collective-permute-start.14 = (f32[2,4,8,256]{3,2,1,0:T(8,128)S(1)}, f32[2,4,8,256]{3,2,1,0:T(8,128)S(1)}, u32[]{:S(2)}, u32[]{:S(2)}) collective-permute-start(f32[2,4,8,256]{3,2,1,0:T(8,128)S(1)} %get-tuple-element.164.refs_0_), channel_id=1, source_target_pairs={{0,12},{1,13},{2,14},{3,15},{4,8},{5,9},{6,10},{7,11},{8,4},{9,5},... | collective-permute-start | bytes 196616 | tf_op jit(solution)/shard_map/ppermute | solution.py:376
  110.2 91.5 %reduce-scatter.5.cloned.1.call-start = ((), (), s32[]{:S(2)}) async-start(), calls=%async_computation.3 | async-start | bytes 1310720 | tf_op jit(solution)/shard_map/reduce_scatter | solution.py:442
  110.4 16.2 %collective-permute-start.15 = (bf16[2048,512]{1,0:T(8,128)(2,1)}, bf16[2048,512]{1,0:T(8,128)(2,1)}, u32[]{:S(2)}, u32[]{:S(2)}) collective-permute-start(bf16[2048,512]{1,0:T(8,128)(2,1)} %pack_stores.3.s0), channel_id=1, source_target_pairs={{0,1},{1,0},{2,3},{3,2},{4,5},{5,4},{6,7},{7,6},{8,9},{9,8},{10,11... | collective-permute-start | bytes 6291464 | tf_op jit(solution)/shard_map/ppermute | solution.py:376
  119.1 7.5 %collective-permute-start.17 = (bf16[2048,512]{1,0:T(8,128)(2,1)}, bf16[2048,512]{1,0:T(8,128)(2,1)}, u32[]{:S(2)}, u32[]{:S(2)}) collective-permute-start(bf16[2048,512]{1,0:T(8,128)(2,1)} %collective-permute-done.16.s2), channel_id=1, source_target_pairs={{0,1},{1,0},{2,3},{3,2},{4,5},{5,4},{6,7},{7,6},{8,9},{9,8},{10,11... | collective-permute-start | bytes 6291464 | tf_op jit(solution)/shard_map/ppermute | solution.py:376
  136.0 14.8 %collective-permute-start.18 = (f32[1,4,8,256]{3,2,1,0:T(8,128)S(1)}, f32[1,4,8,256]{3,2,1,0:T(8,128)S(1)}, u32[]{:S(2)}, u32[]{:S(2)}) collective-permute-start(f32[1,4,8,256]{3,2,1,0:T(8,128)S(1)} %get-tuple-element.213.refs_0_), channel_id=1, source_target_pairs={{0,4},{1,5},{2,6},{3,7},{4,0},{5,1},{6,2},{7,3},{8,12},{9,13},{10,... | collective-permute-start | bytes 98312 | tf_op jit(solution)/shard_map/ppermute | solution.py:376
  136.4 14.5 %collective-permute-start.19 = (f32[1,4,8,256]{3,2,1,0:T(8,128)S(1)}, f32[1,4,8,256]{3,2,1,0:T(8,128)S(1)}, u32[]{:S(2)}, u32[]{:S(2)}) collective-permute-start(f32[1,4,8,256]{3,2,1,0:T(8,128)S(1)} %get-tuple-element.213.refs_0_), channel_id=1, source_target_pairs={{0,8},{1,9},{2,10},{3,11},{4,12},{5,13},{6,14},{7,15},{8,0},{9,1},... | collective-permute-start | bytes 98312 | tf_op jit(solution)/shard_map/ppermute | solution.py:376
  137.2 13.6 %collective-permute-start.20 = (f32[1,4,8,256]{3,2,1,0:T(8,128)S(1)}, f32[1,4,8,256]{3,2,1,0:T(8,128)S(1)}, u32[]{:S(2)}, u32[]{:S(2)}) collective-permute-start(f32[1,4,8,256]{3,2,1,0:T(8,128)S(1)} %get-tuple-element.213.refs_0_), channel_id=1, source_target_pairs={{0,12},{1,13},{2,14},{3,15},{4,8},{5,9},{6,10},{7,11},{8,4},{9,5},... | collective-permute-start | bytes 98312 | tf_op jit(solution)/shard_map/ppermute | solution.py:376
  165.0 14.2 %collective-permute-start.27 = (bf16[1,256,512]{2,1,0:T(8,128)(2,1)S(1)}, bf16[1,256,512]{2,1,0:T(8,128)(2,1)S(1)}, u32[]{:S(2)}, u32[]{:S(2)}) collective-permute-start(bf16[1,256,512]{2,1,0:T(8,128)(2,1)S(1)} %get-tuple-element.227), channel_id=1, source_target_pairs={{0,4},{1,5},{2,6},{3,7},{12,8},{13,9},{14,10},{15,11},{16,20},{17,... | collective-permute-start | bytes 786440 | tf_op jit(solution)/shard_map/ppermute | solution.py:382
  167.0 23.5 %collective-permute-start.25 = (bf16[1,256,512]{2,1,0:T(8,128)(2,1)S(1)}, bf16[1,256,512]{2,1,0:T(8,128)(2,1)S(1)}, u32[]{:S(2)}, u32[]{:S(2)}) collective-permute-start(bf16[1,256,512]{2,1,0:T(8,128)(2,1)S(1)} %get-tuple-element.228), channel_id=1, source_target_pairs={{0,4},{1,5},{2,6},{3,7},{12,8},{13,9},{14,10},{15,11},{16,20},{17,... | collective-permute-start | bytes 786440 | tf_op jit(solution)/shard_map/ppermute | solution.py:382
  168.3 30.6 %collective-permute-start.24 = (bf16[1,256,512]{2,1,0:T(8,128)(2,1)S(1)}, bf16[1,256,512]{2,1,0:T(8,128)(2,1)S(1)}, u32[]{:S(2)}, u32[]{:S(2)}) collective-permute-start(bf16[1,256,512]{2,1,0:T(8,128)(2,1)S(1)} %get-tuple-element.226), channel_id=1, source_target_pairs={{0,4},{1,5},{2,6},{3,7},{4,0},{5,1},{6,2},{7,3},{8,12},{9,13},{10,... | collective-permute-start | bytes 786440 | tf_op jit(solution)/shard_map/ppermute | solution.py:376
  179.3 19.6 %collective-permute-start.28 = (bf16[1,256,512]{2,1,0:T(8,128)(2,1)S(1)}, bf16[1,256,512]{2,1,0:T(8,128)(2,1)S(1)}, u32[]{:S(2)}, u32[]{:S(2)}) collective-permute-start(bf16[1,256,512]{2,1,0:T(8,128)(2,1)S(1)} %add_convert_fusion), channel_id=1, source_target_pairs={{4,8},{5,9},{6,10},{7,11},{8,4},{9,5},{10,6},{11,7},{20,24},{21,25... | collective-permute-start | bytes 786440 | tf_op jit(solution)/shard_map/ppermute | solution.py:382
  190.5 10.8 %collective-permute-start.26 = (bf16[1,256,512]{2,1,0:T(8,128)(2,1)S(1)}, bf16[1,256,512]{2,1,0:T(8,128)(2,1)S(1)}, u32[]{:S(2)}, u32[]{:S(2)}) collective-permute-start(bf16[1,256,512]{2,1,0:T(8,128)(2,1)S(1)} %add_convert_fusion.1), channel_id=1, source_target_pairs={{4,12},{5,13},{6,14},{7,15},{8,0},{9,1},{10,2},{11,3},{20,28},{21,... | collective-permute-start | bytes 786440 | tf_op jit(solution)/shard_map/ppermute | solution.py:382
  (39 other events, 356.2 us)
Sparse Core Ops, SparseCore 0:
  8.9 48.6 all-gather.4
  59.2 50.1 all-gather.6
  111.7 46.1 reduce-scatter.2
  160.2 41.3 reduce-scatter.4

commit v7 on v6

--- a/solution.py
+++ b/solution.py
@@ -460,8 +460,8 @@
     uc3, ctx_lse3 = ctx_step(spread[1], 3, 1, planes)
     um2, lses2 = mem_step(2, 1, ctx_lse2)
     um3, lses3 = mem_step(3, 1, ctx_lse3)
-    coming.append(scale_step(2, um2, uc2, lses2, True))
-    coming.append(scale_step(3, um3, uc3, lses3, False))
+    last = scale_step(3, um3, uc3, lses3, False)
+    coming += [scale_step(2, um2, uc2, lses2, True), last]
     return finish_call(coming[1:], 1, finish_call(coming[:1], 0))
 
 

time: 212 us -> 213 us (level)
  starting transfers between devices: 30.8 us -> 34.3 us
    ppermute x4, starting transfers between devices: 5.21 us -> 8.84 us  [between(): lax.ppermute(x, 'seq', [(a * WITHIN + w, b * WITHIN + w) for a, b in plan...]
where the time goes in v7:
time: 213 us
  Pallas kernels  99.7 us (47%)
  waiting for transfers between devices  61.6 us (29%)
  starting transfers between devices  34.3 us (16%)
  between operations  13.5 us (6%)
  local copies, waits for them, and re-layouts  3.34 us (2%)
    pallas_call x4, Pallas kernels, ctx_call(): pl.pallas_call(functools.partial(ctx_kernel, base), grid_spec=pltpu.Prefe...  36.6 us
    pallas_call x3, Pallas kernels, mem_call(): pl.pallas_call(functools.partial(mem_kernel, masked), grid_spec=pltpu.Pre...  34.7 us
    ppermute x25, waiting for transfers between devices, xor(): return lax.ppermute(x, 'seq', [(i, i ^ bits) for i in range(devices)])  33.2 us
    ppermute x25, starting transfers between devices, xor(): return lax.ppermute(x, 'seq', [(i, i ^ bits) for i in range(devices)])  25.1 us
    ppermute x4, waiting for transfers between devices, between(): lax.ppermute(x, 'seq', [(a * WITHIN + w, b * WITHIN + w) for a, b in plan...  23.7 us
    pallas_call x3, Pallas kernels, scale_call(): pl.pallas_call(functools.partial(scale_kernel, planes, heads, first, scat...  11.8 us
    ppermute x4, starting transfers between devices, between(): lax.ppermute(x, 'seq', [(a * WITHIN + w, b * WITHIN + w) for a, b in plan...  8.84 us
    pallas_call x2, Pallas kernels, pack_stores(): pl.pallas_call(pack_stores_kernel, grid=(steps,), in_specs=[pl.BlockSpec(...  7.79 us
  transfers between devices with their start and end apart: 33, of which 18 were waited for; matrix products, arithmetic and copies ran while one was open for 0% of the time, Pallas kernels for 45%

profile of v7, /device:TPU:0, one launch (start us, length us, event | category | flops | bytes accessed | tf_op | source)
XLA Modules:
  0.0 212.6 jit_solution(13312418540752222471)
XLA Ops:
  11.7 3.9 %pack_stores.2.s0 = bf16[2048,512]{1,0:T(8,128)(2,1)} custom-call(bf16[2048,512]{1,0:T(8,128)(2,1)} %bitcast.24, bf16[2048,512]{1,0:T(8,128)(2,1)} %bitcast.26), custom_call_target="tpu_custom_call" | custom-call | flops 1000 | bytes 1000 | tf_op jit(solution)/shard_map/pack_stores/pallas_call | solution.py:306
  15.6 3.2 %collective-permute-done.3.k2 = bf16[256,512]{1,0:T(8,128)(2,1)S(1)} collective-permute-done((bf16[256,512]{1,0:T(8,128)(2,1)S(1)}, bf16[256,512]{1,0:T(8,128)(2,1)S(1)}, u32[]{:S(2)}, u32[]{:S(2)}) %collective-permute-start.3) | collective-permute-done | bytes 262176 | tf_op jit(solution)/shard_map/ppermute | solution.py:376
  18.7 4.8 %collective-permute-done.4.v2 = bf16[256,512]{1,0:T(8,128)(2,1)S(1)} collective-permute-done((bf16[256,512]{1,0:T(8,128)(2,1)S(1)}, bf16[256,512]{1,0:T(8,128)(2,1)S(1)}, u32[]{:S(2)}, u32[]{:S(2)}) %collective-permute-start.4) | collective-permute-done | bytes 262176 | tf_op jit(solution)/shard_map/ppermute | solution.py:376
  25.3 3.9 %pack_stores.3.s0 = bf16[2048,512]{1,0:T(8,128)(2,1)} custom-call(bf16[2048,512]{1,0:T(8,128)(2,1)} %bitcast.25, bf16[2048,512]{1,0:T(8,128)(2,1)} %bitcast.27), custom_call_target="tpu_custom_call" | custom-call | flops 1000 | bytes 1000 | tf_op jit(solution)/shard_map/pack_stores/pallas_call | solution.py:306
  37.3 3.5 %collective-permute-done.2.refs_3_ = s32[1,32]{1,0:T(1,128)S(1)} collective-permute-done((s32[1,32]{1,0:T(1,128)S(1)}, s32[1,32]{1,0:T(1,128)S(1)}, u32[]{:S(2)}, u32[]{:S(2)}) %collective-permute-start.2) | collective-permute-done | bytes 160 | tf_op jit(solution)/shard_map/ppermute | solution.py:376
  43.5 9.4 %ctx_attend.4 = (bf16[4,1,256,512]{3,2,1,0:T(8,128)(2,1)}, f32[4,1,8,256]{3,2,1,0:T(8,128)}) custom-call(s32[1,8]{1,0:T(1,128)} %bitcast.16, bf16[256,2048]{1,0:T(8,128)(2,1)} %q_ref, bf16[256,512]{1,0:T(8,128)(2,1)} %k0.3, bf16[256,512]{1,0:T(8,128)(2,1)} %copy-done.19, bf16[256,512]{1,0:T(8,128)(2,1)} %copy-done.17, bf16[256,512]{1,0:T(8,128)(2,1)} %copy-done.22, ...), custom_call_target="tpu_custom_call" | custom-call | flops 1000 | bytes 1000 | tf_op jit(solution)/shard_map/ctx_attend/pallas_call | solution.py:173
  53.0 4.7 %all-gather.5.cloned.1.call-done = bf16[1024,1024]{1,0:T(8,128)(2,1)} async-done(((bf16[256,1024]{1,0:T(8,128)(2,1)}), bf16[1024,1024]{1,0:T(8,128)(2,1)}) %all-gather.5.cloned.1.call-update) | async-done | bytes 2097168 | tf_op jit(solution)/shard_map/all_gather | solution.py:409
  57.6 12.4 %ctx_attend.5 = (bf16[2,3,256,512]{3,2,1,0:T(8,128)(2,1)}, f32[2,3,8,256]{3,2,1,0:T(8,128)}) custom-call(s32[1,8]{1,0:T(1,128)} %bitcast.17, bf16[4,256,1024]{2,1,0:T(8,128)(2,1)} %bitcast.14, bf16[256,512]{1,0:T(8,128)(2,1)} %k0.3, bf16[256,512]{1,0:T(8,128)(2,1)} %copy-done.19, bf16[256,512]{1,0:T(8,128)(2,1)} %copy-done.17, bf16[256,512]{1,0:T(8,128)(2,1)} %copy-done.22, ...), custom_call_target="tpu_custom_call" | custom-call | flops 1000 | bytes 1000 | tf_op jit(solution)/shard_map/ctx_attend/pallas_call | solution.py:173
  75.9 15.9 %mem_attend.3 = (bf16[2,4,256,512]{3,2,1,0:T(8,128)(2,1)S(1)}, f32[2,4,8,256]{3,2,1,0:T(8,128)S(1)}) custom-call(s32[5,8]{1,0:T(8,128)S(1)} %pad_add_fusion.info, bf16[4,256,1024]{2,1,0:T(8,128)(2,1)S(1)} %bitcast.15, bf16[2048,512]{1,0:T(8,128)(2,1)} %pack_stores.2.s0, bf16[2048,512]{1,0:T(8,128)(2,1)} %collective-permute-done.5.s1, ...), custom_call_target="tpu_custom_call" | custom-call | flops 1000 | bytes 1000 | tf_op jit(solution)/shard_map/mem_attend/pallas_call | solution.py:192
  96.3 4.8 %collective-permute-done.12.refs_1_ = f32[2,4,8,256]{3,2,1,0:T(8,128)S(1)} collective-permute-done((f32[2,4,8,256]{3,2,1,0:T(8,128)S(1)}, f32[2,4,8,256]{3,2,1,0:T(8,128)S(1)}, u32[]{:S(2)}, u32[]{:S(2)}) %collective-permute-start.12) | collective-permute-done | bytes 65568 | tf_op jit(solution)/shard_map/ppermute | solution.py:376
  101.1 3.4 %collective-permute-done.13.refs_2_ = f32[2,4,8,256]{3,2,1,0:T(8,128)S(1)} collective-permute-done((f32[2,4,8,256]{3,2,1,0:T(8,128)S(1)}, f32[2,4,8,256]{3,2,1,0:T(8,128)S(1)}, u32[]{:S(2)}, u32[]{:S(2)}) %collective-permute-start.13) | collective-permute-done | bytes 65568 | tf_op jit(solution)/shard_map/ppermute | solution.py:376
  105.4 4.7 %scale_mix.3 = bf16[4,2,256,512]{3,2,1,0:T(8,128)(2,1)} custom-call(s32[1,8]{1,0:T(1,128)S(1)} %bitcast.21, bf16[2,4,256,512]{3,2,1,0:T(8,128)(2,1)S(1)} %get-tuple-element.161.um_ref, bf16[4,1,256,512]{3,2,1,0:T(8,128)(2,1)S(1)} %copy-done.1, bf16[2,3,256,512]{3,2,1,0:T(8,128)(2,1)S(1)} %copy-done.3, f32[16]{0:T(128)S(1)} %add_divide_fusion.gate_ref, ...), custom_call_target="tpu_custom_call" | custom-call | flops 1000 | bytes 1000 | tf_op jit(solution)/shard_map/scale_mix/pallas_call | solution.py:225
  110.5 7.3 %ctx_attend.6 = (bf16[1,3,256,512]{3,2,1,0:T(8,128)(2,1)}, f32[1,3,8,256]{3,2,1,0:T(8,128)}) custom-call(s32[1,8]{1,0:T(1,128)} %bitcast.18, bf16[4,256,1024]{2,1,0:T(8,128)(2,1)} %bitcast.10, bf16[256,512]{1,0:T(8,128)(2,1)} %k0.3, bf16[256,512]{1,0:T(8,128)(2,1)} %copy-done.19, bf16[256,512]{1,0:T(8,128)(2,1)} %copy-done.17, bf16[256,512]{1,0:T(8,128)(2,1)} %copy-done.22, ...), custom_call_target="tpu_custom_call" | custom-call | flops 1000 | bytes 1000 | tf_op jit(solution)/shard_map/ctx_attend/pallas_call | solution.py:173
  119.1 7.4 %ctx_attend.7 = (bf16[1,3,256,512]{3,2,1,0:T(8,128)(2,1)}, f32[1,3,8,256]{3,2,1,0:T(8,128)}) custom-call(s32[1,8]{1,0:T(1,128)} %bitcast.19, bf16[4,256,1024]{2,1,0:T(8,128)(2,1)} %bitcast.11, bf16[256,512]{1,0:T(8,128)(2,1)} %k0.3, bf16[256,512]{1,0:T(8,128)(2,1)} %copy-done.19, bf16[256,512]{1,0:T(8,128)(2,1)} %copy-done.17, bf16[256,512]{1,0:T(8,128)(2,1)} %copy-done.22, ...), custom_call_target="tpu_custom_call" | custom-call | flops 1000 | bytes 1000 | tf_op jit(solution)/shard_map/ctx_attend/pallas_call | solution.py:173
  126.6 9.4 %mem_attend.4 = (bf16[1,4,256,512]{3,2,1,0:T(8,128)(2,1)S(1)}, f32[1,4,8,256]{3,2,1,0:T(8,128)S(1)}) custom-call(s32[5,8]{1,0:T(8,128)S(1)} %pad_add_fusion.info, bf16[4,256,1024]{2,1,0:T(8,128)(2,1)S(1)} %bitcast.12, bf16[2048,512]{1,0:T(8,128)(2,1)} %pack_stores.3.s0, bf16[2048,512]{1,0:T(8,128)(2,1)} %collective-permute-done.15.s1, ...), custom_call_target="tpu_custom_call" | custom-call | flops 1000 | bytes 1000 | tf_op jit(solution)/shard_map/mem_attend/pallas_call | solution.py:192
  136.0 9.4 %mem_attend.5 = (bf16[1,4,256,512]{3,2,1,0:T(8,128)(2,1)S(1)}, f32[1,4,8,256]{3,2,1,0:T(8,128)S(1)}) custom-call(s32[5,8]{1,0:T(8,128)S(1)} %pad_add_fusion.info, bf16[4,256,1024]{2,1,0:T(8,128)(2,1)S(1)} %bitcast.13, bf16[2048,512]{1,0:T(8,128)(2,1)} %pack_stores.3.s0, bf16[2048,512]{1,0:T(8,128)(2,1)} %collective-permute-done.15.s1, ...), custom_call_target="tpu_custom_call" | custom-call | flops 1000 | bytes 1000 | tf_op jit(solution)/shard_map/mem_attend/pallas_call | solution.py:192
  146.6 3.3 %collective-permute-start.23 = (f32[1,4,8,256]{3,2,1,0:T(8,128)S(1)}, f32[1,4,8,256]{3,2,1,0:T(8,128)S(1)}, u32[]{:S(2)}, u32[]{:S(2)}) collective-permute-start(f32[1,4,8,256]{3,2,1,0:T(8,128)S(1)} %get-tuple-element.215.refs_0_), channel_id=1, source_target_pairs={{0,12},{1,13},{2,14},{3,15},{4,8},{5,9},{6,10},{7,11},{8,4},{9,5},... | collective-permute-start | bytes 98312 | tf_op jit(solution)/shard_map/ppermute | solution.py:376
  154.5 3.4 %scale_mix.4 = (bf16[1,256,512]{2,1,0:T(8,128)(2,1)S(1)}, bf16[1,256,512]{2,1,0:T(8,128)(2,1)S(1)}, bf16[1,256,512]{2,1,0:T(8,128)(2,1)S(1)}, bf16[1,256,512]{2,1,0:T(8,128)(2,1)S(1)}) custom-call(s32[1,8]{1,0:T(1,128)S(1)} %bitcast.22, bf16[1,4,256,512]{3,2,1,0:T(8,128)(2,1)S(1)} %get-tuple-element.213.um_ref, bf16[4,1,256,512]{3,2,1,0:T(8,128)(2,1)S(1)} %copy-done.1, ...), custom_call_target="tpu_custom_call" | custom-call | flops 1000 | bytes 1000 | tf_op jit(solution)/shard_map/scale_mix/pallas_call | solution.py:225
  159.5 3.8 %scale_mix.5 = bf16[4,1,256,512]{3,2,1,0:T(8,128)(2,1)} custom-call(s32[1,8]{1,0:T(1,128)S(1)} %bitcast.23, bf16[1,4,256,512]{3,2,1,0:T(8,128)(2,1)S(1)} %get-tuple-element.220.um_ref, bf16[4,1,256,512]{3,2,1,0:T(8,128)(2,1)S(1)} %copy-done.1, bf16[1,3,256,512]{3,2,1,0:T(8,128)(2,1)S(1)} %copy-done.4, f32[16]{0:T(128)S(1)} %add_divide_fusion.gate_ref, ...), custom_call_target="tpu_custom_call" | custom-call | flops 1000 | bytes 1000 | tf_op jit(solution)/shard_map/scale_mix/pallas_call | solution.py:225
  163.3 5.6 %collective-permute-start.27 = (bf16[1,256,512]{2,1,0:T(8,128)(2,1)S(1)}, bf16[1,256,512]{2,1,0:T(8,128)(2,1)S(1)}, u32[]{:S(2)}, u32[]{:S(2)}) collective-permute-start(bf16[1,256,512]{2,1,0:T(8,128)(2,1)S(1)} %get-tuple-element.227), channel_id=1, source_target_pairs={{0,4},{1,5},{2,6},{3,7},{12,8},{13,9},{14,10},{15,11},{16,20},{17,... | collective-permute-start | bytes 786440 | tf_op jit(solution)/shard_map/ppermute | solution.py:382
  170.2 10.5 %collective-permute-done.27 = bf16[1,256,512]{2,1,0:T(8,128)(2,1)S(1)} collective-permute-done((bf16[1,256,512]{2,1,0:T(8,128)(2,1)S(1)}, bf16[1,256,512]{2,1,0:T(8,128)(2,1)S(1)}, u32[]{:S(2)}, u32[]{:S(2)}) %collective-permute-start.27) | collective-permute-done | bytes 262176 | tf_op jit(solution)/shard_map/ppermute | solution.py:382
  181.5 9.6 %collective-permute-done.25 = bf16[1,256,512]{2,1,0:T(8,128)(2,1)S(1)} collective-permute-done((bf16[1,256,512]{2,1,0:T(8,128)(2,1)S(1)}, bf16[1,256,512]{2,1,0:T(8,128)(2,1)S(1)}, u32[]{:S(2)}, u32[]{:S(2)}) %collective-permute-start.25) | collective-permute-done | bytes 262176 | tf_op jit(solution)/shard_map/ppermute | solution.py:382
  194.4 5.2 %collective-permute-done.24.refs_3_ = bf16[1,256,512]{2,1,0:T(8,128)(2,1)S(1)} collective-permute-done((bf16[1,256,512]{2,1,0:T(8,128)(2,1)S(1)}, bf16[1,256,512]{2,1,0:T(8,128)(2,1)S(1)}, u32[]{:S(2)}, u32[]{:S(2)}) %collective-permute-start.24) | collective-permute-done | bytes 262176 | tf_op jit(solution)/shard_map/ppermute | solution.py:376
  199.5 3.6 %collective-permute-done.26.refs_4_ = bf16[1,256,512]{2,1,0:T(8,128)(2,1)S(1)} collective-permute-done((bf16[1,256,512]{2,1,0:T(8,128)(2,1)S(1)}, bf16[1,256,512]{2,1,0:T(8,128)(2,1)S(1)}, u32[]{:S(2)}, u32[]{:S(2)}) %collective-permute-start.26) | collective-permute-done | bytes 262176 | tf_op jit(solution)/shard_map/ppermute | solution.py:382
  (125 shorter events, 46.2 us)
Async XLA Ops:
  6.5 51.1 %all-gather.5.cloned.1.call-start = ((), (), s32[]{:S(2)}) async-start(), calls=%async_computation.4 | async-start | bytes 2621440 | tf_op jit(solution)/shard_map/all_gather | solution.py:409
  8.5 102.0 %all-gather.7.cloned.1.call-start = ((), (), s32[]{:S(2)}) async-start(), calls=%async_computation.5 | async-start | bytes 2621440 | tf_op jit(solution)/shard_map/all_gather | solution.py:409
  8.6 10.2 %collective-permute-start.3 = (bf16[256,512]{1,0:T(8,128)(2,1)S(1)}, bf16[256,512]{1,0:T(8,128)(2,1)S(1)}, u32[]{:S(2)}, u32[]{:S(2)}) collective-permute-start(bf16[256,512]{1,0:T(8,128)(2,1)S(1)} %copy-done.15), channel_id=1, source_target_pairs={{0,2},{1,3},{2,0},{3,1},{4,6},{5,7},{6,4},{7,5},{8,10},{9,11},{10,... | collective-permute-start | bytes 786440 | tf_op jit(solution)/shard_map/ppermute | solution.py:376
  11.6 11.9 %collective-permute-start.4 = (bf16[256,512]{1,0:T(8,128)(2,1)S(1)}, bf16[256,512]{1,0:T(8,128)(2,1)S(1)}, u32[]{:S(2)}, u32[]{:S(2)}) collective-permute-start(bf16[256,512]{1,0:T(8,128)(2,1)S(1)} %copy-done.16), channel_id=1, source_target_pairs={{0,2},{1,3},{2,0},{3,1},{4,6},{5,7},{6,4},{7,5},{8,10},{9,11},{10,... | collective-permute-start | bytes 786440 | tf_op jit(solution)/shard_map/ppermute | solution.py:376
  23.5 47.2 %collective-permute-start.6 = (bf16[2048,512]{1,0:T(8,128)(2,1)}, bf16[2048,512]{1,0:T(8,128)(2,1)}, u32[]{:S(2)}, u32[]{:S(2)}) collective-permute-start(bf16[2048,512]{1,0:T(8,128)(2,1)} %pack_stores.2.s0), channel_id=1, source_target_pairs={{0,2},{1,3},{2,0},{3,1},{4,6},{5,7},{6,4},{7,5},{8,10},{9,11},{10,... | collective-permute-start | bytes 6291464 | tf_op jit(solution)/shard_map/ppermute | solution.py:376
  31.1 161.4 %reduce-scatter.3.cloned.1.call-start = ((), (), s32[]{:S(2)}) async-start(), calls=%async_computation.2 | async-start | bytes 2621440 | tf_op jit(solution)/shard_map/reduce_scatter | solution.py:442
  42.1 30.2 %collective-permute-start.5 = (bf16[2048,512]{1,0:T(8,128)(2,1)}, bf16[2048,512]{1,0:T(8,128)(2,1)}, u32[]{:S(2)}, u32[]{:S(2)}) collective-permute-start(bf16[2048,512]{1,0:T(8,128)(2,1)} %pack_stores.2.s0), channel_id=1, source_target_pairs={{0,1},{1,0},{2,3},{3,2},{4,5},{5,4},{6,7},{7,6},{8,9},{9,8},{10,11... | collective-permute-start | bytes 6291464 | tf_op jit(solution)/shard_map/ppermute | solution.py:376
  70.8 48.4 %collective-permute-start.16 = (bf16[2048,512]{1,0:T(8,128)(2,1)}, bf16[2048,512]{1,0:T(8,128)(2,1)}, u32[]{:S(2)}, u32[]{:S(2)}) collective-permute-start(bf16[2048,512]{1,0:T(8,128)(2,1)} %pack_stores.3.s0), channel_id=1, source_target_pairs={{0,2},{1,3},{2,0},{3,1},{4,6},{5,7},{6,4},{7,5},{8,10},{9,11},{10,... | collective-permute-start | bytes 6291464 | tf_op jit(solution)/shard_map/ppermute | solution.py:376
  91.8 9.3 %collective-permute-start.12 = (f32[2,4,8,256]{3,2,1,0:T(8,128)S(1)}, f32[2,4,8,256]{3,2,1,0:T(8,128)S(1)}, u32[]{:S(2)}, u32[]{:S(2)}) collective-permute-start(f32[2,4,8,256]{3,2,1,0:T(8,128)S(1)} %get-tuple-element.164.refs_0_), channel_id=1, source_target_pairs={{0,4},{1,5},{2,6},{3,7},{4,0},{5,1},{6,2},{7,3},{8,12},{9,13},{10,... | collective-permute-start | bytes 196616 | tf_op jit(solution)/shard_map/ppermute | solution.py:376
  93.4 11.1 %collective-permute-start.13 = (f32[2,4,8,256]{3,2,1,0:T(8,128)S(1)}, f32[2,4,8,256]{3,2,1,0:T(8,128)S(1)}, u32[]{:S(2)}, u32[]{:S(2)}) collective-permute-start(f32[2,4,8,256]{3,2,1,0:T(8,128)S(1)} %get-tuple-element.164.refs_0_), channel_id=1, source_target_pairs={{0,8},{1,9},{2,10},{3,11},{4,12},{5,13},{6,14},{7,15},{8,0},{9,1},... | collective-permute-start | bytes 196616 | tf_op jit(solution)/shard_map/ppermute | solution.py:376
  96.0 9.4 %collective-permute-start.14 = (f32[2,4,8,256]{3,2,1,0:T(8,128)S(1)}, f32[2,4,8,256]{3,2,1,0:T(8,128)S(1)}, u32[]{:S(2)}, u32[]{:S(2)}) collective-permute-start(f32[2,4,8,256]{3,2,1,0:T(8,128)S(1)} %get-tuple-element.164.refs_0_), channel_id=1, source_target_pairs={{0,12},{1,13},{2,14},{3,15},{4,8},{5,9},{6,10},{7,11},{8,4},{9,5},... | collective-permute-start | bytes 196616 | tf_op jit(solution)/shard_map/ppermute | solution.py:376
  110.1 93.0 %reduce-scatter.5.cloned.1.call-start = ((), (), s32[]{:S(2)}) async-start(), calls=%async_computation.3 | async-start | bytes 1310720 | tf_op jit(solution)/shard_map/reduce_scatter | solution.py:442
  110.4 16.2 %collective-permute-start.15 = (bf16[2048,512]{1,0:T(8,128)(2,1)}, bf16[2048,512]{1,0:T(8,128)(2,1)}, u32[]{:S(2)}, u32[]{:S(2)}) collective-permute-start(bf16[2048,512]{1,0:T(8,128)(2,1)} %pack_stores.3.s0), channel_id=1, source_target_pairs={{0,1},{1,0},{2,3},{3,2},{4,5},{5,4},{6,7},{7,6},{8,9},{9,8},{10,11... | collective-permute-start | bytes 6291464 | tf_op jit(solution)/shard_map/ppermute | solution.py:376
  119.1 7.5 %collective-permute-start.17 = (bf16[2048,512]{1,0:T(8,128)(2,1)}, bf16[2048,512]{1,0:T(8,128)(2,1)}, u32[]{:S(2)}, u32[]{:S(2)}) collective-permute-start(bf16[2048,512]{1,0:T(8,128)(2,1)} %collective-permute-done.16.s2), channel_id=1, source_target_pairs={{0,1},{1,0},{2,3},{3,2},{4,5},{5,4},{6,7},{7,6},{8,9},{9,8},{10,11... | collective-permute-start | bytes 6291464 | tf_op jit(solution)/shard_map/ppermute | solution.py:376
  145.8 8.7 %collective-permute-start.22 = (f32[1,4,8,256]{3,2,1,0:T(8,128)S(1)}, f32[1,4,8,256]{3,2,1,0:T(8,128)S(1)}, u32[]{:S(2)}, u32[]{:S(2)}) collective-permute-start(f32[1,4,8,256]{3,2,1,0:T(8,128)S(1)} %get-tuple-element.215.refs_0_), channel_id=1, source_target_pairs={{0,8},{1,9},{2,10},{3,11},{4,12},{5,13},{6,14},{7,15},{8,0},{9,1},... | collective-permute-start | bytes 98312 | tf_op jit(solution)/shard_map/ppermute | solution.py:376
  146.6 7.8 %collective-permute-start.23 = (f32[1,4,8,256]{3,2,1,0:T(8,128)S(1)}, f32[1,4,8,256]{3,2,1,0:T(8,128)S(1)}, u32[]{:S(2)}, u32[]{:S(2)}) collective-permute-start(f32[1,4,8,256]{3,2,1,0:T(8,128)S(1)} %get-tuple-element.215.refs_0_), channel_id=1, source_target_pairs={{0,12},{1,13},{2,14},{3,15},{4,8},{5,9},{6,10},{7,11},{8,4},{9,5},... | collective-permute-start | bytes 98312 | tf_op jit(solution)/shard_map/ppermute | solution.py:376
  149.9 8.6 %collective-permute-start.18 = (f32[1,4,8,256]{3,2,1,0:T(8,128)S(1)}, f32[1,4,8,256]{3,2,1,0:T(8,128)S(1)}, u32[]{:S(2)}, u32[]{:S(2)}) collective-permute-start(f32[1,4,8,256]{3,2,1,0:T(8,128)S(1)} %get-tuple-element.222.refs_0_), channel_id=1, source_target_pairs={{0,4},{1,5},{2,6},{3,7},{4,0},{5,1},{6,2},{7,3},{8,12},{9,13},{10,... | collective-permute-start | bytes 98312 | tf_op jit(solution)/shard_map/ppermute | solution.py:376
  149.9 9.6 %collective-permute-start.19 = (f32[1,4,8,256]{3,2,1,0:T(8,128)S(1)}, f32[1,4,8,256]{3,2,1,0:T(8,128)S(1)}, u32[]{:S(2)}, u32[]{:S(2)}) collective-permute-start(f32[1,4,8,256]{3,2,1,0:T(8,128)S(1)} %get-tuple-element.222.refs_0_), channel_id=1, source_target_pairs={{0,8},{1,9},{2,10},{3,11},{4,12},{5,13},{6,14},{7,15},{8,0},{9,1},... | collective-permute-start | bytes 98312 | tf_op jit(solution)/shard_map/ppermute | solution.py:376
  151.2 8.3 %collective-permute-start.20 = (f32[1,4,8,256]{3,2,1,0:T(8,128)S(1)}, f32[1,4,8,256]{3,2,1,0:T(8,128)S(1)}, u32[]{:S(2)}, u32[]{:S(2)}) collective-permute-start(f32[1,4,8,256]{3,2,1,0:T(8,128)S(1)} %get-tuple-element.222.refs_0_), channel_id=1, source_target_pairs={{0,12},{1,13},{2,14},{3,15},{4,8},{5,9},{6,10},{7,11},{8,4},{9,5},... | collective-permute-start | bytes 98312 | tf_op jit(solution)/shard_map/ppermute | solution.py:376
  163.3 17.5 %collective-permute-start.27 = (bf16[1,256,512]{2,1,0:T(8,128)(2,1)S(1)}, bf16[1,256,512]{2,1,0:T(8,128)(2,1)S(1)}, u32[]{:S(2)}, u32[]{:S(2)}) collective-permute-start(bf16[1,256,512]{2,1,0:T(8,128)(2,1)S(1)} %get-tuple-element.227), channel_id=1, source_target_pairs={{0,4},{1,5},{2,6},{3,7},{12,8},{13,9},{14,10},{15,11},{16,20},{17,... | collective-permute-start | bytes 786440 | tf_op jit(solution)/shard_map/ppermute | solution.py:382
  168.9 22.2 %collective-permute-start.25 = (bf16[1,256,512]{2,1,0:T(8,128)(2,1)S(1)}, bf16[1,256,512]{2,1,0:T(8,128)(2,1)S(1)}, u32[]{:S(2)}, u32[]{:S(2)}) collective-permute-start(bf16[1,256,512]{2,1,0:T(8,128)(2,1)S(1)} %get-tuple-element.228), channel_id=1, source_target_pairs={{0,4},{1,5},{2,6},{3,7},{12,8},{13,9},{14,10},{15,11},{16,20},{17,... | collective-permute-start | bytes 786440 | tf_op jit(solution)/shard_map/ppermute | solution.py:382
  170.2 29.3 %collective-permute-start.24 = (bf16[1,256,512]{2,1,0:T(8,128)(2,1)S(1)}, bf16[1,256,512]{2,1,0:T(8,128)(2,1)S(1)}, u32[]{:S(2)}, u32[]{:S(2)}) collective-permute-start(bf16[1,256,512]{2,1,0:T(8,128)(2,1)S(1)} %get-tuple-element.226), channel_id=1, source_target_pairs={{0,4},{1,5},{2,6},{3,7},{4,0},{5,1},{6,2},{7,3},{8,12},{9,13},{10,... | collective-permute-start | bytes 786440 | tf_op jit(solution)/shard_map/ppermute | solution.py:376
  180.8 18.7 %collective-permute-start.28 = (bf16[1,256,512]{2,1,0:T(8,128)(2,1)S(1)}, bf16[1,256,512]{2,1,0:T(8,128)(2,1)S(1)}, u32[]{:S(2)}, u32[]{:S(2)}) collective-permute-start(bf16[1,256,512]{2,1,0:T(8,128)(2,1)S(1)} %add_convert_fusion), channel_id=1, source_target_pairs={{4,8},{5,9},{6,10},{7,11},{8,4},{9,5},{10,6},{11,7},{20,24},{21,25... | collective-permute-start | bytes 786440 | tf_op jit(solution)/shard_map/ppermute | solution.py:382
  191.2 12.0 %collective-permute-start.26 = (bf16[1,256,512]{2,1,0:T(8,128)(2,1)S(1)}, bf16[1,256,512]{2,1,0:T(8,128)(2,1)S(1)}, u32[]{:S(2)}, u32[]{:S(2)}) collective-permute-start(bf16[1,256,512]{2,1,0:T(8,128)(2,1)S(1)} %add_convert_fusion.1), channel_id=1, source_target_pairs={{4,12},{5,13},{6,14},{7,15},{8,0},{9,1},{10,2},{11,3},{20,28},{21,... | collective-permute-start | bytes 786440 | tf_op jit(solution)/shard_map/ppermute | solution.py:382
  (37 other events, 331.2 us)
Sparse Core Ops, SparseCore 0:
  8.9 48.6 all-gather.4
  59.2 50.1 all-gather.6
  111.7 48.0 reduce-scatter.2
  163.4 38.8 reduce-scatter.4
